TPU v7x, 128 devices: a whole 4x4x4 slice. The times are simulated.
128 devices in a mesh: lat: 16 (over z, y_hi, core), lon: 8 (over x, y_lo).
Axes of the slice: x: 4, y: 4 (y_hi: 2, y_lo: 2; y = y_hi * 2 + y_lo), z: 4, core: 2. Of those that a mesh axis runs over, the one named last changes fastest.
Arguments:
- tokens: bfloat16 [2, 192, 384, 512], P(None, 'lat', 'lon'), may hold values from -610 to 610
- cotangent: bfloat16 [2, 192, 384, 512], P(None, 'lat', 'lon'), may hold values from -6 to 6
- w_qkv: bfloat16 [512, 1536], replicated, may hold values from -0.25 to 0.25
- w_proj: bfloat16 [512, 512], replicated, may hold values from -0.25 to 0.25
- w_up: bfloat16 [512, 2048], replicated, may hold values from -0.25 to 0.25
- w_down: bfloat16 [2048, 512], replicated, may hold values from -0.125 to 0.125
- pair_bias: float32 [8, 144, 144], replicated, may hold values from -4 to 320
- gain_one: float32 [512], replicated, may hold values from 0.5 to 1.5
- gain_two: float32 [512], replicated, may hold values from 0.5 to 1.5
Outputs:
- grad_tokens: bfloat16 [2, 192, 384, 512], P(None, 'lat', 'lon')
- grad_w_qkv: float32 [512, 1536], replicated
- grad_w_proj: float32 [512, 512], replicated
- grad_w_up: float32 [512, 2048], replicated
- grad_w_down: float32 [2048, 512], replicated
- grad_pair_bias: float32 [8, 144, 144], replicated
- grad_gain_one: float32 [512], replicated
- grad_gain_two: float32 [512], replicated
All inputs are finite; a program needn't handle non-finite values.
Results may differ from a plain program's by a relative error of at most 0.015.
Values may be sent and summed in bfloat16 or wider, within the bound.
No kernel may reach another device: no remote copies, remote signals or barrier semaphores. Data moves between devices by JAX's collectives and lax.ppermute only.
A program may use at most 128 MiB of HBM per device.

v0:
```python
import functools

import jax
import jax.numpy as jnp
from jax import lax
from jax.experimental import pallas as pl
from jax.experimental.pallas import tpu as pltpu
from jax.sharding import PartitionSpec as P

HEADS = 8
WLAT = 6
WLON = 12
WT = 144
D = 512
QKV = 1536
FF = 2048
LEVELS = 2
HEIGHT = 12
BREADTH = 48
WINDOWS = 8
ROWS = WINDOWS * WT
EPSILON = 1e-05
MASKED = -1e30
F32 = jnp.float32
BF16 = jnp.bfloat16
PIECES = 32
BAND_ROWS = 512
PROJ_ROWS = 64
ONE_ROWS = BAND_ROWS + PROJ_ROWS
QKV_ROWS = 192
REST_ROWS = 48
TWO_ROWS = QKV_ROWS + REST_ROWS
ALL_ROWS = ONE_ROWS + TWO_ROWS
GAIN_AT = (HEADS + 1) * WT
MIB = 1024 * 1024
M_NORM = 576
M_UP = 1152
M_BACK = 576
M_BRANCH = 576
G_FORWARD = 4
G_BACKWARD = 2
F_STEP = 512

NN = (((1,), (0,)), ((), ()))
NT = (((1,), (1,)), ((), ()))
TN = (((0,), (0,)), ((), ()))


def mm(a, b, dims=NN):
    return lax.dot_general(a, b, dims, preferred_element_type=F32)


def stats_of(values):
    average = jnp.mean(values, -1, keepdims=True)
    centred = values - average
    variance = jnp.mean(centred * centred, -1, keepdims=True)
    inv_std = lax.rsqrt(variance + EPSILON)
    return centred * inv_std, inv_std


def back_of(grad_out, gain_vec, normed, inv_std):
    scaled = grad_out * gain_vec
    return (
        scaled
        - jnp.mean(scaled, -1, keepdims=True)
        - normed * jnp.mean(scaled * normed, -1, keepdims=True)
    ) * inv_std


def run_at(level, row, column):
    window = (row // WLAT) * 4 + column
    return window * WT + level * (WT // 2) + (row % WLAT) * WLON


def gather_windows(main_ref, lon_ref, lat_ref, both_ref, line, wide, out_ref):
    for level in range(LEVELS):
        for row in range(HEIGHT):
            if row < HEIGHT - WLAT // 2:
                line[0:BREADTH] = main_ref[level, row + WLAT // 2].astype(F32)
                line[BREADTH : BREADTH + 6] = lon_ref[level, row + WLAT // 2].astype(F32)
            else:
                line[0:BREADTH] = lat_ref[level, row - (HEIGHT - WLAT // 2)].astype(F32)
                line[BREADTH : BREADTH + 6] = both_ref[level, row - (HEIGHT - WLAT // 2)].astype(F32)
            for column in range(4):
                at = run_at(level, row, column)
                wide[at : at + WLON] = line[6 + WLON * column : 18 + WLON * column]

    def narrow(window, _):
        rows = pl.ds(pl.multiple_of(window * WT, 16), WT)
        out_ref[rows] = wide[rows].astype(BF16)
        return 0

    lax.fori_loop(0, WINDOWS, narrow, 0)


def position(lat, lon):
    return lat % 2, (lon // 2, (lat // 2) % 2 * 2 + lon % 2, lat // 4)


ORDERS = ((0, 1, 2), (1, 2, 0))


def here():
    return position(lax.axis_index("lat"), lax.axis_index("lon"))


def slot_of(core, block):
    _, chip = here()
    first, second = chip[ORDERS[core][0]], chip[ORDERS[core][1]]
    return (block // 4 + 4 - first) % 4 * 4 + (block % 4 + 4 - second) % 4


def block_at(core, first_by, second_by):
    _, chip = here()
    first = jnp.where(core == 0, chip[ORDERS[0][0]], chip[ORDERS[1][0]])
    second = jnp.where(core == 0, chip[ORDERS[0][1]], chip[ORDERS[1][1]])
    return (first + 4 - first_by) % 4 * 4 + (second + 4 - second_by) % 4


def window_rows(window):
    return pl.ds(pl.multiple_of(window * WT, 16), WT)


def softmax_first(scores):
    top = jnp.max(scores, 0, keepdims=True)
    exponent = jnp.exp(scores - top)
    total = jnp.sum(exponent, 0, keepdims=True)
    return (exponent * (1.0 / total)).astype(BF16)


def head_masks():
    lane = lax.broadcasted_iota(jnp.int32, (1, 128), 1)
    first = lane < 64
    row = lax.broadcasted_iota(jnp.int32, (128, D), 0) // 16
    column = lax.broadcasted_iota(jnp.int32, (128, D), 1) // 64
    halves = (first.astype(F32).astype(BF16), (lane >= 64).astype(F32).astype(BF16))
    return first, halves, (row == column).astype(F32)


def tiled(block):
    return jnp.concatenate([block] * HEADS, 0)


def pair_of(head):
    return slice(head // 2 * 128, head // 2 * 128 + 128)


def tail_sum(block, tail):
    return jnp.sum((block * tail).reshape(HEADS, 16, D), 0)


def pack_kernel(ref, lon, lat, both):
    edge, top = WLON // 2, WLAT // 2
    lat[...] = ref[:, :top]
    for level in range(LEVELS):
        for row in range(HEIGHT):
            lon[level, row] = ref[level, row, :edge]
        for row in range(top):
            both[level, row] = ref[level, row, :edge]


def attention_kernel(
    tok, tok_lon, tok_lat, tok_both, w_qkv, pair_bias, gain_one,
    xw, mix, act_t, qkv_out, probs_out,
    line, wide, act, qkv, probs, bias, sent,
):
    gather_windows(tok, tok_lon, tok_lat, tok_both, line, wide, xw)

    def norm_one(window, _):
        rows = window_rows(window)
        values, _ = stats_of(xw[rows].astype(F32))
        act[rows] = (values * gain_one[...]).astype(BF16)
        return 0

    lax.fori_loop(0, WINDOWS, norm_one, 0)

    def project(n, _):
        cols = pl.ds(pl.multiple_of(n * 256, 256), 256)
        qkv[:, cols] = mm(act[...], w_qkv[:, cols]).astype(BF16)
        return 0

    lax.fori_loop(0, QKV // 256, project, 0)
    copies = [pltpu.make_async_copy(qkv, qkv_out, sent.at[WINDOWS])]
    copies[0].start()
    act_t[...] = act[...].T

    is_last = lax.axis_index("lat") == lax.axis_size("lat") - 1
    key_at = lax.broadcasted_iota(jnp.int32, (WT, 128), 0)
    query_at = lax.broadcasted_iota(jnp.int32, (WT, 128), 1)

    def masked(query_at):
        apart = (key_at // WLON % WLAT >= WLAT // 2) != (query_at // WLON % WLAT >= WLAT // 2)
        return jnp.where(apart & is_last, MASKED, 0.0)

    mask_main = masked(query_at)
    mask_tail = masked(128 + query_at % 16)
    for head in range(HEADS):
        block = pair_bias[head, 0:128].T
        bias[0, head] = block
        bias[1, head] = block + mask_main
    block = jnp.concatenate([pair_bias[head, 128:WT] for head in range(HEADS)], 0).T
    bias[0, HEADS] = block
    bias[1, HEADS] = block + mask_tail

    first, halves, tail = head_masks()
    halves = [half * 0.125 for half in halves]
    tail_low = (tail * 0.125).astype(BF16)

    def attend(group, _):
        windows = [group * G_FORWARD + i for i in range(G_FORWARD)]
        heads = [(i, head) for i in range(G_FORWARD) for head in range(HEADS)]
        rows = [window_rows(window) for window in windows]
        main = [pl.ds(pl.multiple_of(window * WT, 16), 128) for window in windows]
        last = [pl.ds(pl.multiple_of(window * WT + 128, 16), 16) for window in windows]
        key = [qkv[r, D : 2 * D] for r in rows]
        val = [qkv[r, 2 * D : 3 * D] for r in rows]
        tail_scores = [
            mm(k, tiled(qkv[r, 0:D]) * tail_low, NT) for k, r in zip(key, last)
        ]
        scores = [
            mm(key[i][:, pair_of(head)], qkv[main[i], pair_of(head)] * halves[head % 2], NT)
            for i, head in heads
        ]
        tail_weights = [
            softmax_first(t + bias[window // 4, HEADS]) for t, window in zip(tail_scores, windows)
        ]
        weights = [
            softmax_first(t + bias[windows[i] // 4, head]) for t, (i, head) in zip(scores, heads)
        ]
        tail_mixed = [mm(w, v, TN) for w, v in zip(tail_weights, val)]
        mixed = [mm(w, val[i][:, pair_of(head)], TN) for w, (i, head) in zip(weights, heads)]
        for i, window in enumerate(windows):
            probs[window, HEADS] = tail_weights[i]
            mix[last[i]] = tail_sum(tail_mixed[i], tail).astype(BF16)
        for w, (i, head) in zip(weights, heads):
            probs[windows[i], head] = w
        for n, (i, head) in enumerate(heads):
            if head % 2 == 0:
                mix[main[i], pair_of(head)] = jnp.where(first, mixed[n], mixed[n + 1]).astype(BF16)
        for window in windows:
            pltpu.make_async_copy(probs.at[window], probs_out.at[window], sent.at[window]).start()
        return 0

    lax.fori_loop(0, WINDOWS // G_FORWARD, attend, 0)
    copies[0].wait()
    for window in range(WINDOWS):
        pltpu.make_async_copy(probs.at[window], probs_out.at[window], sent.at[window]).wait()


def mlp_kernel(
    xw, mix, cot, cot_lon, cot_lat, cot_both, w_proj, w_up_in, w_down_in, gain_two,
    grad_mixed, grad_res, keep_one, send_one, sum_gain,
    line, wide, cotw, act, normed, inv_two, act_t, activated, grad_hidden, sums, w_up, w_down,
    got, sent,
):
    loads = [
        pltpu.make_async_copy(w_up_in, w_up, got.at[0]),
        pltpu.make_async_copy(w_down_in, w_down, got.at[1]),
    ]
    for load in loads:
        load.start()
    gather_windows(cot, cot_lon, cot_lat, cot_both, line, wide, cotw)

    def norm_two(part, _):
        rows = pl.ds(pl.multiple_of(part * M_NORM, 16), M_NORM)
        residual = xw[rows].astype(F32) + mm(mix[rows], w_proj[...])
        values, inv_std = stats_of(residual)
        normed[rows] = values
        inv_two[rows] = inv_std
        act[rows] = (values * gain_two[...]).astype(BF16)
        return 0

    lax.fori_loop(0, ROWS // M_NORM, norm_two, 0)
    act_t[...] = act[...].T
    for load in loads:
        load.wait()

    c0 = 0.7978845608028654
    c1 = c0 * 0.044715

    def mlp(f, _):
        cols = pl.ds(pl.multiple_of(f * F_STEP, F_STEP), F_STEP)

        def rows_of(r, _):
            rows = pl.ds(pl.multiple_of(r * M_UP, 16), M_UP)
            u = mm(act[rows], w_up[:, cols])
            grad_act = mm(cotw[rows], w_down[cols, :], NT)
            square = u * u
            gate = 0.5 + 0.5 * jnp.tanh(u * (c0 + c1 * square))
            value = u * gate
            activated[rows] = value.astype(BF16)
            slope = gate + value * (1.0 - gate) * (2.0 * c0 + 6.0 * c1 * square)
            grad_hidden[rows, cols] = (grad_act * slope).astype(BF16)
            return 0

        lax.fori_loop(0, ROWS // M_UP, rows_of, 0)
        up = mm(act_t[...], grad_hidden[:, cols]).astype(BF16)
        for j in range(4):
            at = pl.ds(pl.multiple_of(f * 128 + 32 * j, 32), 32)
            sums[0:16, at] = up[:, 128 * j : 128 * j + 128].reshape(16, 32, 128)
        down = mm(activated[...], cotw[...], TN).astype(BF16)
        for i in range(4):
            for j in range(4):
                part = down[128 * i : 128 * i + 128, 128 * j : 128 * j + 128]
                sums[16 + f * 4 + i, 128 * j : 128 * j + 128] = part
        return 0

    lax.fori_loop(0, FF // F_STEP, mlp, 0)

    core, _ = here()

    def send(rows, at, act_on):
        for owner in range(2):
            for block in range(16):
                piece = owner * 16 + block
                slot = slot_of(owner, block)

                def copy_to(out):
                    return pltpu.make_async_copy(
                        sums.at[piece, rows], out.at[slot, rows], sent.at[at, piece]
                    )

                @pl.when(core == owner)
                def _():
                    act_on(copy_to(keep_one))

                @pl.when(core != owner)
                def _():
                    act_on(copy_to(send_one))

    bands, tails = pl.ds(0, BAND_ROWS), pl.ds(BAND_ROWS, PROJ_ROWS)
    send(bands, 0, lambda copy: copy.start())

    def back(part, total):
        rows = pl.ds(pl.multiple_of(part * M_BACK, 16), M_BACK)
        grads = mm(grad_hidden[rows], w_up[...], NT)
        values = normed[rows]
        total = total + jnp.sum(grads * values, 0, keepdims=True)
        residual = cotw[rows].astype(F32) + back_of(grads, gain_two[...], values, inv_two[rows])
        grad_res[rows] = residual
        low = residual.astype(BF16)
        act[rows] = low
        grad_mixed[rows] = mm(low, w_proj[...], NT).astype(BF16)
        return total

    sum_gain[...] = lax.fori_loop(0, ROWS // M_BACK, back, jnp.zeros((1, D), F32))
    proj = mm(mix[...], act[...], TN).astype(BF16)
    for j in range(4):
        at = slice(BAND_ROWS + 16 * j, BAND_ROWS + 16 * j + 16)
        sums[:, at] = proj[:, 128 * j : 128 * j + 128].reshape(PIECES, 16, 128)
    send(tails, 1, lambda copy: copy.start())
    send(bands, 0, lambda copy: copy.wait())
    send(tails, 1, lambda copy: copy.wait())


def first_back_kernel(qkv, probs, grad_mixed, grad_qkv, bias):
    window_back(qkv, probs, grad_mixed, grad_qkv, bias, None)


def second_back_kernel(
    qkv, probs, grad_mixed, act_t, sum_gain_two, bias_before, grads_before,
    grad_qkv, keep_two, send_two,
    grads_all, bias, flat,
):
    step = pl.program_id(0)

    @pl.when(step == 0)
    def _():
        grads_all[0 : ROWS // 2] = grads_before[...]

    window_back(qkv, probs, grad_mixed, grad_qkv, bias, bias_before)
    size = G_BACKWARD * WT
    at = pl.multiple_of(ROWS // 2 + step * size, 16)
    grads_all[pl.ds(at, size)] = grad_qkv[...]

    @pl.when(step == WINDOWS // 2 // G_BACKWARD - 1)
    def _():
        for n in range(QKV // 512):
            part = mm(act_t[...], grads_all[:, 512 * n : 512 * n + 512]).astype(BF16)
            for j in range(4):
                at = (n * 4 + j) * 16
                flat[:, at : at + 16] = part[:, 128 * j : 128 * j + 128].reshape(PIECES, 16, 128)
        gains = [sum_gain_two[:, 128 * j : 128 * j + 128] for j in range(4)]
        gains = jnp.concatenate(gains + [jnp.zeros((12, 128), F32)], 0)
        rest = [bias[block].astype(BF16) for block in range(HEADS + 1)] + [gains.astype(BF16)]
        rest.append(jnp.zeros((PIECES * REST_ROWS - GAIN_AT - 16, 128), BF16))
        rest = jnp.concatenate(rest, 0)
        flat[:, QKV_ROWS:TWO_ROWS] = rest.reshape(PIECES, REST_ROWS, 128)
        core, _ = here()
        for owner in range(2):
            for block in range(16):
                slot = slot_of(owner, block)
                piece = flat[owner * 16 + block]

                @pl.when(core == owner)
                def _():
                    keep_two[slot] = piece

                @pl.when(core != owner)
                def _():
                    send_two[slot] = piece


def window_back(qkv, probs, grad_mixed, grad_qkv, bias, bias_before):
    step = pl.program_id(0)
    first, halves, tail = head_masks()
    tail_low = tail.astype(BF16)

    @pl.when(step == 0)
    def _():
        bias[...] = jnp.zeros_like(bias) if bias_before is None else bias_before[...]

    group = range(G_BACKWARD)
    heads = [(i, head) for i in group for head in range(HEADS)]
    rows = [slice(i * WT, i * WT + WT) for i in group]
    main = [slice(i * WT, i * WT + 128) for i in group]
    last = [slice(i * WT + 128, i * WT + WT) for i in group]
    key = [qkv[r, D : 2 * D] for r in rows]
    val = [qkv[r, 2 * D : 3 * D] for r in rows]
    query_tail = [tiled(qkv[r, 0:D]) * tail_low for r in last]
    out_tail = [tiled(grad_mixed[r]) * tail_low for r in last]
    query = [qkv[main[i], pair_of(head)] * halves[head % 2] for i, head in heads]
    out = [grad_mixed[main[i], pair_of(head)] * halves[head % 2] for i, head in heads]

    tail_probs = [mm(v, o, NT) for v, o in zip(val, out_tail)]
    grad_probs = [mm(val[i][:, pair_of(head)], o, NT) for o, (i, head) in zip(out, heads)]

    def score_grads(low_probs, grad_probs):
        weights = low_probs.astype(F32)
        product = grad_probs * weights
        return product - weights * jnp.sum(product, 0, keepdims=True)

    tail_low_probs = [probs[i, HEADS] for i in group]
    low_probs = [probs[i, head] for i, head in heads]
    tail_grads = [score_grads(p, g) for p, g in zip(tail_low_probs, tail_probs)]
    grads = [score_grads(p, g) for p, g in zip(low_probs, grad_probs)]
    bias[HEADS] += sum(tail_grads[1:], tail_grads[0])
    for head in range(HEADS):
        mine = grads[head::HEADS]
        bias[head] += sum(mine[1:], mine[0])
    tail_grads = [g.astype(BF16) for g in tail_grads]
    grads = [g.astype(BF16) for g in grads]

    query_last = [mm(g, k, TN) for g, k in zip(tail_grads, key)]
    key_more = [mm(g, q) for g, q in zip(tail_grads, query_tail)]
    val_more = [mm(p, o) for p, o in zip(tail_low_probs, out_tail)]
    query_parts = [mm(g, key[i][:, pair_of(head)], TN) for g, (i, head) in zip(grads, heads)]
    key_parts = [mm(g, q) for g, q in zip(grads, query)]
    val_parts = [mm(p, o) for p, o in zip(low_probs, out)]
    for i in group:
        grad_qkv[last[i], 0:D] = (tail_sum(query_last[i], tail) * 0.125).astype(BF16)
    for n, (i, head) in enumerate(heads):
        if head % 2:
            continue
        cols = pair_of(head)
        at = head // 2 * 128
        part = jnp.where(first, query_parts[n], query_parts[n + 1]) * 0.125
        grad_qkv[main[i], cols] = part.astype(BF16)
        part = (key_parts[n] + key_parts[n + 1] + key_more[i][:, cols]) * 0.125
        grad_qkv[rows[i], D + at : D + at + 128] = part.astype(BF16)
        part = val_parts[n] + val_parts[n + 1] + val_more[i][:, cols]
        grad_qkv[rows[i], 2 * D + at : 2 * D + at + 128] = part.astype(BF16)

def branch_kernel(xw, grads_first, grads_second, grad_res, w_qkv, gain_one, main, lon, lat, both, wide, line):
    for part, grad_qkv in enumerate((grads_first, grads_second)):
        rows = slice(part * ROWS // 2, (part + 1) * ROWS // 2)
        values, inv_std = stats_of(xw[rows].astype(F32))
        grads = mm(grad_qkv[...], w_qkv[...], NT)
        low = back_of(grads, gain_one[...], values, inv_std).astype(BF16)
        wide[rows] = grad_res[rows] + low.astype(F32)

    for level in range(LEVELS):
        for row in range(HEIGHT):
            for column in range(4):
                at = run_at(level, row, column)
                line[WLON * column : WLON * column + WLON] = wide[at : at + WLON]
            inner, outer = (main, lon) if row < HEIGHT - WLAT // 2 else (lat, both)
            at = row if row < HEIGHT - WLAT // 2 else row - (HEIGHT - WLAT // 2)
            inner[level, at] = line[0 : BREADTH - 6].astype(BF16)
            outer[level, at] = line[BREADTH - 6 : BREADTH].astype(BF16)


def write_bands(scale, owner, pieces, up_out, down_out, buffer_up, buffer_down, sent):
    depth = buffer_up.shape[0]

    def run(buffer, rows, fill, out):
        def copy(n, block):
            at = pl.ds(pl.multiple_of(block * rows, rows), rows)
            return pltpu.make_async_copy(buffer.at[n % depth], out.at[at], sent.at[n % depth])

        for n in range(16):
            block = block_at(owner, n // 4, n % 4)
            if n >= depth:
                copy(n, block).wait()
            fill(n)
            copy(n, block).start()
        for n in range(16 - depth, 16):
            copy(n, block_at(owner, n // 4, n % 4)).wait()

    def fill_up(n):
        for j in range(16):
            part = pieces[n // 4][n % 4, 32 * j : 32 * j + 32]
            buffer_up[n % depth, :, 128 * j : 128 * j + 128] = part.astype(F32) * scale

    def fill_down(n):
        for j in range(4):
            part = pieces[n // 4][n % 4, 128 * j : 128 * j + 128]
            buffer_down[n % depth, :, 128 * j : 128 * j + 128] = part.astype(F32) * scale

    @pl.when(owner == 0)
    def _():
        run(buffer_up, 32, fill_up, up_out)

    @pl.when(owner == 1)
    def _():
        run(buffer_down, 128, fill_down, down_out)


def finish_own_kernel(scale, *refs):
    pieces, (up_out, down_out, buffer_up, buffer_down, sent) = refs[:4], refs[4:]
    write_bands(scale, here()[0], pieces, up_out, down_out, buffer_up, buffer_down, sent)


def finish_kernel(scale, *refs):
    own, other, (up_in, down_in, w_qkv, gain_vec) = refs[:4], refs[4:8], refs[8:12]
    up_out, down_out, qkv, proj, bias, gain_one, gain_two = refs[12:19]
    buffer_up, buffer_down, sent, rest, sums = refs[19:]
    core, _ = here()
    write_bands(scale, 1 - core, other, up_out, down_out, buffer_up, buffer_down, sent)
    for owner, pieces in ((core, own), (1 - core, other)):
        for n in range(16):
            piece = owner * 16 + block_at(owner, n // 4, n % 4)
            rows = pl.ds(pl.multiple_of(piece * 16, 16), 16)
            held = pieces[n // 4]
            for j in range(4):
                at = BAND_ROWS + 16 * j
                part = held[n % 4, at : at + 16].astype(F32) * scale
                proj[rows, 128 * j : 128 * j + 128] = part
            total = jnp.zeros((16, 128), F32)
            for j in range(12):
                cols = slice(128 * j, 128 * j + 128)
                at = ONE_ROWS + 16 * j
                part = held[n % 4, at : at + 16].astype(F32) * scale
                qkv[rows, cols] = part
                total = total + part * w_qkv[rows, cols].astype(F32)
            sums[rows] = total
            rest[piece] = held[n % 4, ONE_ROWS + QKV_ROWS : ALL_ROWS]
    gain_one[...] = jnp.sum(sums[...].T, 0, keepdims=True) / gain_vec[...]
    flat = rest[...].reshape(PIECES * REST_ROWS, 128).astype(F32)
    last = flat[HEADS * WT : GAIN_AT].T * (scale * WT)
    for head in range(HEADS):
        bias[head, 0:128] = flat[head * WT : head * WT + WT].T * (scale * WT)
        bias[head, 128:WT] = last[16 * head : 16 * head + 16]
    for j in range(4):
        part = flat[GAIN_AT + j : GAIN_AT + j + 1] * scale
        gain_two[:, 128 * j : 128 * j + 128] = part


def shape(*dims, dtype=BF16):
    return jax.ShapeDtypeStruct(dims, dtype)


def params(mib):
    return pltpu.CompilerParams(vmem_limit_bytes=mib * MIB)


def vmem(*dims, dtype=BF16):
    return pltpu.VMEM(dims, dtype)


def cost(flops, moved):
    return pl.CostEstimate(flops=flops, bytes_accessed=moved, transcendentals=0)


ANY = pl.BlockSpec(memory_space=pl.ANY)
INSIDE = pl.BlockSpec(memory_space=pltpu.VMEM)
SCALARS = pl.BlockSpec(memory_space=pltpu.SMEM)


def pack(grid):
    edge, top = WLON // 2, WLAT // 2
    return pl.pallas_call(
        pack_kernel,
        out_shape=(
            shape(LEVELS, HEIGHT, edge, D), shape(LEVELS, top, BREADTH, D),
            shape(LEVELS, top, edge, D),
        ),
        in_specs=[INSIDE],
        out_specs=[INSIDE] * 3,
        compiler_params=params(16),
        name="pack",
    )(grid)


def attention(*operands):
    return pl.pallas_call(
        attention_kernel,
        out_shape=(
            shape(ROWS, D), shape(ROWS, D), shape(D, ROWS), shape(ROWS, QKV),
            shape(WINDOWS, HEADS + 1, WT, 128),
        ),
        in_specs=[INSIDE] * len(operands),
        out_specs=[INSIDE, INSIDE, INSIDE, ANY, ANY],
        scratch_shapes=[
            vmem(56, D, dtype=F32), vmem(ROWS, D, dtype=F32), vmem(ROWS, D), vmem(ROWS, QKV),
            vmem(WINDOWS, HEADS + 1, WT, 128), vmem(2, HEADS + 1, WT, 128, dtype=F32),
            pltpu.SemaphoreType.DMA((WINDOWS + 1,)),
        ],
        compiler_params=params(48),
        cost_estimate=cost(ROWS * D * QKV * 2 * 4, 20_000_000),
        name="attention",
    )(*operands)


def mlp_call(*operands):
    return pl.pallas_call(
        mlp_kernel,
        out_shape=(
            shape(ROWS, D), shape(ROWS, D, dtype=F32), shape(16, ONE_ROWS, 128),
            shape(16, ONE_ROWS, 128), shape(1, D, dtype=F32),
        ),
        in_specs=[INSIDE] * 7 + [ANY, ANY, INSIDE],
        out_specs=[INSIDE, INSIDE, ANY, ANY, INSIDE],
        scratch_shapes=[
            vmem(56, D, dtype=F32), vmem(ROWS, D, dtype=F32), vmem(ROWS, D), vmem(ROWS, D),
            vmem(ROWS, D, dtype=F32), vmem(ROWS, 1, dtype=F32), vmem(D, ROWS),
            vmem(ROWS, F_STEP), vmem(ROWS, FF), vmem(PIECES, ONE_ROWS, 128),
            vmem(D, FF), vmem(FF, D),
            pltpu.SemaphoreType.DMA((2,)), pltpu.SemaphoreType.DMA((2, PIECES)),
        ],
        compiler_params=params(56),
        cost_estimate=cost(ROWS * D * FF * 2 * 8, 40_000_000),
        name="mlp",
    )(*operands)


def back_specs(half):
    start = half * (WINDOWS // 2 // G_BACKWARD)
    return [
        pl.BlockSpec((G_BACKWARD * WT, QKV), lambda i: (start + i, 0)),
        pl.BlockSpec((G_BACKWARD, HEADS + 1, WT, 128), lambda i: (start + i, 0, 0, 0)),
        pl.BlockSpec((G_BACKWARD * WT, D), lambda i: (start + i, 0)),
    ]


def first_back(qkv, probs, grad_mixed):
    return pl.pallas_call(
        first_back_kernel,
        out_shape=(shape(ROWS // 2, QKV), shape(HEADS + 1, WT, 128, dtype=F32)),
        grid=(WINDOWS // 2 // G_BACKWARD,),
        in_specs=back_specs(0),
        out_specs=[
            pl.BlockSpec((G_BACKWARD * WT, QKV), lambda i: (i, 0)),
            pl.BlockSpec((HEADS + 1, WT, 128), lambda i: (0, 0, 0)),
        ],
        compiler_params=params(32),
        cost_estimate=cost(ROWS * D * QKV * 2 * 3, 10_000_000),
        name="first_back",
    )(qkv, probs, grad_mixed)


def second_back(*operands):
    return pl.pallas_call(
        second_back_kernel,
        out_shape=(
            shape(ROWS // 2, QKV), shape(16, TWO_ROWS, 128), shape(16, TWO_ROWS, 128),
        ),
        grid=(WINDOWS // 2 // G_BACKWARD,),
        in_specs=back_specs(1) + [INSIDE] * 4,
        out_specs=[pl.BlockSpec((G_BACKWARD * WT, QKV), lambda i: (i, 0)), INSIDE, INSIDE],
        scratch_shapes=[
            vmem(ROWS, QKV), vmem(HEADS + 1, WT, 128, dtype=F32), vmem(PIECES, TWO_ROWS, 128),
        ],
        compiler_params=params(40),
        cost_estimate=cost(ROWS * D * QKV * 2 * 4, 10_000_000),
        name="second_back",
    )(*operands)


def branch(*operands):
    return pl.pallas_call(
        branch_kernel,
        out_shape=(
            shape(LEVELS, 9, 42, D), shape(LEVELS, 9, 6, D), shape(LEVELS, 3, 42, D),
            shape(LEVELS, 3, 6, D),
        ),
        in_specs=[INSIDE] * len(operands),
        out_specs=[INSIDE] * 4,
        scratch_shapes=[vmem(ROWS, D, dtype=F32), vmem(48, D, dtype=F32)],
        compiler_params=params(24),
        cost_estimate=cost(ROWS * D * QKV * 2 * 4, 10_000_000),
        name="branch",
    )(*operands)


BUFFERS = 4


def finish_scratch():
    return [
        vmem(BUFFERS, 32, FF, dtype=F32), vmem(BUFFERS, 128, D, dtype=F32),
        pltpu.SemaphoreType.DMA((BUFFERS,)),
    ]


def finish_own(pieces, scale):
    return pl.pallas_call(
        functools.partial(finish_own_kernel, scale),
        out_shape=(shape(D, FF, dtype=F32), shape(FF, D, dtype=F32)),
        in_specs=[INSIDE] * 4,
        out_specs=[ANY, ANY],
        scratch_shapes=finish_scratch(),
        compiler_params=params(24),
        cost_estimate=cost(10_000_000, 10_000_000),
        name="finish_own",
    )(*pieces)


def finish(own, other, up, down, w_qkv, gain_one, scale):
    return pl.pallas_call(
        functools.partial(finish_kernel, scale),
        out_shape=(
            shape(D, FF, dtype=F32), shape(FF, D, dtype=F32), shape(D, QKV, dtype=F32),
            shape(D, D, dtype=F32), shape(HEADS, WT, WT, dtype=F32), shape(1, D, dtype=F32),
            shape(1, D, dtype=F32),
        ),
        in_specs=[INSIDE] * 8 + [ANY, ANY, INSIDE, INSIDE],
        out_specs=[ANY, ANY] + [INSIDE] * 5,
        input_output_aliases={8: 0, 9: 1},
        scratch_shapes=finish_scratch() + [vmem(PIECES, REST_ROWS, 128), vmem(D, 128, dtype=F32)],
        compiler_params=params(40),
        cost_estimate=cost(10_000_000, 20_000_000),
        name="finish",
    )(*own, *other, up, down, w_qkv, gain_one)


def neighbour(array, lat_by, lon_by):
    lat_count, lon_count = lax.axis_size("lat"), lax.axis_size("lon")
    pairs = []
    for i in range(lat_count):
        for j in range(lon_count):
            to = ((i + lat_by) % lat_count) * lon_count + (j + lon_by) % lon_count
            pairs.append((i * lon_count + j, to))
    return lax.ppermute(array, ("lat", "lon"), pairs)


def halos(grid):
    lon, lat, both = pack(grid)
    return neighbour(lat, -1, 0), neighbour(lon, 0, -1), neighbour(both, -1, -1)


def send_home(main, lon, lat, both):
    return main, neighbour(lon, 0, 1), neighbour(lat, 1, 0), neighbour(both, 1, 1)


def assemble(main, lon, lat, both):
    upper = jnp.concatenate([both, lat], 2)
    lower = jnp.concatenate([lon, main], 2)
    return jnp.concatenate([upper, lower], 1)


def along(array, stage, by):
    pairs = []
    for lat in range(16):
        for lon in range(8):
            core, chip = position(lat, lon)
            chip = list(chip)
            axis = ORDERS[core][stage]
            chip[axis] = (chip[axis] + by) % 4
            x, y, z = chip
            to = (z * 4 + y // 2 * 2 + core) * 8 + x * 2 + y % 2
            pairs.append((lat * 8 + lon, to))
    return lax.ppermute(array, ("lat", "lon"), pairs)


def other_core(array):
    return lax.ppermute(array, "lat", [(i, i ^ 1) for i in range(16)])


def added(*terms):
    total = terms[0].astype(F32)
    for term in terms[1:]:
        total = total + term.astype(F32)
    return total.astype(BF16)


def after(value, *others):
    return lax.optimization_barrier((value, others))[0]


def core_sum(keep, send):
    return added(keep, other_core(send))


def first_sum(held):
    return added(held[:4], *[along(held[4 * k : 4 * k + 4], 0, k) for k in (1, 2, 3)])


def second_sum(held):
    return added(held[0], *[along(held[k], 1, k) for k in (1, 2, 3)])


def last_sum(share):
    share = lax.optimization_barrier(share)
    one, two, three = [along(share, 2, k).astype(F32) for k in (1, 2, 3)]
    return ((share.astype(F32) + two) + (one + three)).astype(BF16)


def spread(share, before):
    held = jnp.stack([share] + [along(share, 1, k) for k in (1, 2, 3)])
    held = after(held, before)
    own = [held] + [along(held, 0, k) for k in (1, 2, 3)]
    return own, [other_core(piece) for piece in own]


def local(tokens, cotangent, w_qkv, w_proj, w_up, w_down, pair_bias, gain_one, gain_two):
    total_tokens = ROWS * lax.axis_size("lat") * lax.axis_size("lon")
    scale = total_tokens ** (-0.5)
    gain_one = gain_one.reshape(1, D)
    gain_two = gain_two.reshape(1, D)
    lat_edge, lon_edge, corner = halos(tokens)
    cot_lat, cot_lon, cot_corner = halos(cotangent)
    xw, mix, act_t, qkv, probs = attention(
        tokens, lon_edge, lat_edge, corner, w_qkv, pair_bias, gain_one
    )
    grad_mixed, grad_res, keep_one, send_one, sum_gain_two = mlp_call(
        xw, mix, cotangent, cot_lon, cot_lat, cot_corner, w_proj, w_up, w_down, gain_two
    )
    grads_first, bias = first_back(qkv, probs, grad_mixed)
    held_one = core_sum(keep_one, send_one)
    grads_second, keep_two, send_two = second_back(
        qkv, probs, grad_mixed, act_t, sum_gain_two, after(bias, held_one), grads_first
    )
    held_one = first_sum(held_one)
    held_two = first_sum(core_sum(keep_two, after(send_two, held_one)))
    share = second_sum(jnp.concatenate([held_one, held_two], 1))
    home = branch(xw, after(grads_first, share), grads_second, grad_res, w_qkv, gain_one)
    share = after(last_sum(share), home)
    home = send_home(*home)
    own, other = spread(share, home)
    up, down = finish_own(own, scale)
    sum_up, sum_down, sum_qkv, sum_proj, sum_bias, sum_one, sum_two = finish(
        own, other, up, down, w_qkv, gain_one, scale
    )
    return (
        assemble(*[after(piece, up) for piece in home]),
        sum_qkv,
        sum_proj,
        sum_up,
        sum_down,
        sum_bias,
        sum_one.reshape(D),
        sum_two.reshape(D),
    )


def solution(mesh):
    grid = P(None, "lat", "lon", None)
    in_specs = (grid, grid, P(), P(), P(), P(), P(), P(), P())
    out_specs = (grid, P(), P(), P(), P(), P(), P(), P())
    return jax.shard_map(local, mesh=mesh, in_specs=in_specs, out_specs=out_specs, check_vma=False)
```

profile of v0, /device:TPU:0, one launch (start us, length us, event | category | flops | bytes accessed | tf_op | source)
XLA Modules:
  0.0 178.4 jit_solution(4624965604492711723)
XLA Ops:
  0.6 1.3 copy-done.1
  2.0 6.3 %collective-permute-start.1 = (bf16[2,3,48,512]{3,2,1,0:T(8,128)(2,1)S(1)}, bf16[2,3,48,512]{3,2,1,0:T(8,128)(2,1)S(1)}, u32[]{:S(2)}, u32[]{:S(2)}) collective-permute-start(bf16[2,3,48,512]{3,2,1,0:T(8,128)(2,1)S(1)} %get-tuple-element.52), channel_id=1, source_target_pairs={{0,120},{1,121},{2,122},{3,123},{4,124},{5,125},{6,126},{7,127},{8... | collective-permute-start | bytes 884744 | tf_op jit(solution)/shard_map/ppermute | solution.py:744
  8.2 2.9 %collective-permute-start = (bf16[2,12,6,512]{3,2,1,0:T(8,128)(2,1)S(1)}, bf16[2,12,6,512]{3,2,1,0:T(8,128)(2,1)S(1)}, u32[]{:S(2)}, u32[]{:S(2)}) collective-permute-start(bf16[2,12,6,512]{3,2,1,0:T(8,128)(2,1)S(1)} %get-tuple-element.51), channel_id=1, source_target_pairs={{0,7},{1,0},{2,1},{3,2},{4,3},{5,4},{6,5},{7,6},{8,15},{9,8},{10,9... | collective-permute-start | bytes 442376 | tf_op jit(solution)/shard_map/ppermute | solution.py:744
  11.1 0.3 collective-permute-start.2
  11.4 1.3 copy-done.3
  12.7 2.2 %collective-permute-start.5 = (bf16[2,3,6,512]{3,2,1,0:T(8,128)(2,1)S(1)}, bf16[2,3,6,512]{3,2,1,0:T(8,128)(2,1)S(1)}, u32[]{:S(2)}, u32[]{:S(2)}) collective-permute-start(bf16[2,3,6,512]{3,2,1,0:T(8,128)(2,1)S(1)} %get-tuple-element.60), channel_id=1, source_target_pairs={{0,127},{1,120},{2,121},{3,122},{4,123},{5,124},{6,125},{7,126},{8... | collective-permute-start | bytes 110600 | tf_op jit(solution)/shard_map/ppermute | solution.py:744
  14.9 1.4 collective-permute-done.2.tok_both
  16.3 1.4 collective-permute-start.4
  17.7 12.3 %attention.1 = (bf16[1152,512]{1,0:T(8,128)(2,1)S(1)}, bf16[1152,512]{1,0:T(8,128)(2,1)S(1)}, bf16[512,1152]{1,0:T(8,128)(2,1)S(1)}, bf16[1152,1536]{1,0:T(8,128)(2,1)}, bf16[8,9,144,128]{3,2,1,0:T(8,128)(2,1)}) custom-call(bf16[2,12,48,512]{3,2,1,0:T(8,128)(2,1)S(1)} %copy-done.2, bf16[2,12,6,512]{3,2,1,0:T(8,128)(2,1)S(1)} %collective-permute-done.tok_lon, ...), custom_call_target="tpu_custom_call" | custom-call | flops 7247757312 | bytes 20000000 | tf_op jit(solution)/shard_map/attention/pallas_call | solution.py:596
  30.1 1.0 copy-done.9
  31.1 1.0 copy-done.11
  32.1 0.6 copy-done.16
  32.7 0.1 copy-done.15
  32.8 0.1 copy-done.14
  32.9 28.2 %mlp.1 = (bf16[1152,512]{1,0:T(8,128)(2,1)}, f32[1152,512]{1,0:T(8,128)}, bf16[16,576,128]{2,1,0:T(8,128)(2,1)}, bf16[16,576,128]{2,1,0:T(8,128)(2,1)}, f32[1,512]{1,0:T(1,128)}) custom-call(bf16[1152,512]{1,0:T(8,128)(2,1)} %copy-done.9, bf16[1152,512]{1,0:T(8,128)(2,1)} %copy-done.11, bf16[2,12,48,512]{3,2,1,0:T(8,128)(2,1)} %cot.1, ...), custom_call_target="tpu_custom_call" | custom-call | flops 19327352832 | bytes 40000000 | tf_op jit(solution)/shard_map/mlp/pallas_call | solution.py:616
  61.1 0.3 collective-permute-start.6
  61.4 1.3 copy-done.7
  62.7 3.7 %first_back.1 = (bf16[576,1536]{1,0:T(8,128)(2,1)S(1)}, f32[9,144,128]{2,1,0:T(8,128)S(1)}) custom-call(bf16[1152,1536]{1,0:T(8,128)(2,1)S(1)} %copy-done.5, bf16[8,9,144,128]{3,2,1,0:T(8,128)(2,1)S(1)} %copy-done.6, bf16[1152,512]{1,0:T(8,128)(2,1)S(1)} %copy-done.7), custom_call_target="tpu_custom_call" | custom-call | flops 5435817984 | bytes 10000000 | tf_op jit(solution)/shard_map/first_back/pallas_call | solution.py:647
  66.5 0.6 add_convert_fusion
  67.1 0.1 fusion.10
  67.2 3.7 %collective-permute-start.7 = (bf16[4,576,128]{2,1,0:T(8,128)(2,1)S(1)}, bf16[4,576,128]{2,1,0:T(8,128)(2,1)S(1)}, u32[]{:S(2)}, u32[]{:S(2)}) collective-permute-start(bf16[4,576,128]{2,1,0:T(8,128)(2,1)S(1)} %get-tuple-element.94), channel_id=1, source_target_pairs={{0,2},{1,3},{2,4},{3,5},{4,6},{5,7},{6,0},{7,1},{8,9},{9,24},{10,1... | collective-permute-start | bytes 1769480 | tf_op jit(solution)/shard_map/ppermute | solution.py:773
  70.9 0.1 collective-permute-start.9
  71.0 3.5 %collective-permute-start.8 = (bf16[4,576,128]{2,1,0:T(8,128)(2,1)S(1)}, bf16[4,576,128]{2,1,0:T(8,128)(2,1)S(1)}, u32[]{:S(2)}, u32[]{:S(2)}) collective-permute-start(bf16[4,576,128]{2,1,0:T(8,128)(2,1)S(1)} %get-tuple-element.96), channel_id=1, source_target_pairs={{0,4},{1,5},{2,6},{3,7},{4,0},{5,1},{6,2},{7,3},{8,24},{9,25},{10,... | collective-permute-start | bytes 1769480 | tf_op jit(solution)/shard_map/ppermute | solution.py:773
  74.5 8.2 %second_back.1 = (bf16[576,1536]{1,0:T(8,128)(2,1)S(1)}, bf16[16,240,128]{2,1,0:T(8,128)(2,1)S(1)}, bf16[16,240,128]{2,1,0:T(8,128)(2,1)S(1)}) custom-call(bf16[1152,1536]{1,0:T(8,128)(2,1)} %get-tuple-element.55.qkv, bf16[8,9,144,128]{3,2,1,0:T(8,128)(2,1)S(1)} %copy-done.6, bf16[1152,512]{1,0:T(8,128)(2,1)S(1)} %copy-done.7, ...), custom_call_target="tpu_custom_call" | custom-call | flops 7247757312 | bytes 10000000 | tf_op jit(solution)/shard_map/second_back/pallas_call | solution.py:663
  82.7 3.9 %collective-permute-done.8 = bf16[4,576,128]{2,1,0:T(8,128)(2,1)S(1)} collective-permute-done((bf16[4,576,128]{2,1,0:T(8,128)(2,1)S(1)}, bf16[4,576,128]{2,1,0:T(8,128)(2,1)S(1)}, u32[]{:S(2)}, u32[]{:S(2)}) %collective-permute-start.8) | collective-permute-done | bytes 589856 | tf_op jit(solution)/shard_map/ppermute | solution.py:773
  86.7 0.3 add_convert_fusion.2
  87.0 0.1 collective-permute-start.10
  87.1 2.6 %collective-permute-done.10 = bf16[16,240,128]{2,1,0:T(8,128)(2,1)S(1)} collective-permute-done((bf16[16,240,128]{2,1,0:T(8,128)(2,1)S(1)}, bf16[16,240,128]{2,1,0:T(8,128)(2,1)S(1)}, u32[]{:S(2)}, u32[]{:S(2)}) %collective-permute-start.10) | collective-permute-done | bytes 983072 | tf_op jit(solution)/shard_map/ppermute | solution.py:777
  89.6 0.3 add_convert_fusion.1
  90.0 2.1 %collective-permute-start.11 = (bf16[4,240,128]{2,1,0:T(8,128)(2,1)S(1)}, bf16[4,240,128]{2,1,0:T(8,128)(2,1)S(1)}, u32[]{:S(2)}, u32[]{:S(2)}) collective-permute-start(bf16[4,240,128]{2,1,0:T(8,128)(2,1)S(1)} %get-tuple-element.97), channel_id=1, source_target_pairs={{0,2},{1,3},{2,4},{3,5},{4,6},{5,7},{6,0},{7,1},{8,9},{9,24},{10,1... | collective-permute-start | bytes 737288 | tf_op jit(solution)/shard_map/ppermute | solution.py:773
  92.0 1.3 collective-permute-start.13
  93.3 1.4 collective-permute-start.12
  94.6 2.8 %collective-permute-done.11 = bf16[4,240,128]{2,1,0:T(8,128)(2,1)S(1)} collective-permute-done((bf16[4,240,128]{2,1,0:T(8,128)(2,1)S(1)}, bf16[4,240,128]{2,1,0:T(8,128)(2,1)S(1)}, u32[]{:S(2)}, u32[]{:S(2)}) %collective-permute-start.11) | collective-permute-done | bytes 245792 | tf_op jit(solution)/shard_map/ppermute | solution.py:773
  97.4 0.8 collective-permute-done.13
  98.2 3.2 %collective-permute-done.12 = bf16[4,240,128]{2,1,0:T(8,128)(2,1)S(1)} collective-permute-done((bf16[4,240,128]{2,1,0:T(8,128)(2,1)S(1)}, bf16[4,240,128]{2,1,0:T(8,128)(2,1)S(1)}, u32[]{:S(2)}, u32[]{:S(2)}) %collective-permute-start.12) | collective-permute-done | bytes 245792 | tf_op jit(solution)/shard_map/ppermute | solution.py:773
  101.4 0.1 add_convert_fusion.3
  101.6 3.3 %collective-permute-start.14 = (bf16[816,128]{1,0:T(8,128)(2,1)S(1)}, bf16[816,128]{1,0:T(8,128)(2,1)S(1)}, u32[]{:S(2)}, u32[]{:S(2)}) collective-permute-start(bf16[816,128]{1,0:T(8,128)(2,1)S(1)} %get-tuple-element.100), channel_id=1, source_target_pairs={{0,1},{1,16},{2,3},{3,18},{4,5},{5,20},{6,7},{7,22},{8,40},{9,41},... | collective-permute-start | bytes 626696 | tf_op jit(solution)/shard_map/ppermute | solution.py:773
  104.9 2.8 %collective-permute-start.15 = (bf16[816,128]{1,0:T(8,128)(2,1)S(1)}, bf16[816,128]{1,0:T(8,128)(2,1)S(1)}, u32[]{:S(2)}, u32[]{:S(2)}) collective-permute-start(bf16[816,128]{1,0:T(8,128)(2,1)S(1)} %get-tuple-element.102), channel_id=1, source_target_pairs={{0,16},{1,17},{2,18},{3,19},{4,20},{5,21},{6,22},{7,23},{8,72},{9,... | collective-permute-start | bytes 626696 | tf_op jit(solution)/shard_map/ppermute | solution.py:773
  107.7 1.0 collective-permute-done.14
  108.7 2.0 %collective-permute-done.16 = bf16[816,128]{1,0:T(8,128)(2,1)S(1)} collective-permute-done((bf16[816,128]{1,0:T(8,128)(2,1)S(1)}, bf16[816,128]{1,0:T(8,128)(2,1)S(1)}, u32[]{:S(2)}, u32[]{:S(2)}) %collective-permute-start.16) | collective-permute-done | bytes 208928 | tf_op jit(solution)/shard_map/ppermute | solution.py:773
  110.7 1.6 collective-permute-done.15
  112.2 0.1 fusion.2
  112.4 3.8 %collective-permute-start.20 = (bf16[816,128]{1,0:T(8,128)(2,1)S(1)}, bf16[816,128]{1,0:T(8,128)(2,1)S(1)}, u32[]{:S(2)}, u32[]{:S(2)}) collective-permute-start(bf16[816,128]{1,0:T(8,128)(2,1)S(1)} %fusion.2), channel_id=1, source_target_pairs={{0,96},{1,97},{2,98},{3,99},{4,100},{5,101},{6,102},{7,103},{8,14}... | collective-permute-start | bytes 626696 | tf_op jit(solution)/shard_map/ppermute | solution.py:773
  116.2 1.9 %collective-permute-start.18 = (bf16[816,128]{1,0:T(8,128)(2,1)S(1)}, bf16[816,128]{1,0:T(8,128)(2,1)S(1)}, u32[]{:S(2)}, u32[]{:S(2)}) collective-permute-start(bf16[816,128]{1,0:T(8,128)(2,1)S(1)} %fusion.2), channel_id=1, source_target_pairs={{0,64},{1,65},{2,66},{3,67},{4,68},{5,69},{6,70},{7,71},{8,12},{9,... | collective-permute-start | bytes 626696 | tf_op jit(solution)/shard_map/ppermute | solution.py:773
  118.0 3.2 %branch.1 = (bf16[2,9,42,512]{3,2,1,0:T(8,128)(2,1)S(1)}, bf16[2,9,6,512]{3,2,1,0:T(8,128)(2,1)S(1)}, bf16[2,3,42,512]{3,2,1,0:T(8,128)(2,1)S(1)}, bf16[2,3,6,512]{3,2,1,0:T(8,128)(2,1)S(1)}) custom-call(bf16[1152,512]{1,0:T(8,128)(2,1)S(1)} %copy-done.10, bf16[576,1536]{1,0:T(8,128)(2,1)S(1)} %get-tuple-element.72.grads_before.grads_first, ...), custom_call_target="tpu_custom_call" | custom-call | flops 7247757312 | bytes 10000000 | tf_op jit(solution)/shard_map/branch/pallas_call | solution.py:681
  121.3 4.1 %collective-permute-done.19 = bf16[816,128]{1,0:T(8,128)(2,1)S(1)} collective-permute-done((bf16[816,128]{1,0:T(8,128)(2,1)S(1)}, bf16[816,128]{1,0:T(8,128)(2,1)S(1)}, u32[]{:S(2)}, u32[]{:S(2)}) %collective-permute-start.19) | collective-permute-done | bytes 208928 | tf_op jit(solution)/shard_map/ppermute | solution.py:773
  125.4 0.1 add_convert_fusion.4
  125.5 2.0 %collective-permute-start.23 = (bf16[816,128]{1,0:T(8,128)(2,1)S(1)}, bf16[816,128]{1,0:T(8,128)(2,1)S(1)}, u32[]{:S(2)}, u32[]{:S(2)}) collective-permute-start(bf16[816,128]{1,0:T(8,128)(2,1)S(1)} %add_convert_fusion.4), channel_id=1, source_target_pairs={{0,17},{1,0},{2,19},{3,2},{4,21},{5,4},{6,23},{7,6},{8,104},{9,105... | collective-permute-start | bytes 626696 | tf_op jit(solution)/shard_map/ppermute | solution.py:773
  127.6 0.5 collective-permute-start.22
  128.0 0.7 collective-permute-start.21
  128.7 3.1 %collective-permute-start.17 = (bf16[2,3,6,512]{3,2,1,0:T(8,128)(2,1)S(1)}, bf16[2,3,6,512]{3,2,1,0:T(8,128)(2,1)S(1)}, u32[]{:S(2)}, u32[]{:S(2)}) collective-permute-start(bf16[2,3,6,512]{3,2,1,0:T(8,128)(2,1)S(1)} %get-tuple-element.75), channel_id=1, source_target_pairs={{0,9},{1,10},{2,11},{3,12},{4,13},{5,14},{6,15},{7,8},{8,17},{9,18... | collective-permute-start | bytes 110600 | tf_op jit(solution)/shard_map/ppermute | solution.py:744
  131.9 4.5 %collective-permute-done.23 = bf16[816,128]{1,0:T(8,128)(2,1)S(1)} collective-permute-done((bf16[816,128]{1,0:T(8,128)(2,1)S(1)}, bf16[816,128]{1,0:T(8,128)(2,1)S(1)}, u32[]{:S(2)}, u32[]{:S(2)}) %collective-permute-start.23) | collective-permute-done | bytes 208928 | tf_op jit(solution)/shard_map/ppermute | solution.py:773
  136.3 1.3 collective-permute-start.24
  137.7 2.6 %collective-permute-done.21 = bf16[816,128]{1,0:T(8,128)(2,1)S(1)} collective-permute-done((bf16[816,128]{1,0:T(8,128)(2,1)S(1)}, bf16[816,128]{1,0:T(8,128)(2,1)S(1)}, u32[]{:S(2)}, u32[]{:S(2)}) %collective-permute-start.21) | collective-permute-done | bytes 208928 | tf_op jit(solution)/shard_map/ppermute | solution.py:773
  140.2 0.1 pad_maximum_fusion.refs_0_
  140.3 3.3 %collective-permute-done.24 = bf16[2,9,6,512]{3,2,1,0:T(8,128)(2,1)S(1)} collective-permute-done((bf16[2,9,6,512]{3,2,1,0:T(8,128)(2,1)S(1)}, bf16[2,9,6,512]{3,2,1,0:T(8,128)(2,1)S(1)}, u32[]{:S(2)}, u32[]{:S(2)}) %collective-permute-start.24) | collective-permute-done | bytes 110624 | tf_op jit(solution)/shard_map/ppermute | solution.py:744
  143.7 0.2 collective-permute-start.28
  143.9 3.3 %collective-permute-start.27 = (bf16[4,816,128]{2,1,0:T(8,128)(2,1)S(1)}, bf16[4,816,128]{2,1,0:T(8,128)(2,1)S(1)}, u32[]{:S(2)}, u32[]{:S(2)}) collective-permute-start(bf16[4,816,128]{2,1,0:T(8,128)(2,1)S(1)} %pad_maximum_fusion.refs_0_), channel_id=1, source_target_pairs={{0,4},{1,5},{2,6},{3,7},{4,0},{5,1},{6,2},{7,3},{8,24},{9,25},{10,... | collective-permute-start | bytes 2506760 | tf_op jit(solution)/shard_map/ppermute | solution.py:773
  147.2 9.0 %collective-permute-done.28.refs_3_ = bf16[4,816,128]{2,1,0:T(8,128)(2,1)S(1)} collective-permute-done((bf16[4,816,128]{2,1,0:T(8,128)(2,1)S(1)}, bf16[4,816,128]{2,1,0:T(8,128)(2,1)S(1)}, u32[]{:S(2)}, u32[]{:S(2)}) %collective-permute-start.28) | collective-permute-done | bytes 835616 | tf_op jit(solution)/shard_map/ppermute | solution.py:773
  156.2 4.7 %collective-permute-start.32 = (bf16[4,816,128]{2,1,0:T(8,128)(2,1)S(1)}, bf16[4,816,128]{2,1,0:T(8,128)(2,1)S(1)}, u32[]{:S(2)}, u32[]{:S(2)}) collective-permute-start(bf16[4,816,128]{2,1,0:T(8,128)(2,1)S(1)} %collective-permute-done.28.refs_3_), channel_id=1, source_target_pairs={{0,8},{8,0},{16,24},{24,16},{32,40},{40,32},{48,56},{56,48},{64,72... | collective-permute-start | bytes 2506760 | tf_op jit(solution)/shard_map/ppermute | solution.py:777
  160.9 6.0 %collective-permute-done.26.refs_1_ = bf16[4,816,128]{2,1,0:T(8,128)(2,1)S(1)} collective-permute-done((bf16[4,816,128]{2,1,0:T(8,128)(2,1)S(1)}, bf16[4,816,128]{2,1,0:T(8,128)(2,1)S(1)}, u32[]{:S(2)}, u32[]{:S(2)}) %collective-permute-start.26) | collective-permute-done | bytes 835616 | tf_op jit(solution)/shard_map/ppermute | solution.py:773
  166.9 3.2 %finish_own.1 = (f32[512,2048]{1,0:T(8,128)}, f32[2048,512]{1,0:T(8,128)}) custom-call(bf16[4,816,128]{2,1,0:T(8,128)(2,1)S(1)} %pad_maximum_fusion.refs_0_, bf16[4,816,128]{2,1,0:T(8,128)(2,1)S(1)} %collective-permute-done.26.refs_1_, bf16[4,816,128]{2,1,0:T(8,128)(2,1)S(1)} %collective-permute-done.27.refs_2_, ...), custom_call_target="tpu_custom_call" | custom-call | flops 10000000 | bytes 10000000 | tf_op jit(solution)/shard_map/finish_own/pallas_call | solution.py:707
  170.1 1.6 maximum_maximum_fusion
  171.7 6.5 %finish.1 = (f32[512,2048]{1,0:T(8,128)}, f32[2048,512]{1,0:T(8,128)}, f32[512,1536]{1,0:T(8,128)}, f32[512,512]{1,0:T(8,128)}, f32[8,144,144]{2,1,0:T(8,128)}, /*index=5*/f32[1,512]{1,0:T(1,128)}, f32[1,512]{1,0:T(1,128)}) custom-call(bf16[4,816,128]{2,1,0:T(8,128)(2,1)S(1)} %pad_maximum_fusion.refs_0_, ...), custom_call_target="tpu_custom_call", output_to_operand_aliasing={{0}: (8, {}), {1}: (9, {})} | custom-call | flops 10000000 | bytes 20000000 | tf_op jit(solution)/shard_map/finish/pallas_call | solution.py:720
  (56 shorter events, 0.4 us)
Async XLA Ops:
  0.6 1.3 copy-start.1
  1.9 15.8 %copy-start.2 = (bf16[2,12,48,512]{3,2,1,0:T(8,128)(2,1)S(1)}, bf16[2,12,48,512]{3,2,1,0:T(8,128)(2,1)}, u32[]{:S(2)}) copy-start(bf16[2,12,48,512]{3,2,1,0:T(8,128)(2,1)} %tok.1) | copy-start | bytes 3538948
  1.9 15.8 %copy-start.4 = (f32[512]{0:T(512)S(1)}, f32[512]{0:T(512)}, u32[]{:S(2)}) copy-start(f32[512]{0:T(512)} %param.16) | copy-start | bytes 6148
  2.0 15.8 %collective-permute-start.1 = (bf16[2,3,48,512]{3,2,1,0:T(8,128)(2,1)S(1)}, bf16[2,3,48,512]{3,2,1,0:T(8,128)(2,1)S(1)}, u32[]{:S(2)}, u32[]{:S(2)}) collective-permute-start(bf16[2,3,48,512]{3,2,1,0:T(8,128)(2,1)S(1)} %get-tuple-element.52), channel_id=1, source_target_pairs={{0,120},{1,121},{2,122},{3,123},{4,124},{5,125},{6,126},{7,127},{8... | collective-permute-start | bytes 884744 | tf_op jit(solution)/shard_map/ppermute | solution.py:744
  8.2 9.5 %collective-permute-start = (bf16[2,12,6,512]{3,2,1,0:T(8,128)(2,1)S(1)}, bf16[2,12,6,512]{3,2,1,0:T(8,128)(2,1)S(1)}, u32[]{:S(2)}, u32[]{:S(2)}) collective-permute-start(bf16[2,12,6,512]{3,2,1,0:T(8,128)(2,1)S(1)} %get-tuple-element.51), channel_id=1, source_target_pairs={{0,7},{1,0},{2,1},{3,2},{4,3},{5,4},{6,5},{7,6},{8,15},{9,8},{10,9... | collective-permute-start | bytes 442376 | tf_op jit(solution)/shard_map/ppermute | solution.py:744
  11.1 5.2 %collective-permute-start.2 = (bf16[2,3,6,512]{3,2,1,0:T(8,128)(2,1)S(1)}, bf16[2,3,6,512]{3,2,1,0:T(8,128)(2,1)S(1)}, u32[]{:S(2)}, u32[]{:S(2)}) collective-permute-start(bf16[2,3,6,512]{3,2,1,0:T(8,128)(2,1)S(1)} %get-tuple-element.53), channel_id=1, source_target_pairs={{0,127},{1,120},{2,121},{3,122},{4,123},{5,124},{6,125},{7,126},{8... | collective-permute-start | bytes 110600 | tf_op jit(solution)/shard_map/ppermute | solution.py:744
  11.4 1.3 copy-start.3
  12.7 19.4 %collective-permute-start.5 = (bf16[2,3,6,512]{3,2,1,0:T(8,128)(2,1)S(1)}, bf16[2,3,6,512]{3,2,1,0:T(8,128)(2,1)S(1)}, u32[]{:S(2)}, u32[]{:S(2)}) collective-permute-start(bf16[2,3,6,512]{3,2,1,0:T(8,128)(2,1)S(1)} %get-tuple-element.60), channel_id=1, source_target_pairs={{0,127},{1,120},{2,121},{3,122},{4,123},{5,124},{6,125},{7,126},{8... | collective-permute-start | bytes 110600 | tf_op jit(solution)/shard_map/ppermute | solution.py:744
  14.9 17.2 %collective-permute-start.3 = (bf16[2,12,6,512]{3,2,1,0:T(8,128)(2,1)S(1)}, bf16[2,12,6,512]{3,2,1,0:T(8,128)(2,1)S(1)}, u32[]{:S(2)}, u32[]{:S(2)}) collective-permute-start(bf16[2,12,6,512]{3,2,1,0:T(8,128)(2,1)S(1)} %get-tuple-element.58), channel_id=1, source_target_pairs={{0,7},{1,0},{2,1},{3,2},{4,3},{5,4},{6,5},{7,6},{8,15},{9,8},{10,9... | collective-permute-start | bytes 442376 | tf_op jit(solution)/shard_map/ppermute | solution.py:744
  16.3 15.8 %collective-permute-start.4 = (bf16[2,3,48,512]{3,2,1,0:T(8,128)(2,1)S(1)}, bf16[2,3,48,512]{3,2,1,0:T(8,128)(2,1)S(1)}, u32[]{:S(2)}, u32[]{:S(2)}) collective-permute-start(bf16[2,3,48,512]{3,2,1,0:T(8,128)(2,1)S(1)} %get-tuple-element.59), channel_id=1, source_target_pairs={{0,120},{1,121},{2,122},{3,123},{4,124},{5,125},{6,126},{7,127},{8... | collective-permute-start | bytes 884744 | tf_op jit(solution)/shard_map/ppermute | solution.py:744
  30.1 1.0 copy-start.9
  31.1 1.0 copy-start.11
  32.1 0.6 copy-start.16
  32.1 0.7 copy-start.15
  32.1 0.8 copy-start.14
  32.9 28.5 %copy-start.5 = (bf16[1152,1536]{1,0:T(8,128)(2,1)S(1)}, bf16[1152,1536]{1,0:T(8,128)(2,1)}, u32[]{:S(2)}) copy-start(bf16[1152,1536]{1,0:T(8,128)(2,1)} %get-tuple-element.55.qkv) | copy-start | bytes 10616836
  32.9 28.5 %copy-start.6 = (bf16[8,9,144,128]{3,2,1,0:T(8,128)(2,1)S(1)}, bf16[8,9,144,128]{3,2,1,0:T(8,128)(2,1)}, u32[]{:S(2)}) copy-start(bf16[8,9,144,128]{3,2,1,0:T(8,128)(2,1)} %get-tuple-element.56.probs) | copy-start | bytes 7962628
  61.1 5.4 %collective-permute-start.6 = (bf16[16,576,128]{2,1,0:T(8,128)(2,1)}, bf16[16,576,128]{2,1,0:T(8,128)(2,1)S(1)}, u32[]{:S(2)}, u32[]{:S(2)}) collective-permute-start(bf16[16,576,128]{2,1,0:T(8,128)(2,1)} %get-tuple-element.64), channel_id=1, source_target_pairs={{0,8},{8,0},{16,24},{24,16},{32,40},{40,32},{48,56},{56,48},{64,72... | collective-permute-start | bytes 7077896 | tf_op jit(solution)/shard_map/ppermute | solution.py:777
  61.4 1.3 copy-start.7
  62.7 3.8 %copy-start.13 = (bf16[16,576,128]{2,1,0:T(8,128)(2,1)S(1)}, bf16[16,576,128]{2,1,0:T(8,128)(2,1)}, u32[]{:S(2)}) copy-start(bf16[16,576,128]{2,1,0:T(8,128)(2,1)} %get-tuple-element.63) | copy-start | bytes 7077892
  67.1 7.4 %copy-start.12 = (f32[1,512]{1,0:T(1,128)S(1)}, f32[1,512]{1,0:T(1,128)}, u32[]{:S(2)}) copy-start(f32[1,512]{1,0:T(1,128)} %get-tuple-element.66.sum_gain_two) | copy-start | bytes 6148
  67.2 15.5 %collective-permute-start.7 = (bf16[4,576,128]{2,1,0:T(8,128)(2,1)S(1)}, bf16[4,576,128]{2,1,0:T(8,128)(2,1)S(1)}, u32[]{:S(2)}, u32[]{:S(2)}) collective-permute-start(bf16[4,576,128]{2,1,0:T(8,128)(2,1)S(1)} %get-tuple-element.94), channel_id=1, source_target_pairs={{0,2},{1,3},{2,4},{3,5},{4,6},{5,7},{6,0},{7,1},{8,9},{9,24},{10,1... | collective-permute-start | bytes 1769480 | tf_op jit(solution)/shard_map/ppermute | solution.py:773
  70.9 11.8 %collective-permute-start.9 = (bf16[4,576,128]{2,1,0:T(8,128)(2,1)S(1)}, bf16[4,576,128]{2,1,0:T(8,128)(2,1)S(1)}, u32[]{:S(2)}, u32[]{:S(2)}) collective-permute-start(bf16[4,576,128]{2,1,0:T(8,128)(2,1)S(1)} %get-tuple-element.95), channel_id=1, source_target_pairs={{0,6},{1,7},{2,0},{3,1},{4,2},{5,3},{6,4},{7,5},{8,25},{9,8},{10,2... | collective-permute-start | bytes 1769480 | tf_op jit(solution)/shard_map/ppermute | solution.py:773
  71.0 15.7 %collective-permute-start.8 = (bf16[4,576,128]{2,1,0:T(8,128)(2,1)S(1)}, bf16[4,576,128]{2,1,0:T(8,128)(2,1)S(1)}, u32[]{:S(2)}, u32[]{:S(2)}) collective-permute-start(bf16[4,576,128]{2,1,0:T(8,128)(2,1)S(1)} %get-tuple-element.96), channel_id=1, source_target_pairs={{0,4},{1,5},{2,6},{3,7},{4,0},{5,1},{6,2},{7,3},{8,24},{9,25},{10,... | collective-permute-start | bytes 1769480 | tf_op jit(solution)/shard_map/ppermute | solution.py:773
  87.0 2.6 %collective-permute-start.10 = (bf16[16,240,128]{2,1,0:T(8,128)(2,1)S(1)}, bf16[16,240,128]{2,1,0:T(8,128)(2,1)S(1)}, u32[]{:S(2)}, u32[]{:S(2)}) collective-permute-start(bf16[16,240,128]{2,1,0:T(8,128)(2,1)S(1)} %get-tuple-element.71), channel_id=1, source_target_pairs={{0,8},{8,0},{16,24},{24,16},{32,40},{40,32},{48,56},{56,48},{64,72... | collective-permute-start | bytes 2949128 | tf_op jit(solution)/shard_map/ppermute | solution.py:777
  89.9 28.2 %copy-start.10 = (bf16[1152,512]{1,0:T(8,128)(2,1)S(1)}, bf16[1152,512]{1,0:T(8,128)(2,1)}, u32[]{:S(2)}) copy-start(bf16[1152,512]{1,0:T(8,128)(2,1)} %copy-done.9) | copy-start | bytes 3538948
  90.0 7.5 %collective-permute-start.11 = (bf16[4,240,128]{2,1,0:T(8,128)(2,1)S(1)}, bf16[4,240,128]{2,1,0:T(8,128)(2,1)S(1)}, u32[]{:S(2)}, u32[]{:S(2)}) collective-permute-start(bf16[4,240,128]{2,1,0:T(8,128)(2,1)S(1)} %get-tuple-element.97), channel_id=1, source_target_pairs={{0,2},{1,3},{2,4},{3,5},{4,6},{5,7},{6,0},{7,1},{8,9},{9,24},{10,1... | collective-permute-start | bytes 737288 | tf_op jit(solution)/shard_map/ppermute | solution.py:773
  92.0 6.2 %collective-permute-start.13 = (bf16[4,240,128]{2,1,0:T(8,128)(2,1)S(1)}, bf16[4,240,128]{2,1,0:T(8,128)(2,1)S(1)}, u32[]{:S(2)}, u32[]{:S(2)}) collective-permute-start(bf16[4,240,128]{2,1,0:T(8,128)(2,1)S(1)} %get-tuple-element.98), channel_id=1, source_target_pairs={{0,6},{1,7},{2,0},{3,1},{4,2},{5,3},{6,4},{7,5},{8,25},{9,8},{10,2... | collective-permute-start | bytes 737288 | tf_op jit(solution)/shard_map/ppermute | solution.py:773
  93.3 24.8 %copy-start = (bf16[512,1536]{1,0:T(8,128)(2,1)S(1)}, bf16[512,1536]{1,0:T(8,128)(2,1)}, u32[]{:S(2)}) copy-start(bf16[512,1536]{1,0:T(8,128)(2,1)} %refs_10_.1) | copy-start | bytes 4718596
  93.3 24.8 %copy-start.8 = (f32[1152,512]{1,0:T(8,128)S(1)}, f32[1152,512]{1,0:T(8,128)}, u32[]{:S(2)}) copy-start(f32[1152,512]{1,0:T(8,128)} %get-tuple-element.74.grad_res) | copy-start | bytes 7077892
  93.3 8.2 %collective-permute-start.12 = (bf16[4,240,128]{2,1,0:T(8,128)(2,1)S(1)}, bf16[4,240,128]{2,1,0:T(8,128)(2,1)S(1)}, u32[]{:S(2)}, u32[]{:S(2)}) collective-permute-start(bf16[4,240,128]{2,1,0:T(8,128)(2,1)S(1)} %get-tuple-element.99), channel_id=1, source_target_pairs={{0,4},{1,5},{2,6},{3,7},{4,0},{5,1},{6,2},{7,3},{8,24},{9,25},{10,... | collective-permute-start | bytes 737288 | tf_op jit(solution)/shard_map/ppermute | solution.py:773
  101.6 7.1 %collective-permute-start.14 = (bf16[816,128]{1,0:T(8,128)(2,1)S(1)}, bf16[816,128]{1,0:T(8,128)(2,1)S(1)}, u32[]{:S(2)}, u32[]{:S(2)}) collective-permute-start(bf16[816,128]{1,0:T(8,128)(2,1)S(1)} %get-tuple-element.100), channel_id=1, source_target_pairs={{0,1},{1,16},{2,3},{3,18},{4,5},{5,20},{6,7},{7,22},{8,40},{9,41},... | collective-permute-start | bytes 626696 | tf_op jit(solution)/shard_map/ppermute | solution.py:773
  104.9 5.8 %collective-permute-start.16 = (bf16[816,128]{1,0:T(8,128)(2,1)S(1)}, bf16[816,128]{1,0:T(8,128)(2,1)S(1)}, u32[]{:S(2)}, u32[]{:S(2)}) collective-permute-start(bf16[816,128]{1,0:T(8,128)(2,1)S(1)} %get-tuple-element.101), channel_id=1, source_target_pairs={{0,17},{1,0},{2,19},{3,2},{4,21},{5,4},{6,23},{7,6},{8,104},{9,105... | collective-permute-start | bytes 626696 | tf_op jit(solution)/shard_map/ppermute | solution.py:773
  104.9 7.3 %collective-permute-start.15 = (bf16[816,128]{1,0:T(8,128)(2,1)S(1)}, bf16[816,128]{1,0:T(8,128)(2,1)S(1)}, u32[]{:S(2)}, u32[]{:S(2)}) collective-permute-start(bf16[816,128]{1,0:T(8,128)(2,1)S(1)} %get-tuple-element.102), channel_id=1, source_target_pairs={{0,16},{1,17},{2,18},{3,19},{4,20},{5,21},{6,22},{7,23},{8,72},{9,... | collective-permute-start | bytes 626696 | tf_op jit(solution)/shard_map/ppermute | solution.py:773
  112.4 8.9 %collective-permute-start.20 = (bf16[816,128]{1,0:T(8,128)(2,1)S(1)}, bf16[816,128]{1,0:T(8,128)(2,1)S(1)}, u32[]{:S(2)}, u32[]{:S(2)}) collective-permute-start(bf16[816,128]{1,0:T(8,128)(2,1)S(1)} %fusion.2), channel_id=1, source_target_pairs={{0,96},{1,97},{2,98},{3,99},{4,100},{5,101},{6,102},{7,103},{8,14}... | collective-permute-start | bytes 626696 | tf_op jit(solution)/shard_map/ppermute | solution.py:773
  116.2 9.3 %collective-permute-start.19 = (bf16[816,128]{1,0:T(8,128)(2,1)S(1)}, bf16[816,128]{1,0:T(8,128)(2,1)S(1)}, u32[]{:S(2)}, u32[]{:S(2)}) collective-permute-start(bf16[816,128]{1,0:T(8,128)(2,1)S(1)} %fusion.2), channel_id=1, source_target_pairs={{0,32},{1,33},{2,34},{3,35},{4,36},{5,37},{6,38},{7,39},{8,10},{9,... | collective-permute-start | bytes 626696 | tf_op jit(solution)/shard_map/ppermute | solution.py:773
  116.2 9.3 %collective-permute-start.18 = (bf16[816,128]{1,0:T(8,128)(2,1)S(1)}, bf16[816,128]{1,0:T(8,128)(2,1)S(1)}, u32[]{:S(2)}, u32[]{:S(2)}) collective-permute-start(bf16[816,128]{1,0:T(8,128)(2,1)S(1)} %fusion.2), channel_id=1, source_target_pairs={{0,64},{1,65},{2,66},{3,67},{4,68},{5,69},{6,70},{7,71},{8,12},{9,... | collective-permute-start | bytes 626696 | tf_op jit(solution)/shard_map/ppermute | solution.py:773
  125.5 10.8 %collective-permute-start.23 = (bf16[816,128]{1,0:T(8,128)(2,1)S(1)}, bf16[816,128]{1,0:T(8,128)(2,1)S(1)}, u32[]{:S(2)}, u32[]{:S(2)}) collective-permute-start(bf16[816,128]{1,0:T(8,128)(2,1)S(1)} %add_convert_fusion.4), channel_id=1, source_target_pairs={{0,17},{1,0},{2,19},{3,2},{4,21},{5,4},{6,23},{7,6},{8,104},{9,105... | collective-permute-start | bytes 626696 | tf_op jit(solution)/shard_map/ppermute | solution.py:773
  127.6 10.1 %collective-permute-start.22 = (bf16[816,128]{1,0:T(8,128)(2,1)S(1)}, bf16[816,128]{1,0:T(8,128)(2,1)S(1)}, u32[]{:S(2)}, u32[]{:S(2)}) collective-permute-start(bf16[816,128]{1,0:T(8,128)(2,1)S(1)} %add_convert_fusion.4), channel_id=1, source_target_pairs={{0,16},{1,17},{2,18},{3,19},{4,20},{5,21},{6,22},{7,23},{8,72},{9,... | collective-permute-start | bytes 626696 | tf_op jit(solution)/shard_map/ppermute | solution.py:773
  128.0 12.2 %collective-permute-start.21 = (bf16[816,128]{1,0:T(8,128)(2,1)S(1)}, bf16[816,128]{1,0:T(8,128)(2,1)S(1)}, u32[]{:S(2)}, u32[]{:S(2)}) collective-permute-start(bf16[816,128]{1,0:T(8,128)(2,1)S(1)} %add_convert_fusion.4), channel_id=1, source_target_pairs={{0,1},{1,16},{2,3},{3,18},{4,5},{5,20},{6,7},{7,22},{8,40},{9,41},... | collective-permute-start | bytes 626696 | tf_op jit(solution)/shard_map/ppermute | solution.py:773
  128.7 14.9 %collective-permute-start.25 = (bf16[2,3,42,512]{3,2,1,0:T(8,128)(2,1)S(1)}, bf16[2,3,42,512]{3,2,1,0:T(8,128)(2,1)S(1)}, u32[]{:S(2)}, u32[]{:S(2)}) collective-permute-start(bf16[2,3,42,512]{3,2,1,0:T(8,128)(2,1)S(1)} %get-tuple-element.78), channel_id=1, source_target_pairs={{0,8},{1,9},{2,10},{3,11},{4,12},{5,13},{6,14},{7,15},{8,16},{9,17... | collective-permute-start | bytes 774152 | tf_op jit(solution)/shard_map/ppermute | solution.py:744
  128.7 11.6 %collective-permute-start.17 = (bf16[2,3,6,512]{3,2,1,0:T(8,128)(2,1)S(1)}, bf16[2,3,6,512]{3,2,1,0:T(8,128)(2,1)S(1)}, u32[]{:S(2)}, u32[]{:S(2)}) collective-permute-start(bf16[2,3,6,512]{3,2,1,0:T(8,128)(2,1)S(1)} %get-tuple-element.75), channel_id=1, source_target_pairs={{0,9},{1,10},{2,11},{3,12},{4,13},{5,14},{6,15},{7,8},{8,17},{9,18... | collective-permute-start | bytes 110600 | tf_op jit(solution)/shard_map/ppermute | solution.py:744
  136.3 7.4 %collective-permute-start.24 = (bf16[2,9,6,512]{3,2,1,0:T(8,128)(2,1)S(1)}, bf16[2,9,6,512]{3,2,1,0:T(8,128)(2,1)S(1)}, u32[]{:S(2)}, u32[]{:S(2)}) collective-permute-start(bf16[2,9,6,512]{3,2,1,0:T(8,128)(2,1)S(1)} %get-tuple-element.77), channel_id=1, source_target_pairs={{0,1},{1,2},{2,3},{3,4},{4,5},{5,6},{6,7},{7,0},{8,9},{9,10},{10,1... | collective-permute-start | bytes 331784 | tf_op jit(solution)/shard_map/ppermute | solution.py:744
  143.7 12.5 %collective-permute-start.28 = (bf16[4,816,128]{2,1,0:T(8,128)(2,1)S(1)}, bf16[4,816,128]{2,1,0:T(8,128)(2,1)S(1)}, u32[]{:S(2)}, u32[]{:S(2)}) collective-permute-start(bf16[4,816,128]{2,1,0:T(8,128)(2,1)S(1)} %pad_maximum_fusion.refs_0_), channel_id=1, source_target_pairs={{0,6},{1,7},{2,0},{3,1},{4,2},{5,3},{6,4},{7,5},{8,25},{9,8},{10,2... | collective-permute-start | bytes 2506760 | tf_op jit(solution)/shard_map/ppermute | solution.py:773
  143.9 17.0 %collective-permute-start.27 = (bf16[4,816,128]{2,1,0:T(8,128)(2,1)S(1)}, bf16[4,816,128]{2,1,0:T(8,128)(2,1)S(1)}, u32[]{:S(2)}, u32[]{:S(2)}) collective-permute-start(bf16[4,816,128]{2,1,0:T(8,128)(2,1)S(1)} %pad_maximum_fusion.refs_0_), channel_id=1, source_target_pairs={{0,4},{1,5},{2,6},{3,7},{4,0},{5,1},{6,2},{7,3},{8,24},{9,25},{10,... | collective-permute-start | bytes 2506760 | tf_op jit(solution)/shard_map/ppermute | solution.py:773
  147.2 19.7 %collective-permute-start.26 = (bf16[4,816,128]{2,1,0:T(8,128)(2,1)S(1)}, bf16[4,816,128]{2,1,0:T(8,128)(2,1)S(1)}, u32[]{:S(2)}, u32[]{:S(2)}) collective-permute-start(bf16[4,816,128]{2,1,0:T(8,128)(2,1)S(1)} %pad_maximum_fusion.refs_0_), channel_id=1, source_target_pairs={{0,2},{1,3},{2,4},{3,5},{4,6},{5,7},{6,0},{7,1},{8,9},{9,24},{10,1... | collective-permute-start | bytes 2506760 | tf_op jit(solution)/shard_map/ppermute | solution.py:773
  147.2 24.5 %collective-permute-start.29 = (bf16[4,816,128]{2,1,0:T(8,128)(2,1)S(1)}, bf16[4,816,128]{2,1,0:T(8,128)(2,1)S(1)}, u32[]{:S(2)}, u32[]{:S(2)}) collective-permute-start(bf16[4,816,128]{2,1,0:T(8,128)(2,1)S(1)} %pad_maximum_fusion.refs_0_), channel_id=1, source_target_pairs={{0,8},{8,0},{16,24},{24,16},{32,40},{40,32},{48,56},{56,48},{64,72... | collective-permute-start | bytes 2506760 | tf_op jit(solution)/shard_map/ppermute | solution.py:777
  156.2 15.5 %collective-permute-start.32 = (bf16[4,816,128]{2,1,0:T(8,128)(2,1)S(1)}, bf16[4,816,128]{2,1,0:T(8,128)(2,1)S(1)}, u32[]{:S(2)}, u32[]{:S(2)}) collective-permute-start(bf16[4,816,128]{2,1,0:T(8,128)(2,1)S(1)} %collective-permute-done.28.refs_3_), channel_id=1, source_target_pairs={{0,8},{8,0},{16,24},{24,16},{32,40},{40,32},{48,56},{56,48},{64,72... | collective-permute-start | bytes 2506760 | tf_op jit(solution)/shard_map/ppermute | solution.py:777
  160.9 10.8 %collective-permute-start.31 = (bf16[4,816,128]{2,1,0:T(8,128)(2,1)S(1)}, bf16[4,816,128]{2,1,0:T(8,128)(2,1)S(1)}, u32[]{:S(2)}, u32[]{:S(2)}) collective-permute-start(bf16[4,816,128]{2,1,0:T(8,128)(2,1)S(1)} %collective-permute-done.27.refs_2_), channel_id=1, source_target_pairs={{0,8},{8,0},{16,24},{24,16},{32,40},{40,32},{48,56},{56,48},{64,72... | collective-permute-start | bytes 2506760 | tf_op jit(solution)/shard_map/ppermute | solution.py:777
  166.9 4.8 %collective-permute-start.30 = (bf16[4,816,128]{2,1,0:T(8,128)(2,1)S(1)}, bf16[4,816,128]{2,1,0:T(8,128)(2,1)S(1)}, u32[]{:S(2)}, u32[]{:S(2)}) collective-permute-start(bf16[4,816,128]{2,1,0:T(8,128)(2,1)S(1)} %collective-permute-done.26.refs_1_), channel_id=1, source_target_pairs={{0,8},{8,0},{16,24},{24,16},{32,40},{40,32},{48,56},{56,48},{64,72... | collective-permute-start | bytes 2506760 | tf_op jit(solution)/shard_map/ppermute | solution.py:777
where the time goes:
time: 180 us; the launch traced here: 178 us
  Pallas kernels  65.5 us (36%)
  starting transfers between devices  52.9 us (29%)
  waiting for transfers between devices  48.8 us (27%)
  local copies, waits for them, and re-layouts  6.79 us (4%)
  other arithmetic  3.33 us (2%)
    ppermute x18, waiting for transfers between devices, along(): return lax.ppermute(array, ('lat', 'lon'), pairs)  41.4 us
    ppermute x18, starting transfers between devices, along(): return lax.ppermute(array, ('lat', 'lon'), pairs)  30.4 us
    pallas_call x1, Pallas kernels, mlp_call(): pl.pallas_call(mlp_kernel, out_shape=(shape(ROWS, D), shape(ROWS, D, dtyp...  28.2 us
    ppermute x9, starting transfers between devices, neighbour(): return lax.ppermute(array, ('lat', 'lon'), pairs)  17.4 us
    pallas_call x1, Pallas kernels, attention(): pl.pallas_call(attention_kernel, out_shape=(shape(ROWS, D), shape(ROWS, D...  12.3 us
    pallas_call x1, Pallas kernels, second_back(): pl.pallas_call(second_back_kernel, out_shape=(shape(ROWS // 2, QKV), shap...  8.21 us
    unnamed x34, local copies, waits for them, and re-layouts  6.62 us
    pallas_call x1, Pallas kernels, finish(): pl.pallas_call(functools.partial(finish_kernel, scale), out_shape=(shape(...  6.51 us
  transfers between devices with their start and end apart: 33, of which 16 were waited for; matrix products, arithmetic and copies ran while one was open for 1% of the time, Pallas kernels for 17%

commit v1 on v0

--- a/solution.py
+++ b/solution.py
@@ -161,10 +161,12 @@
 
 def attention_kernel(
     tok, tok_lon, tok_lat, tok_both, w_qkv, pair_bias, gain_one,
-    xw, mix, act_t, qkv_out, probs_out,
-    line, wide, act, qkv, probs, bias, sent,
+    xw_out, mix_out, act_t_out, qkv_out, probs_out,
+    line, wide, act, qkv, probs, bias, xw, mix, act_t, sent,
 ):
     gather_windows(tok, tok_lon, tok_lat, tok_both, line, wide, xw)
+    copies = [pltpu.make_async_copy(xw, xw_out, sent.at[WINDOWS + 1])]
+    copies[0].start()
 
     def norm_one(window, _):
         rows = window_rows(window)
@@ -180,9 +182,11 @@
         return 0
 
     lax.fori_loop(0, QKV // 256, project, 0)
-    copies = [pltpu.make_async_copy(qkv, qkv_out, sent.at[WINDOWS])]
-    copies[0].start()
     act_t[...] = act[...].T
+    copies.append(pltpu.make_async_copy(qkv, qkv_out, sent.at[WINDOWS]))
+    copies.append(pltpu.make_async_copy(act_t, act_t_out, sent.at[WINDOWS + 2]))
+    for copy in copies[1:]:
+        copy.start()
 
     is_last = lax.axis_index("lat") == lax.axis_size("lat") - 1
     key_at = lax.broadcasted_iota(jnp.int32, (WT, 128), 0)
@@ -205,6 +209,10 @@
     first, halves, tail = head_masks()
     halves = [half * 0.125 for half in halves]
     tail_low = (tail * 0.125).astype(BF16)
+
+    def mix_copy(group):
+        at = pl.ds(pl.multiple_of(group * G_FORWARD * WT, 16), G_FORWARD * WT)
+        return pltpu.make_async_copy(mix.at[at], mix_out.at[at], sent.at[WINDOWS + 3 + group])
 
     def attend(group, _):
         windows = [group * G_FORWARD + i for i in range(G_FORWARD)]
@@ -239,10 +247,12 @@
                 mix[main[i], pair_of(head)] = jnp.where(first, mixed[n], mixed[n + 1]).astype(BF16)
         for window in windows:
             pltpu.make_async_copy(probs.at[window], probs_out.at[window], sent.at[window]).start()
+        mix_copy(group).start()
         return 0
 
     lax.fori_loop(0, WINDOWS // G_FORWARD, attend, 0)
-    copies[0].wait()
+    for copy in copies + [mix_copy(group) for group in range(WINDOWS // G_FORWARD)]:
+        copy.wait()
     for window in range(WINDOWS):
         pltpu.make_async_copy(probs.at[window], probs_out.at[window], sent.at[window]).wait()
 
@@ -480,71 +490,85 @@
             outer[level, at] = line[BREADTH - 6 : BREADTH].astype(BF16)
 
 
-def write_bands(scale, owner, pieces, up_out, down_out, buffer_up, buffer_down, sent):
-    depth = buffer_up.shape[0]
-
-    def run(buffer, rows, fill, out):
-        def copy(n, block):
-            at = pl.ds(pl.multiple_of(block * rows, rows), rows)
-            return pltpu.make_async_copy(buffer.at[n % depth], out.at[at], sent.at[n % depth])
+def write_pieces(scale, owner, pieces, w_qkv, outs, sums, rest, buffers, sent):
+    up_out, down_out, qkv_out, proj_out = outs
+    buffer_up, buffer_down, buffer_qkv, buffer_proj = buffers
+
+    def run(buffer_band, band, fill_band, band_out):
+        def copies(n):
+            block = block_at(owner, n // 4, n % 4)
+            piece = owner * 16 + block
+            slot = n % BUFFERS
+            targets = ((buffer_band, band_out, band, block), (buffer_qkv, qkv_out, 16, piece),
+                       (buffer_proj, proj_out, 16, piece))
+            return [
+                pltpu.make_async_copy(
+                    buffer.at[slot],
+                    out.at[pl.ds(pl.multiple_of(at * size, size), size)],
+                    sent.at[i, slot],
+                )
+                for i, (buffer, out, size, at) in enumerate(targets)
+            ]
 
         for n in range(16):
-            block = block_at(owner, n // 4, n % 4)
-            if n >= depth:
-                copy(n, block).wait()
-            fill(n)
-            copy(n, block).start()
-        for n in range(16 - depth, 16):
-            copy(n, block_at(owner, n // 4, n % 4)).wait()
-
-    def fill_up(n):
-        for j in range(16):
-            part = pieces[n // 4][n % 4, 32 * j : 32 * j + 32]
-            buffer_up[n % depth, :, 128 * j : 128 * j + 128] = part.astype(F32) * scale
-
-    def fill_down(n):
-        for j in range(4):
-            part = pieces[n // 4][n % 4, 128 * j : 128 * j + 128]
-            buffer_down[n % depth, :, 128 * j : 128 * j + 128] = part.astype(F32) * scale
-
-    @pl.when(owner == 0)
-    def _():
-        run(buffer_up, 32, fill_up, up_out)
-
-    @pl.when(owner == 1)
-    def _():
-        run(buffer_down, 128, fill_down, down_out)
-
-
-def finish_own_kernel(scale, *refs):
-    pieces, (up_out, down_out, buffer_up, buffer_down, sent) = refs[:4], refs[4:]
-    write_bands(scale, here()[0], pieces, up_out, down_out, buffer_up, buffer_down, sent)
-
-
-def finish_kernel(scale, *refs):
-    own, other, (up_in, down_in, w_qkv, gain_vec) = refs[:4], refs[4:8], refs[8:12]
-    up_out, down_out, qkv, proj, bias, gain_one, gain_two = refs[12:19]
-    buffer_up, buffer_down, sent, rest, sums = refs[19:]
-    core, _ = here()
-    write_bands(scale, 1 - core, other, up_out, down_out, buffer_up, buffer_down, sent)
-    for owner, pieces in ((core, own), (1 - core, other)):
-        for n in range(16):
+            if n >= BUFFERS:
+                for copy in copies(n - BUFFERS):
+                    copy.wait()
+            slot = n % BUFFERS
             piece = owner * 16 + block_at(owner, n // 4, n % 4)
             rows = pl.ds(pl.multiple_of(piece * 16, 16), 16)
             held = pieces[n // 4]
+            fill_band(held, n % 4, slot)
             for j in range(4):
                 at = BAND_ROWS + 16 * j
                 part = held[n % 4, at : at + 16].astype(F32) * scale
-                proj[rows, 128 * j : 128 * j + 128] = part
+                buffer_proj[slot, :, 128 * j : 128 * j + 128] = part
             total = jnp.zeros((16, 128), F32)
             for j in range(12):
                 cols = slice(128 * j, 128 * j + 128)
                 at = ONE_ROWS + 16 * j
                 part = held[n % 4, at : at + 16].astype(F32) * scale
-                qkv[rows, cols] = part
+                buffer_qkv[slot, :, cols] = part
                 total = total + part * w_qkv[rows, cols].astype(F32)
             sums[rows] = total
             rest[piece] = held[n % 4, ONE_ROWS + QKV_ROWS : ALL_ROWS]
+            for copy in copies(n):
+                copy.start()
+        for n in range(16 - BUFFERS, 16):
+            for copy in copies(n):
+                copy.wait()
+
+    def fill_up(held, at, slot):
+        for j in range(16):
+            part = held[at, 32 * j : 32 * j + 32].astype(F32) * scale
+            buffer_up[slot, :, 128 * j : 128 * j + 128] = part
+
+    def fill_down(held, at, slot):
+        for j in range(4):
+            part = held[at, 128 * j : 128 * j + 128].astype(F32) * scale
+            buffer_down[slot, :, 128 * j : 128 * j + 128] = part
+
+    @pl.when(owner == 0)
+    def _():
+        run(buffer_up, 32, fill_up, up_out)
+
+    @pl.when(owner == 1)
+    def _():
+        run(buffer_down, 128, fill_down, down_out)
+
+
+def finish_own_kernel(scale, *refs):
+    pieces, w_qkv, outs, sums, rest = refs[:4], refs[4], refs[5:9], refs[9], refs[10]
+    write_pieces(scale, here()[0], pieces, w_qkv, outs, sums, rest, refs[11:15], refs[15])
+
+
+def finish_kernel(scale, *refs):
+    pieces, w_qkv, gain_vec, sums_own, rest_own = refs[:4], refs[4], refs[5], refs[6], refs[7]
+    outs, (bias, gain_one, gain_two) = refs[12:16], refs[16:19]
+    buffers, sent, sums, rest = refs[19:23], refs[23], refs[24], refs[25]
+    sums[...] = sums_own[...]
+    rest[...] = rest_own[...]
+    write_pieces(scale, 1 - here()[0], pieces, w_qkv, outs, sums, rest, buffers, sent)
     gain_one[...] = jnp.sum(sums[...].T, 0, keepdims=True) / gain_vec[...]
     flat = rest[...].reshape(PIECES * REST_ROWS, 128).astype(F32)
     last = flat[HEADS * WT : GAIN_AT].T * (scale * WT)
@@ -600,13 +624,14 @@
             shape(WINDOWS, HEADS + 1, WT, 128),
         ),
         in_specs=[INSIDE] * len(operands),
-        out_specs=[INSIDE, INSIDE, INSIDE, ANY, ANY],
+        out_specs=[ANY] * 5,
         scratch_shapes=[
             vmem(56, D, dtype=F32), vmem(ROWS, D, dtype=F32), vmem(ROWS, D), vmem(ROWS, QKV),
             vmem(WINDOWS, HEADS + 1, WT, 128), vmem(2, HEADS + 1, WT, 128, dtype=F32),
-            pltpu.SemaphoreType.DMA((WINDOWS + 1,)),
+            vmem(ROWS, D), vmem(ROWS, D), vmem(D, ROWS),
+            pltpu.SemaphoreType.DMA((WINDOWS + 3 + WINDOWS // G_FORWARD,)),
         ],
-        compiler_params=params(48),
+        compiler_params=params(60),
         cost_estimate=cost(ROWS * D * QKV * 2 * 4, 20_000_000),
         name="attention",
     )(*operands)
@@ -699,39 +724,46 @@
 def finish_scratch():
     return [
         vmem(BUFFERS, 32, FF, dtype=F32), vmem(BUFFERS, 128, D, dtype=F32),
-        pltpu.SemaphoreType.DMA((BUFFERS,)),
+        vmem(BUFFERS, 16, QKV, dtype=F32), vmem(BUFFERS, 16, D, dtype=F32),
+        pltpu.SemaphoreType.DMA((3, BUFFERS)),
     ]
 
 
-def finish_own(pieces, scale):
+WEIGHT_SHAPES = (
+    shape(D, FF, dtype=F32), shape(FF, D, dtype=F32), shape(D, QKV, dtype=F32),
+    shape(D, D, dtype=F32),
+)
+
+
+def finish_own(pieces, w_qkv, scale):
     return pl.pallas_call(
         functools.partial(finish_own_kernel, scale),
-        out_shape=(shape(D, FF, dtype=F32), shape(FF, D, dtype=F32)),
-        in_specs=[INSIDE] * 4,
-        out_specs=[ANY, ANY],
+        out_shape=WEIGHT_SHAPES + (shape(D, 128, dtype=F32), shape(PIECES, REST_ROWS, 128)),
+        in_specs=[INSIDE] * 5,
+        out_specs=[ANY] * 4 + [INSIDE] * 2,
         scratch_shapes=finish_scratch(),
         compiler_params=params(24),
         cost_estimate=cost(10_000_000, 10_000_000),
         name="finish_own",
-    )(*pieces)
-
-
-def finish(own, other, up, down, w_qkv, gain_one, scale):
+    )(*pieces, w_qkv)
+
+
+def finish(pieces, w_qkv, gain_one, sums, rest, weights, scale):
     return pl.pallas_call(
         functools.partial(finish_kernel, scale),
-        out_shape=(
-            shape(D, FF, dtype=F32), shape(FF, D, dtype=F32), shape(D, QKV, dtype=F32),
-            shape(D, D, dtype=F32), shape(HEADS, WT, WT, dtype=F32), shape(1, D, dtype=F32),
-            shape(1, D, dtype=F32),
+        out_shape=WEIGHT_SHAPES + (
+            shape(HEADS, WT, WT, dtype=F32), shape(1, D, dtype=F32), shape(1, D, dtype=F32),
         ),
-        in_specs=[INSIDE] * 8 + [ANY, ANY, INSIDE, INSIDE],
-        out_specs=[ANY, ANY] + [INSIDE] * 5,
-        input_output_aliases={8: 0, 9: 1},
-        scratch_shapes=finish_scratch() + [vmem(PIECES, REST_ROWS, 128), vmem(D, 128, dtype=F32)],
-        compiler_params=params(40),
-        cost_estimate=cost(10_000_000, 20_000_000),
+        in_specs=[INSIDE] * 8 + [ANY] * 4,
+        out_specs=[ANY] * 4 + [INSIDE] * 3,
+        input_output_aliases={8: 0, 9: 1, 10: 2, 11: 3},
+        scratch_shapes=finish_scratch() + [
+            vmem(D, 128, dtype=F32), vmem(PIECES, REST_ROWS, 128),
+        ],
+        compiler_params=params(24),
+        cost_estimate=cost(10_000_000, 10_000_000),
         name="finish",
-    )(*own, *other, up, down, w_qkv, gain_one)
+    )(*pieces, w_qkv, gain_one, sums, rest, *weights)
 
 
 def neighbour(array, lat_by, lon_by):
@@ -838,12 +870,12 @@
     share = after(last_sum(share), home)
     home = send_home(*home)
     own, other = spread(share, home)
-    up, down = finish_own(own, scale)
+    *weights, sums, rest = finish_own(own, w_qkv, scale)
     sum_up, sum_down, sum_qkv, sum_proj, sum_bias, sum_one, sum_two = finish(
-        own, other, up, down, w_qkv, gain_one, scale
+        other, w_qkv, gain_one, sums, rest, weights, scale
     )
     return (
-        assemble(*[after(piece, up) for piece in home]),
+        assemble(*[after(piece, sums) for piece in home]),
         sum_qkv,
         sum_proj,
         sum_up,

time: 180 us -> 178 us (0.989)
  waiting for transfers between devices: 48.8 us -> 58.1 us
  starting transfers between devices: 52.9 us -> 43.7 us
    ppermute x18, waiting for transfers between devices: 41.4 us -> 53.4 us  [along(): return lax.ppermute(array, ('lat', 'lon'), pairs)]
    ppermute x18, starting transfers between devices: 30.4 us -> 21.1 us  [along(): return lax.ppermute(array, ('lat', 'lon'), pairs)]
    ppermute x9, starting transfers between devices: 17.4 us -> 21.4 us  [neighbour(): return lax.ppermute(array, ('lat', 'lon'), pairs)]
    ppermute x6, starting transfers between devices: 5.1 us -> 1.16 us  [other_core(): return lax.ppermute(array, 'lat', [(i, i ^ 1) for i in range(16)])]
    ppermute x9, waiting for transfers between devices: 4.8 us -> 2.14 us  [neighbour(): return lax.ppermute(array, ('lat', 'lon'), pairs)]
    unnamed x34 -> x36, local copies, waits for them, and re-layouts: 6.62 us -> 5.35 us
  transfers between devices with their start and end apart: 33 -> 33, of which waited for: 16 -> 17; matrix products, arithmetic and copies ran while one was open for 1% -> 1% of each run, Pallas kernels for 17% -> 18%
where the time goes in v1:
time: 178 us; the launch traced here: 177 us
  Pallas kernels  64.7 us (36%)
  waiting for transfers between devices  58.1 us (33%)
  starting transfers between devices  43.7 us (25%)
  local copies, waits for them, and re-layouts  5.52 us (3%)
  other arithmetic  3.33 us (2%)
    ppermute x18, waiting for transfers between devices, along(): return lax.ppermute(array, ('lat', 'lon'), pairs)  53.4 us
    pallas_call x1, Pallas kernels, mlp_call(): pl.pallas_call(mlp_kernel, out_shape=(shape(ROWS, D), shape(ROWS, D, dtyp...  28.2 us
    ppermute x9, starting transfers between devices, neighbour(): return lax.ppermute(array, ('lat', 'lon'), pairs)  21.4 us
    ppermute x18, starting transfers between devices, along(): return lax.ppermute(array, ('lat', 'lon'), pairs)  21.1 us
    pallas_call x1, Pallas kernels, attention(): pl.pallas_call(attention_kernel, out_shape=(shape(ROWS, D), shape(ROWS, D...  12.9 us
    pallas_call x1, Pallas kernels, second_back(): pl.pallas_call(second_back_kernel, out_shape=(shape(ROWS // 2, QKV), shap...  8.22 us
    unnamed x36, local copies, waits for them, and re-layouts  5.35 us
    pallas_call x1, Pallas kernels, finish(): pl.pallas_call(functools.partial(finish_kernel, scale), out_shape=WEIGHT_...  4.94 us
  transfers between devices with their start and end apart: 33, of which 17 were waited for; matrix products, arithmetic and copies ran while one was open for 1% of the time, Pallas kernels for 18%

profile of v1, /device:TPU:0, one launch (start us, length us, event | category | flops | bytes accessed | tf_op | source)
XLA Modules:
  0.0 176.5 jit_solution(3750082427576612309)
XLA Ops:
  0.6 1.3 copy-done.1
  1.9 6.3 %collective-permute-start.1 = (bf16[2,3,48,512]{3,2,1,0:T(8,128)(2,1)S(1)}, bf16[2,3,48,512]{3,2,1,0:T(8,128)(2,1)S(1)}, u32[]{:S(2)}, u32[]{:S(2)}) collective-permute-start(bf16[2,3,48,512]{3,2,1,0:T(8,128)(2,1)S(1)} %get-tuple-element.56), channel_id=1, source_target_pairs={{0,120},{1,121},{2,122},{3,123},{4,124},{5,125},{6,126},{7,127},{8... | collective-permute-start | bytes 884744 | tf_op jit(solution)/shard_map/ppermute | solution.py:776
  8.2 2.9 %collective-permute-start = (bf16[2,12,6,512]{3,2,1,0:T(8,128)(2,1)S(1)}, bf16[2,12,6,512]{3,2,1,0:T(8,128)(2,1)S(1)}, u32[]{:S(2)}, u32[]{:S(2)}) collective-permute-start(bf16[2,12,6,512]{3,2,1,0:T(8,128)(2,1)S(1)} %get-tuple-element.55), channel_id=1, source_target_pairs={{0,7},{1,0},{2,1},{3,2},{4,3},{5,4},{6,5},{7,6},{8,15},{9,8},{10,9... | collective-permute-start | bytes 442376 | tf_op jit(solution)/shard_map/ppermute | solution.py:776
  11.1 0.3 collective-permute-start.2
  11.4 1.3 copy-done.2
  12.7 1.1 collective-permute-start.3
  13.8 2.2 %collective-permute-start.4 = (bf16[2,3,48,512]{3,2,1,0:T(8,128)(2,1)S(1)}, bf16[2,3,48,512]{3,2,1,0:T(8,128)(2,1)S(1)}, u32[]{:S(2)}, u32[]{:S(2)}) collective-permute-start(bf16[2,3,48,512]{3,2,1,0:T(8,128)(2,1)S(1)} %get-tuple-element.63), channel_id=1, source_target_pairs={{0,120},{1,121},{2,122},{3,123},{4,124},{5,125},{6,126},{7,127},{8... | collective-permute-start | bytes 884744 | tf_op jit(solution)/shard_map/ppermute | solution.py:776
  16.0 7.0 %collective-permute-start.5 = (bf16[2,3,6,512]{3,2,1,0:T(8,128)(2,1)S(1)}, bf16[2,3,6,512]{3,2,1,0:T(8,128)(2,1)S(1)}, u32[]{:S(2)}, u32[]{:S(2)}) collective-permute-start(bf16[2,3,6,512]{3,2,1,0:T(8,128)(2,1)S(1)} %get-tuple-element.64), channel_id=1, source_target_pairs={{0,127},{1,120},{2,121},{3,122},{4,123},{5,124},{6,125},{7,126},{8... | collective-permute-start | bytes 110600 | tf_op jit(solution)/shard_map/ppermute | solution.py:776
  23.1 0.6 copy-done.15
  23.7 0.1 copy-done.13
  23.8 12.9 %attention.1 = (bf16[1152,512]{1,0:T(8,128)(2,1)}, bf16[1152,512]{1,0:T(8,128)(2,1)}, bf16[512,1152]{1,0:T(8,128)(2,1)}, bf16[1152,1536]{1,0:T(8,128)(2,1)}, bf16[8,9,144,128]{3,2,1,0:T(8,128)(2,1)}) custom-call(bf16[2,12,48,512]{3,2,1,0:T(8,128)(2,1)} %tok.1, bf16[2,12,6,512]{3,2,1,0:T(8,128)(2,1)} %copy-done.15, bf16[2,3,48,512]{3,2,1,0:T(8,128)(2,1)} %copy-done.13, ...), custom_call_target="tpu_custom_call" | custom-call | flops 7247757312 | bytes 20000000 | tf_op jit(solution)/shard_map/attention/pallas_call | solution.py:620
  36.7 0.6 copy-done.17
  37.5 28.2 %mlp.1 = (bf16[1152,512]{1,0:T(8,128)(2,1)}, f32[1152,512]{1,0:T(8,128)}, bf16[16,576,128]{2,1,0:T(8,128)(2,1)}, bf16[16,576,128]{2,1,0:T(8,128)(2,1)}, f32[1,512]{1,0:T(1,128)}) custom-call(bf16[1152,512]{1,0:T(8,128)(2,1)} %get-tuple-element.58.xw, bf16[1152,512]{1,0:T(8,128)(2,1)} %get-tuple-element.61.mix, bf16[2,12,48,512]{3,2,1,0:T(8,128)(2,1)} %cot.1, ...), custom_call_target="tpu_custom_call" | custom-call | flops 19327352832 | bytes 40000000 | tf_op jit(solution)/shard_map/mlp/pallas_call | solution.py:641
  65.7 0.3 collective-permute-start.6
  66.0 1.3 copy-done.6
  67.3 3.7 %first_back.1 = (bf16[576,1536]{1,0:T(8,128)(2,1)S(1)}, f32[9,144,128]{2,1,0:T(8,128)S(1)}) custom-call(bf16[1152,1536]{1,0:T(8,128)(2,1)S(1)} %copy-done.4, bf16[8,9,144,128]{3,2,1,0:T(8,128)(2,1)S(1)} %copy-done.5, bf16[1152,512]{1,0:T(8,128)(2,1)S(1)} %copy-done.6), custom_call_target="tpu_custom_call" | custom-call | flops 5435817984 | bytes 10000000 | tf_op jit(solution)/shard_map/first_back/pallas_call | solution.py:672
  71.1 0.6 add_convert_fusion
  71.7 0.1 fusion.10
  71.9 0.3 collective-permute-start.8
  72.2 1.7 collective-permute-start.7
  74.0 8.2 %second_back.1 = (bf16[576,1536]{1,0:T(8,128)(2,1)S(1)}, bf16[16,240,128]{2,1,0:T(8,128)(2,1)S(1)}, bf16[16,240,128]{2,1,0:T(8,128)(2,1)S(1)}) custom-call(bf16[1152,1536]{1,0:T(8,128)(2,1)} %get-tuple-element.59.qkv, bf16[8,9,144,128]{3,2,1,0:T(8,128)(2,1)S(1)} %copy-done.5, bf16[1152,512]{1,0:T(8,128)(2,1)S(1)} %copy-done.6, ...), custom_call_target="tpu_custom_call" | custom-call | flops 7247757312 | bytes 10000000 | tf_op jit(solution)/shard_map/second_back/pallas_call | solution.py:688
  82.2 1.3 collective-permute-done.8
  83.5 6.2 %collective-permute-done.7 = bf16[4,576,128]{2,1,0:T(8,128)(2,1)S(1)} collective-permute-done((bf16[4,576,128]{2,1,0:T(8,128)(2,1)S(1)}, bf16[4,576,128]{2,1,0:T(8,128)(2,1)S(1)}, u32[]{:S(2)}, u32[]{:S(2)}) %collective-permute-start.7) | collective-permute-done | bytes 589856 | tf_op jit(solution)/shard_map/ppermute | solution.py:805
  89.7 0.3 add_convert_fusion.2
  90.1 2.6 %collective-permute-done.10 = bf16[16,240,128]{2,1,0:T(8,128)(2,1)S(1)} collective-permute-done((bf16[16,240,128]{2,1,0:T(8,128)(2,1)S(1)}, bf16[16,240,128]{2,1,0:T(8,128)(2,1)S(1)}, u32[]{:S(2)}, u32[]{:S(2)}) %collective-permute-start.10) | collective-permute-done | bytes 983072 | tf_op jit(solution)/shard_map/ppermute | solution.py:809
  92.7 0.3 add_convert_fusion.1
  93.0 1.1 collective-permute-start.13
  94.2 1.0 collective-permute-start.11
  95.2 4.1 %collective-permute-done.13 = bf16[4,240,128]{2,1,0:T(8,128)(2,1)S(1)} collective-permute-done((bf16[4,240,128]{2,1,0:T(8,128)(2,1)S(1)}, bf16[4,240,128]{2,1,0:T(8,128)(2,1)S(1)}, u32[]{:S(2)}, u32[]{:S(2)}) %collective-permute-start.13) | collective-permute-done | bytes 245792 | tf_op jit(solution)/shard_map/ppermute | solution.py:805
  99.3 2.7 %collective-permute-done.12 = bf16[4,240,128]{2,1,0:T(8,128)(2,1)S(1)} collective-permute-done((bf16[4,240,128]{2,1,0:T(8,128)(2,1)S(1)}, bf16[4,240,128]{2,1,0:T(8,128)(2,1)S(1)}, u32[]{:S(2)}, u32[]{:S(2)}) %collective-permute-start.12) | collective-permute-done | bytes 245792 | tf_op jit(solution)/shard_map/ppermute | solution.py:805
  102.0 2.5 %collective-permute-done.11 = bf16[4,240,128]{2,1,0:T(8,128)(2,1)S(1)} collective-permute-done((bf16[4,240,128]{2,1,0:T(8,128)(2,1)S(1)}, bf16[4,240,128]{2,1,0:T(8,128)(2,1)S(1)}, u32[]{:S(2)}, u32[]{:S(2)}) %collective-permute-start.11) | collective-permute-done | bytes 245792 | tf_op jit(solution)/shard_map/ppermute | solution.py:805
  104.5 0.1 add_convert_fusion.3
  104.8 2.3 %collective-permute-start.15 = (bf16[816,128]{1,0:T(8,128)(2,1)S(1)}, bf16[816,128]{1,0:T(8,128)(2,1)S(1)}, u32[]{:S(2)}, u32[]{:S(2)}) collective-permute-start(bf16[816,128]{1,0:T(8,128)(2,1)S(1)} %get-tuple-element.110), channel_id=1, source_target_pairs={{0,16},{1,17},{2,18},{3,19},{4,20},{5,21},{6,22},{7,23},{8,72},{9,... | collective-permute-start | bytes 626696 | tf_op jit(solution)/shard_map/ppermute | solution.py:805
  107.1 1.3 collective-permute-start.14
  108.4 2.2 %collective-permute-done.16 = bf16[816,128]{1,0:T(8,128)(2,1)S(1)} collective-permute-done((bf16[816,128]{1,0:T(8,128)(2,1)S(1)}, bf16[816,128]{1,0:T(8,128)(2,1)S(1)}, u32[]{:S(2)}, u32[]{:S(2)}) %collective-permute-start.16) | collective-permute-done | bytes 208928 | tf_op jit(solution)/shard_map/ppermute | solution.py:805
  110.6 1.6 collective-permute-done.15
  112.2 2.2 %collective-permute-done.14 = bf16[816,128]{1,0:T(8,128)(2,1)S(1)} collective-permute-done((bf16[816,128]{1,0:T(8,128)(2,1)S(1)}, bf16[816,128]{1,0:T(8,128)(2,1)S(1)}, u32[]{:S(2)}, u32[]{:S(2)}) %collective-permute-start.14) | collective-permute-done | bytes 208928 | tf_op jit(solution)/shard_map/ppermute | solution.py:805
  114.4 0.1 fusion.2
  114.5 1.5 collective-permute-start.20
  116.0 0.6 collective-permute-start.19
  116.6 3.6 %collective-permute-start.18 = (bf16[816,128]{1,0:T(8,128)(2,1)S(1)}, bf16[816,128]{1,0:T(8,128)(2,1)S(1)}, u32[]{:S(2)}, u32[]{:S(2)}) collective-permute-start(bf16[816,128]{1,0:T(8,128)(2,1)S(1)} %fusion.2), channel_id=1, source_target_pairs={{0,64},{1,65},{2,66},{3,67},{4,68},{5,69},{6,70},{7,71},{8,12},{9,... | collective-permute-start | bytes 626696 | tf_op jit(solution)/shard_map/ppermute | solution.py:805
  120.2 3.2 %branch.1 = (bf16[2,9,42,512]{3,2,1,0:T(8,128)(2,1)S(1)}, bf16[2,9,6,512]{3,2,1,0:T(8,128)(2,1)S(1)}, bf16[2,3,42,512]{3,2,1,0:T(8,128)(2,1)S(1)}, bf16[2,3,6,512]{3,2,1,0:T(8,128)(2,1)S(1)}) custom-call(bf16[1152,512]{1,0:T(8,128)(2,1)S(1)} %copy-done.9, bf16[576,1536]{1,0:T(8,128)(2,1)S(1)} %get-tuple-element.76.grads_before.grads_first, ...), custom_call_target="tpu_custom_call" | custom-call | flops 7247757312 | bytes 10000000 | tf_op jit(solution)/shard_map/branch/pallas_call | solution.py:706
  123.4 2.8 %collective-permute-done.18 = bf16[816,128]{1,0:T(8,128)(2,1)S(1)} collective-permute-done((bf16[816,128]{1,0:T(8,128)(2,1)S(1)}, bf16[816,128]{1,0:T(8,128)(2,1)S(1)}, u32[]{:S(2)}, u32[]{:S(2)}) %collective-permute-start.18) | collective-permute-done | bytes 208928 | tf_op jit(solution)/shard_map/ppermute | solution.py:805
  126.2 0.1 add_convert_fusion.4
  126.3 0.8 collective-permute-start.23
  127.2 2.4 %collective-permute-start.22 = (bf16[816,128]{1,0:T(8,128)(2,1)S(1)}, bf16[816,128]{1,0:T(8,128)(2,1)S(1)}, u32[]{:S(2)}, u32[]{:S(2)}) collective-permute-start(bf16[816,128]{1,0:T(8,128)(2,1)S(1)} %add_convert_fusion.4), channel_id=1, source_target_pairs={{0,16},{1,17},{2,18},{3,19},{4,20},{5,21},{6,22},{7,23},{8,72},{9,... | collective-permute-start | bytes 626696 | tf_op jit(solution)/shard_map/ppermute | solution.py:805
  129.6 0.7 collective-permute-start.21
  130.2 0.4 collective-permute-start.24
  130.7 1.5 collective-permute-done.23
  132.2 1.2 collective-permute-start.17
  133.4 2.0 %collective-permute-done.22 = bf16[816,128]{1,0:T(8,128)(2,1)S(1)} collective-permute-done((bf16[816,128]{1,0:T(8,128)(2,1)S(1)}, bf16[816,128]{1,0:T(8,128)(2,1)S(1)}, u32[]{:S(2)}, u32[]{:S(2)}) %collective-permute-start.22) | collective-permute-done | bytes 208928 | tf_op jit(solution)/shard_map/ppermute | solution.py:805
  135.5 4.9 %collective-permute-done.21 = bf16[816,128]{1,0:T(8,128)(2,1)S(1)} collective-permute-done((bf16[816,128]{1,0:T(8,128)(2,1)S(1)}, bf16[816,128]{1,0:T(8,128)(2,1)S(1)}, u32[]{:S(2)}, u32[]{:S(2)}) %collective-permute-start.21) | collective-permute-done | bytes 208928 | tf_op jit(solution)/shard_map/ppermute | solution.py:805
  140.4 0.1 pad_maximum_fusion.refs_0_
  140.5 1.9 %collective-permute-done.17 = bf16[2,3,6,512]{3,2,1,0:T(8,128)(2,1)S(1)} collective-permute-done((bf16[2,3,6,512]{3,2,1,0:T(8,128)(2,1)S(1)}, bf16[2,3,6,512]{3,2,1,0:T(8,128)(2,1)S(1)}, u32[]{:S(2)}, u32[]{:S(2)}) %collective-permute-start.17) | collective-permute-done | bytes 36896 | tf_op jit(solution)/shard_map/ppermute | solution.py:776
  142.4 0.2 collective-permute-done.25
  142.6 1.5 collective-permute-start.27
  144.1 2.1 %collective-permute-start.28 = (bf16[4,816,128]{2,1,0:T(8,128)(2,1)S(1)}, bf16[4,816,128]{2,1,0:T(8,128)(2,1)S(1)}, u32[]{:S(2)}, u32[]{:S(2)}) collective-permute-start(bf16[4,816,128]{2,1,0:T(8,128)(2,1)S(1)} %pad_maximum_fusion.refs_0_), channel_id=1, source_target_pairs={{0,6},{1,7},{2,0},{3,1},{4,2},{5,3},{6,4},{7,5},{8,25},{9,8},{10,2... | collective-permute-start | bytes 2506760 | tf_op jit(solution)/shard_map/ppermute | solution.py:805
  146.2 0.3 collective-permute-start.29
  146.4 18.9 %collective-permute-done.26.refs_1_ = bf16[4,816,128]{2,1,0:T(8,128)(2,1)S(1)} collective-permute-done((bf16[4,816,128]{2,1,0:T(8,128)(2,1)S(1)}, bf16[4,816,128]{2,1,0:T(8,128)(2,1)S(1)}, u32[]{:S(2)}, u32[]{:S(2)}) %collective-permute-start.26) | collective-permute-done | bytes 835616 | tf_op jit(solution)/shard_map/ppermute | solution.py:805
  165.3 0.5 collective-permute-start.31
  165.8 0.4 collective-permute-done.28.refs_3_
  166.2 3.5 %finish_own.1 = (f32[512,2048]{1,0:T(8,128)}, f32[2048,512]{1,0:T(8,128)}, f32[512,1536]{1,0:T(8,128)}, f32[512,512]{1,0:T(8,128)}, f32[512,128]{1,0:T(8,128)S(1)}, /*index=5*/bf16[32,48,128]{2,1,0:T(8,128)(2,1)S(1)}) custom-call(bf16[4,816,128]{2,1,0:T(8,128)(2,1)S(1)} %pad_maximum_fusion.refs_0_, bf16[4,816,128]{2,1,0:T(8,128)(2,1)S(1)} %collective-permute-done.26.refs_1_, ...), custom_call_target="tpu_custom_call" | custom-call | flops 10000000 | bytes 10000000 | tf_op jit(solution)/shard_map/finish_own/pallas_call | solution.py:739
  169.7 1.6 maximum_maximum_fusion
  171.4 4.9 %finish.1 = (f32[512,2048]{1,0:T(8,128)}, f32[2048,512]{1,0:T(8,128)}, f32[512,1536]{1,0:T(8,128)}, f32[512,512]{1,0:T(8,128)}, f32[8,144,144]{2,1,0:T(8,128)}, /*index=5*/f32[1,512]{1,0:T(1,128)}, f32[1,512]{1,0:T(1,128)}) custom-call(bf16[4,816,128]{2,1,0:T(8,128)(2,1)S(1)} %collective-per, ...), custom_call_target="tpu_custom_call", output_to_operand_aliasing={{0}: (8, {}), {1}: (9, {}), {2}: (10, {}), {3}: (11, {})} | custom-call | flops 10000000 | bytes 10000000 | tf_op jit(solution)/shard_map/finish/pallas_call | solution.py:752
  (58 shorter events, 0.7 us)
Async XLA Ops:
  0.6 1.3 copy-start.1
  1.9 21.1 %collective-permute-start.1 = (bf16[2,3,48,512]{3,2,1,0:T(8,128)(2,1)S(1)}, bf16[2,3,48,512]{3,2,1,0:T(8,128)(2,1)S(1)}, u32[]{:S(2)}, u32[]{:S(2)}) collective-permute-start(bf16[2,3,48,512]{3,2,1,0:T(8,128)(2,1)S(1)} %get-tuple-element.56), channel_id=1, source_target_pairs={{0,120},{1,121},{2,122},{3,123},{4,124},{5,125},{6,126},{7,127},{8... | collective-permute-start | bytes 884744 | tf_op jit(solution)/shard_map/ppermute | solution.py:776
  8.2 14.8 %collective-permute-start = (bf16[2,12,6,512]{3,2,1,0:T(8,128)(2,1)S(1)}, bf16[2,12,6,512]{3,2,1,0:T(8,128)(2,1)S(1)}, u32[]{:S(2)}, u32[]{:S(2)}) collective-permute-start(bf16[2,12,6,512]{3,2,1,0:T(8,128)(2,1)S(1)} %get-tuple-element.55), channel_id=1, source_target_pairs={{0,7},{1,0},{2,1},{3,2},{4,3},{5,4},{6,5},{7,6},{8,15},{9,8},{10,9... | collective-permute-start | bytes 442376 | tf_op jit(solution)/shard_map/ppermute | solution.py:776
  11.1 5.0 %collective-permute-start.2 = (bf16[2,3,6,512]{3,2,1,0:T(8,128)(2,1)S(1)}, bf16[2,3,6,512]{3,2,1,0:T(8,128)(2,1)S(1)}, u32[]{:S(2)}, u32[]{:S(2)}) collective-permute-start(bf16[2,3,6,512]{3,2,1,0:T(8,128)(2,1)S(1)} %get-tuple-element.57), channel_id=1, source_target_pairs={{0,127},{1,120},{2,121},{3,122},{4,123},{5,124},{6,125},{7,126},{8... | collective-permute-start | bytes 110600 | tf_op jit(solution)/shard_map/ppermute | solution.py:776
  11.4 1.3 copy-start.2
  12.7 24.0 %collective-permute-start.3 = (bf16[2,12,6,512]{3,2,1,0:T(8,128)(2,1)S(1)}, bf16[2,12,6,512]{3,2,1,0:T(8,128)(2,1)S(1)}, u32[]{:S(2)}, u32[]{:S(2)}) collective-permute-start(bf16[2,12,6,512]{3,2,1,0:T(8,128)(2,1)S(1)} %get-tuple-element.62), channel_id=1, source_target_pairs={{0,7},{1,0},{2,1},{3,2},{4,3},{5,4},{6,5},{7,6},{8,15},{9,8},{10,9... | collective-permute-start | bytes 442376 | tf_op jit(solution)/shard_map/ppermute | solution.py:776
  13.8 22.9 %collective-permute-start.4 = (bf16[2,3,48,512]{3,2,1,0:T(8,128)(2,1)S(1)}, bf16[2,3,48,512]{3,2,1,0:T(8,128)(2,1)S(1)}, u32[]{:S(2)}, u32[]{:S(2)}) collective-permute-start(bf16[2,3,48,512]{3,2,1,0:T(8,128)(2,1)S(1)} %get-tuple-element.63), channel_id=1, source_target_pairs={{0,120},{1,121},{2,122},{3,123},{4,124},{5,125},{6,126},{7,127},{8... | collective-permute-start | bytes 884744 | tf_op jit(solution)/shard_map/ppermute | solution.py:776
  16.0 7.0 %copy-start.16 = (bf16[2,3,6,512]{3,2,1,0:T(8,128)(2,1)}, bf16[2,3,6,512]{3,2,1,0:T(8,128)(2,1)S(1)}, u32[]{:S(2)}) copy-start(bf16[2,3,6,512]{3,2,1,0:T(8,128)(2,1)S(1)} %collective-permute-done.2.tok_both) | copy-start | bytes 110596
  16.0 20.6 %collective-permute-start.5 = (bf16[2,3,6,512]{3,2,1,0:T(8,128)(2,1)S(1)}, bf16[2,3,6,512]{3,2,1,0:T(8,128)(2,1)S(1)}, u32[]{:S(2)}, u32[]{:S(2)}) collective-permute-start(bf16[2,3,6,512]{3,2,1,0:T(8,128)(2,1)S(1)} %get-tuple-element.64), channel_id=1, source_target_pairs={{0,127},{1,120},{2,121},{3,122},{4,123},{5,124},{6,125},{7,126},{8... | collective-permute-start | bytes 110600 | tf_op jit(solution)/shard_map/ppermute | solution.py:776
  23.0 0.7 copy-start.15
  23.0 0.8 copy-start.13
  36.7 0.6 copy-start.17
  36.7 0.7 copy-start.14
  36.7 0.8 copy-start.12
  37.5 28.5 %copy-start.4 = (bf16[1152,1536]{1,0:T(8,128)(2,1)S(1)}, bf16[1152,1536]{1,0:T(8,128)(2,1)}, u32[]{:S(2)}) copy-start(bf16[1152,1536]{1,0:T(8,128)(2,1)} %get-tuple-element.59.qkv) | copy-start | bytes 10616836
  37.5 28.5 %copy-start.5 = (bf16[8,9,144,128]{3,2,1,0:T(8,128)(2,1)S(1)}, bf16[8,9,144,128]{3,2,1,0:T(8,128)(2,1)}, u32[]{:S(2)}) copy-start(bf16[8,9,144,128]{3,2,1,0:T(8,128)(2,1)} %get-tuple-element.60.probs) | copy-start | bytes 7962628
  65.7 5.4 %collective-permute-start.6 = (bf16[16,576,128]{2,1,0:T(8,128)(2,1)}, bf16[16,576,128]{2,1,0:T(8,128)(2,1)S(1)}, u32[]{:S(2)}, u32[]{:S(2)}) collective-permute-start(bf16[16,576,128]{2,1,0:T(8,128)(2,1)} %get-tuple-element.68), channel_id=1, source_target_pairs={{0,8},{8,0},{16,24},{24,16},{32,40},{40,32},{48,56},{56,48},{64,72... | collective-permute-start | bytes 7077896 | tf_op jit(solution)/shard_map/ppermute | solution.py:809
  66.0 1.3 copy-start.6
  67.3 3.8 %copy-start.11 = (bf16[16,576,128]{2,1,0:T(8,128)(2,1)S(1)}, bf16[16,576,128]{2,1,0:T(8,128)(2,1)}, u32[]{:S(2)}) copy-start(bf16[16,576,128]{2,1,0:T(8,128)(2,1)} %get-tuple-element.67) | copy-start | bytes 7077892
  71.7 2.3 %copy-start.8 = (bf16[512,1152]{1,0:T(8,128)(2,1)S(1)}, bf16[512,1152]{1,0:T(8,128)(2,1)}, u32[]{:S(2)}) copy-start(bf16[512,1152]{1,0:T(8,128)(2,1)} %get-tuple-element.69.act_t) | copy-start | bytes 3538948
  71.7 2.2 %copy-start.10 = (f32[1,512]{1,0:T(1,128)S(1)}, f32[1,512]{1,0:T(1,128)}, u32[]{:S(2)}) copy-start(f32[1,512]{1,0:T(1,128)} %get-tuple-element.70.sum_gain_two) | copy-start | bytes 6148
  71.9 10.3 %collective-permute-start.9 = (bf16[4,576,128]{2,1,0:T(8,128)(2,1)S(1)}, bf16[4,576,128]{2,1,0:T(8,128)(2,1)S(1)}, u32[]{:S(2)}, u32[]{:S(2)}) collective-permute-start(bf16[4,576,128]{2,1,0:T(8,128)(2,1)S(1)} %get-tuple-element.103), channel_id=1, source_target_pairs={{0,6},{1,7},{2,0},{3,1},{4,2},{5,3},{6,4},{7,5},{8,25},{9,8},{10,2... | collective-permute-start | bytes 1769480 | tf_op jit(solution)/shard_map/ppermute | solution.py:805
  71.9 11.6 %collective-permute-start.8 = (bf16[4,576,128]{2,1,0:T(8,128)(2,1)S(1)}, bf16[4,576,128]{2,1,0:T(8,128)(2,1)S(1)}, u32[]{:S(2)}, u32[]{:S(2)}) collective-permute-start(bf16[4,576,128]{2,1,0:T(8,128)(2,1)S(1)} %get-tuple-element.104), channel_id=1, source_target_pairs={{0,4},{1,5},{2,6},{3,7},{4,0},{5,1},{6,2},{7,3},{8,24},{9,25},{10,... | collective-permute-start | bytes 1769480 | tf_op jit(solution)/shard_map/ppermute | solution.py:805
  72.2 17.5 %collective-permute-start.7 = (bf16[4,576,128]{2,1,0:T(8,128)(2,1)S(1)}, bf16[4,576,128]{2,1,0:T(8,128)(2,1)S(1)}, u32[]{:S(2)}, u32[]{:S(2)}) collective-permute-start(bf16[4,576,128]{2,1,0:T(8,128)(2,1)S(1)} %get-tuple-element.102), channel_id=1, source_target_pairs={{0,2},{1,3},{2,4},{3,5},{4,6},{5,7},{6,0},{7,1},{8,9},{9,24},{10,1... | collective-permute-start | bytes 1769480 | tf_op jit(solution)/shard_map/ppermute | solution.py:805
  90.0 2.6 %collective-permute-start.10 = (bf16[16,240,128]{2,1,0:T(8,128)(2,1)S(1)}, bf16[16,240,128]{2,1,0:T(8,128)(2,1)S(1)}, u32[]{:S(2)}, u32[]{:S(2)}) collective-permute-start(bf16[16,240,128]{2,1,0:T(8,128)(2,1)S(1)} %get-tuple-element.75), channel_id=1, source_target_pairs={{0,8},{8,0},{16,24},{24,16},{32,40},{40,32},{48,56},{56,48},{64,72... | collective-permute-start | bytes 2949128 | tf_op jit(solution)/shard_map/ppermute | solution.py:809
  92.9 27.2 %copy-start.9 = (bf16[1152,512]{1,0:T(8,128)(2,1)S(1)}, bf16[1152,512]{1,0:T(8,128)(2,1)}, u32[]{:S(2)}) copy-start(bf16[1152,512]{1,0:T(8,128)(2,1)} %get-tuple-element.58.xw) | copy-start | bytes 3538948
  93.0 6.3 %collective-permute-start.13 = (bf16[4,240,128]{2,1,0:T(8,128)(2,1)S(1)}, bf16[4,240,128]{2,1,0:T(8,128)(2,1)S(1)}, u32[]{:S(2)}, u32[]{:S(2)}) collective-permute-start(bf16[4,240,128]{2,1,0:T(8,128)(2,1)S(1)} %get-tuple-element.106), channel_id=1, source_target_pairs={{0,6},{1,7},{2,0},{3,1},{4,2},{5,3},{6,4},{7,5},{8,25},{9,8},{10,2... | collective-permute-start | bytes 737288 | tf_op jit(solution)/shard_map/ppermute | solution.py:805
  94.2 7.8 %collective-permute-start.12 = (bf16[4,240,128]{2,1,0:T(8,128)(2,1)S(1)}, bf16[4,240,128]{2,1,0:T(8,128)(2,1)S(1)}, u32[]{:S(2)}, u32[]{:S(2)}) collective-permute-start(bf16[4,240,128]{2,1,0:T(8,128)(2,1)S(1)} %get-tuple-element.107), channel_id=1, source_target_pairs={{0,4},{1,5},{2,6},{3,7},{4,0},{5,1},{6,2},{7,3},{8,24},{9,25},{10,... | collective-permute-start | bytes 737288 | tf_op jit(solution)/shard_map/ppermute | solution.py:805
  94.2 26.0 %copy-start = (bf16[512,1536]{1,0:T(8,128)(2,1)S(1)}, bf16[512,1536]{1,0:T(8,128)(2,1)}, u32[]{:S(2)}) copy-start(bf16[512,1536]{1,0:T(8,128)(2,1)} %refs_4_.3) | copy-start | bytes 4718596
  94.2 26.0 %copy-start.3 = (f32[512]{0:T(512)S(1)}, f32[512]{0:T(512)}, u32[]{:S(2)}) copy-start(f32[512]{0:T(512)} %param.16) | copy-start | bytes 6148
  94.2 26.0 %copy-start.7 = (f32[1152,512]{1,0:T(8,128)S(1)}, f32[1152,512]{1,0:T(8,128)}, u32[]{:S(2)}) copy-start(f32[1152,512]{1,0:T(8,128)} %get-tuple-element.78.grad_res) | copy-start | bytes 7077892
  94.2 10.3 %collective-permute-start.11 = (bf16[4,240,128]{2,1,0:T(8,128)(2,1)S(1)}, bf16[4,240,128]{2,1,0:T(8,128)(2,1)S(1)}, u32[]{:S(2)}, u32[]{:S(2)}) collective-permute-start(bf16[4,240,128]{2,1,0:T(8,128)(2,1)S(1)} %get-tuple-element.105), channel_id=1, source_target_pairs={{0,2},{1,3},{2,4},{3,5},{4,6},{5,7},{6,0},{7,1},{8,9},{9,24},{10,1... | collective-permute-start | bytes 737288 | tf_op jit(solution)/shard_map/ppermute | solution.py:805
  104.7 5.9 %collective-permute-start.16 = (bf16[816,128]{1,0:T(8,128)(2,1)S(1)}, bf16[816,128]{1,0:T(8,128)(2,1)S(1)}, u32[]{:S(2)}, u32[]{:S(2)}) collective-permute-start(bf16[816,128]{1,0:T(8,128)(2,1)S(1)} %get-tuple-element.109), channel_id=1, source_target_pairs={{0,17},{1,0},{2,19},{3,2},{4,21},{5,4},{6,23},{7,6},{8,104},{9,105... | collective-permute-start | bytes 626696 | tf_op jit(solution)/shard_map/ppermute | solution.py:805
  104.8 7.4 %collective-permute-start.15 = (bf16[816,128]{1,0:T(8,128)(2,1)S(1)}, bf16[816,128]{1,0:T(8,128)(2,1)S(1)}, u32[]{:S(2)}, u32[]{:S(2)}) collective-permute-start(bf16[816,128]{1,0:T(8,128)(2,1)S(1)} %get-tuple-element.110), channel_id=1, source_target_pairs={{0,16},{1,17},{2,18},{3,19},{4,20},{5,21},{6,22},{7,23},{8,72},{9,... | collective-permute-start | bytes 626696 | tf_op jit(solution)/shard_map/ppermute | solution.py:805
  107.1 7.3 %collective-permute-start.14 = (bf16[816,128]{1,0:T(8,128)(2,1)S(1)}, bf16[816,128]{1,0:T(8,128)(2,1)S(1)}, u32[]{:S(2)}, u32[]{:S(2)}) collective-permute-start(bf16[816,128]{1,0:T(8,128)(2,1)S(1)} %get-tuple-element.108), channel_id=1, source_target_pairs={{0,1},{1,16},{2,3},{3,18},{4,5},{5,20},{6,7},{7,22},{8,40},{9,41},... | collective-permute-start | bytes 626696 | tf_op jit(solution)/shard_map/ppermute | solution.py:805
  114.5 8.9 %collective-permute-start.20 = (bf16[816,128]{1,0:T(8,128)(2,1)S(1)}, bf16[816,128]{1,0:T(8,128)(2,1)S(1)}, u32[]{:S(2)}, u32[]{:S(2)}) collective-permute-start(bf16[816,128]{1,0:T(8,128)(2,1)S(1)} %fusion.2), channel_id=1, source_target_pairs={{0,96},{1,97},{2,98},{3,99},{4,100},{5,101},{6,102},{7,103},{8,14}... | collective-permute-start | bytes 626696 | tf_op jit(solution)/shard_map/ppermute | solution.py:805
  116.0 7.4 %collective-permute-start.19 = (bf16[816,128]{1,0:T(8,128)(2,1)S(1)}, bf16[816,128]{1,0:T(8,128)(2,1)S(1)}, u32[]{:S(2)}, u32[]{:S(2)}) collective-permute-start(bf16[816,128]{1,0:T(8,128)(2,1)S(1)} %fusion.2), channel_id=1, source_target_pairs={{0,32},{1,33},{2,34},{3,35},{4,36},{5,37},{6,38},{7,39},{8,10},{9,... | collective-permute-start | bytes 626696 | tf_op jit(solution)/shard_map/ppermute | solution.py:805
  116.6 9.6 %collective-permute-start.18 = (bf16[816,128]{1,0:T(8,128)(2,1)S(1)}, bf16[816,128]{1,0:T(8,128)(2,1)S(1)}, u32[]{:S(2)}, u32[]{:S(2)}) collective-permute-start(bf16[816,128]{1,0:T(8,128)(2,1)S(1)} %fusion.2), channel_id=1, source_target_pairs={{0,64},{1,65},{2,66},{3,67},{4,68},{5,69},{6,70},{7,71},{8,12},{9,... | collective-permute-start | bytes 626696 | tf_op jit(solution)/shard_map/ppermute | solution.py:805
  126.3 5.9 %collective-permute-start.23 = (bf16[816,128]{1,0:T(8,128)(2,1)S(1)}, bf16[816,128]{1,0:T(8,128)(2,1)S(1)}, u32[]{:S(2)}, u32[]{:S(2)}) collective-permute-start(bf16[816,128]{1,0:T(8,128)(2,1)S(1)} %add_convert_fusion.4), channel_id=1, source_target_pairs={{0,17},{1,0},{2,19},{3,2},{4,21},{5,4},{6,23},{7,6},{8,104},{9,105... | collective-permute-start | bytes 626696 | tf_op jit(solution)/shard_map/ppermute | solution.py:805
  127.2 8.3 %collective-permute-start.22 = (bf16[816,128]{1,0:T(8,128)(2,1)S(1)}, bf16[816,128]{1,0:T(8,128)(2,1)S(1)}, u32[]{:S(2)}, u32[]{:S(2)}) collective-permute-start(bf16[816,128]{1,0:T(8,128)(2,1)S(1)} %add_convert_fusion.4), channel_id=1, source_target_pairs={{0,16},{1,17},{2,18},{3,19},{4,20},{5,21},{6,22},{7,23},{8,72},{9,... | collective-permute-start | bytes 626696 | tf_op jit(solution)/shard_map/ppermute | solution.py:805
  129.6 10.8 %collective-permute-start.21 = (bf16[816,128]{1,0:T(8,128)(2,1)S(1)}, bf16[816,128]{1,0:T(8,128)(2,1)S(1)}, u32[]{:S(2)}, u32[]{:S(2)}) collective-permute-start(bf16[816,128]{1,0:T(8,128)(2,1)S(1)} %add_convert_fusion.4), channel_id=1, source_target_pairs={{0,1},{1,16},{2,3},{3,18},{4,5},{5,20},{6,7},{7,22},{8,40},{9,41},... | collective-permute-start | bytes 626696 | tf_op jit(solution)/shard_map/ppermute | solution.py:805
  130.2 12.4 %collective-permute-start.25 = (bf16[2,3,42,512]{3,2,1,0:T(8,128)(2,1)S(1)}, bf16[2,3,42,512]{3,2,1,0:T(8,128)(2,1)S(1)}, u32[]{:S(2)}, u32[]{:S(2)}) collective-permute-start(bf16[2,3,42,512]{3,2,1,0:T(8,128)(2,1)S(1)} %get-tuple-element.82), channel_id=1, source_target_pairs={{0,8},{1,9},{2,10},{3,11},{4,12},{5,13},{6,14},{7,15},{8,16},{9,17... | collective-permute-start | bytes 774152 | tf_op jit(solution)/shard_map/ppermute | solution.py:776
  130.2 12.2 %collective-permute-start.24 = (bf16[2,9,6,512]{3,2,1,0:T(8,128)(2,1)S(1)}, bf16[2,9,6,512]{3,2,1,0:T(8,128)(2,1)S(1)}, u32[]{:S(2)}, u32[]{:S(2)}) collective-permute-start(bf16[2,9,6,512]{3,2,1,0:T(8,128)(2,1)S(1)} %get-tuple-element.81), channel_id=1, source_target_pairs={{0,1},{1,2},{2,3},{3,4},{4,5},{5,6},{6,7},{7,0},{8,9},{9,10},{10,1... | collective-permute-start | bytes 331784 | tf_op jit(solution)/shard_map/ppermute | solution.py:776
  132.2 10.2 %collective-permute-start.17 = (bf16[2,3,6,512]{3,2,1,0:T(8,128)(2,1)S(1)}, bf16[2,3,6,512]{3,2,1,0:T(8,128)(2,1)S(1)}, u32[]{:S(2)}, u32[]{:S(2)}) collective-permute-start(bf16[2,3,6,512]{3,2,1,0:T(8,128)(2,1)S(1)} %get-tuple-element.79), channel_id=1, source_target_pairs={{0,9},{1,10},{2,11},{3,12},{4,13},{5,14},{6,15},{7,8},{8,17},{9,18... | collective-permute-start | bytes 110600 | tf_op jit(solution)/shard_map/ppermute | solution.py:776
  142.6 22.7 %collective-permute-start.26 = (bf16[4,816,128]{2,1,0:T(8,128)(2,1)S(1)}, bf16[4,816,128]{2,1,0:T(8,128)(2,1)S(1)}, u32[]{:S(2)}, u32[]{:S(2)}) collective-permute-start(bf16[4,816,128]{2,1,0:T(8,128)(2,1)S(1)} %pad_maximum_fusion.refs_0_), channel_id=1, source_target_pairs={{0,2},{1,3},{2,4},{3,5},{4,6},{5,7},{6,0},{7,1},{8,9},{9,24},{10,1... | collective-permute-start | bytes 2506760 | tf_op jit(solution)/shard_map/ppermute | solution.py:805
  142.6 22.7 %collective-permute-start.27 = (bf16[4,816,128]{2,1,0:T(8,128)(2,1)S(1)}, bf16[4,816,128]{2,1,0:T(8,128)(2,1)S(1)}, u32[]{:S(2)}, u32[]{:S(2)}) collective-permute-start(bf16[4,816,128]{2,1,0:T(8,128)(2,1)S(1)} %pad_maximum_fusion.refs_0_), channel_id=1, source_target_pairs={{0,4},{1,5},{2,6},{3,7},{4,0},{5,1},{6,2},{7,3},{8,24},{9,25},{10,... | collective-permute-start | bytes 2506760 | tf_op jit(solution)/shard_map/ppermute | solution.py:805
  144.1 22.1 %collective-permute-start.28 = (bf16[4,816,128]{2,1,0:T(8,128)(2,1)S(1)}, bf16[4,816,128]{2,1,0:T(8,128)(2,1)S(1)}, u32[]{:S(2)}, u32[]{:S(2)}) collective-permute-start(bf16[4,816,128]{2,1,0:T(8,128)(2,1)S(1)} %pad_maximum_fusion.refs_0_), channel_id=1, source_target_pairs={{0,6},{1,7},{2,0},{3,1},{4,2},{5,3},{6,4},{7,5},{8,25},{9,8},{10,2... | collective-permute-start | bytes 2506760 | tf_op jit(solution)/shard_map/ppermute | solution.py:805
  146.2 25.2 %collective-permute-start.29 = (bf16[4,816,128]{2,1,0:T(8,128)(2,1)S(1)}, bf16[4,816,128]{2,1,0:T(8,128)(2,1)S(1)}, u32[]{:S(2)}, u32[]{:S(2)}) collective-permute-start(bf16[4,816,128]{2,1,0:T(8,128)(2,1)S(1)} %pad_maximum_fusion.refs_0_), channel_id=1, source_target_pairs={{0,8},{8,0},{16,24},{24,16},{32,40},{40,32},{48,56},{56,48},{64,72... | collective-permute-start | bytes 2506760 | tf_op jit(solution)/shard_map/ppermute | solution.py:809
  165.3 6.0 %collective-permute-start.30 = (bf16[4,816,128]{2,1,0:T(8,128)(2,1)S(1)}, bf16[4,816,128]{2,1,0:T(8,128)(2,1)S(1)}, u32[]{:S(2)}, u32[]{:S(2)}) collective-permute-start(bf16[4,816,128]{2,1,0:T(8,128)(2,1)S(1)} %collective-permute-done.26.refs_1_), channel_id=1, source_target_pairs={{0,8},{8,0},{16,24},{24,16},{32,40},{40,32},{48,56},{56,48},{64,72... | collective-permute-start | bytes 2506760 | tf_op jit(solution)/shard_map/ppermute | solution.py:809
  165.3 6.0 %collective-permute-start.31 = (bf16[4,816,128]{2,1,0:T(8,128)(2,1)S(1)}, bf16[4,816,128]{2,1,0:T(8,128)(2,1)S(1)}, u32[]{:S(2)}, u32[]{:S(2)}) collective-permute-start(bf16[4,816,128]{2,1,0:T(8,128)(2,1)S(1)} %collective-permute-done.27.refs_2_), channel_id=1, source_target_pairs={{0,8},{8,0},{16,24},{24,16},{32,40},{40,32},{48,56},{56,48},{64,72... | collective-permute-start | bytes 2506760 | tf_op jit(solution)/shard_map/ppermute | solution.py:809
  166.2 5.2 %collective-permute-start.32 = (bf16[4,816,128]{2,1,0:T(8,128)(2,1)S(1)}, bf16[4,816,128]{2,1,0:T(8,128)(2,1)S(1)}, u32[]{:S(2)}, u32[]{:S(2)}) collective-permute-start(bf16[4,816,128]{2,1,0:T(8,128)(2,1)S(1)} %collective-permute-done.28.refs_3_), channel_id=1, source_target_pairs={{0,8},{8,0},{16,24},{24,16},{32,40},{40,32},{48,56},{56,48},{64,72... | collective-permute-start | bytes 2506760 | tf_op jit(solution)/shard_map/ppermute | solution.py:809

commit v2 on v1

--- a/solution.py
+++ b/solution.py
@@ -149,14 +149,24 @@
     return jnp.sum((block * tail).reshape(HEADS, 16, D), 0)
 
 
-def pack_kernel(ref, lon, lat, both):
+def pack_kernel(tok, cot, *refs):
     edge, top = WLON // 2, WLAT // 2
-    lat[...] = ref[:, :top]
-    for level in range(LEVELS):
-        for row in range(HEIGHT):
-            lon[level, row] = ref[level, row, :edge]
-        for row in range(top):
-            both[level, row] = ref[level, row, :edge]
+    outs, (sides, tops, got) = (refs[0:3], refs[3:6]), refs[6:]
+    loads = []
+    for i, ref in enumerate((tok, cot)):
+        loads.append(pltpu.make_async_copy(ref.at[:, :, pl.ds(0, 16)], sides.at[i], got.at[i, 0]))
+        loads.append(pltpu.make_async_copy(ref.at[:, pl.ds(0, top)], tops.at[i], got.at[i, 1]))
+    for load in loads:
+        load.start()
+    for load in loads:
+        load.wait()
+    for i, (lon, lat, both) in enumerate(outs):
+        lat[...] = tops[i]
+        for level in range(LEVELS):
+            for row in range(HEIGHT):
+                lon[level, row] = sides[i, level, row, :edge]
+            for row in range(top):
+                both[level, row] = sides[i, level, row, :edge]
 
 
 def attention_kernel(
@@ -601,19 +611,23 @@
 SCALARS = pl.BlockSpec(memory_space=pltpu.SMEM)
 
 
-def pack(grid):
+def pack(tokens, cotangent):
     edge, top = WLON // 2, WLAT // 2
     return pl.pallas_call(
         pack_kernel,
         out_shape=(
             shape(LEVELS, HEIGHT, edge, D), shape(LEVELS, top, BREADTH, D),
             shape(LEVELS, top, edge, D),
-        ),
-        in_specs=[INSIDE],
-        out_specs=[INSIDE] * 3,
-        compiler_params=params(16),
+        ) * 2,
+        in_specs=[ANY] * 2,
+        out_specs=[INSIDE] * 6,
+        scratch_shapes=[
+            vmem(2, LEVELS, HEIGHT, 16, D), vmem(2, LEVELS, top, BREADTH, D),
+            pltpu.SemaphoreType.DMA((2, 2)),
+        ],
+        compiler_params=params(60),
         name="pack",
-    )(grid)
+    )(tokens, cotangent)
 
 
 def attention(*operands):
@@ -776,8 +790,7 @@
     return lax.ppermute(array, ("lat", "lon"), pairs)
 
 
-def halos(grid):
-    lon, lat, both = pack(grid)
+def halos(lon, lat, both):
     return neighbour(lat, -1, 0), neighbour(lon, 0, -1), neighbour(both, -1, -1)
 
 
@@ -850,8 +863,9 @@
     scale = total_tokens ** (-0.5)
     gain_one = gain_one.reshape(1, D)
     gain_two = gain_two.reshape(1, D)
-    lat_edge, lon_edge, corner = halos(tokens)
-    cot_lat, cot_lon, cot_corner = halos(cotangent)
+    edges = pack(tokens, cotangent)
+    lat_edge, lon_edge, corner = halos(*edges[:3])
+    cot_lat, cot_lon, cot_corner = halos(*edges[3:])
     xw, mix, act_t, qkv, probs = attention(
         tokens, lon_edge, lat_edge, corner, w_qkv, pair_bias, gain_one
     )

time: 178 us -> 179 us (level)
  waiting for transfers between devices: 58.1 us -> 61.5 us
  local copies, waits for them, and re-layouts: 5.52 us -> 2.98 us
  Pallas kernels: 64.7 us -> 67 us
  starting transfers between devices: 43.7 us -> 41.8 us
    unnamed x36 -> x32, local copies, waits for them, and re-layouts: 5.35 us -> 2.81 us
    ppermute x9, waiting for transfers between devices: 2.14 us -> 4.56 us  [neighbour(): return lax.ppermute(array, ('lat', 'lon'), pairs)]
    pallas_call x2 -> x1, Pallas kernels: 0.08 us -> 2.36 us  [pack(): pl.pallas_call(pack_kernel, out_shape=(shape(LEVELS, HEIGHT, edge, D), sh...]
    ppermute x18, starting transfers between devices: 21.1 us -> 19.1 us  [along(): return lax.ppermute(array, ('lat', 'lon'), pairs)]
  transfers between devices with their start and end apart: 33 -> 33, of which waited for: 17 -> 19; matrix products, arithmetic and copies ran while one was open for 1% -> 1% of each run, Pallas kernels for 18% -> 18%
where the time goes in v2:
time: 179 us; the launch traced here: 178 us
  Pallas kernels  67 us (37%)
  waiting for transfers between devices  61.5 us (34%)
  starting transfers between devices  41.8 us (23%)
  other arithmetic  3.33 us (2%)
  local copies, waits for them, and re-layouts  2.98 us (2%)
    ppermute x18, waiting for transfers between devices, along(): return lax.ppermute(array, ('lat', 'lon'), pairs)  54.4 us
    pallas_call x1, Pallas kernels, mlp_call(): pl.pallas_call(mlp_kernel, out_shape=(shape(ROWS, D), shape(ROWS, D, dtyp...  28.2 us
    ppermute x9, starting transfers between devices, neighbour(): return lax.ppermute(array, ('lat', 'lon'), pairs)  21.6 us
    ppermute x18, starting transfers between devices, along(): return lax.ppermute(array, ('lat', 'lon'), pairs)  19.1 us
    pallas_call x1, Pallas kernels, attention(): pl.pallas_call(attention_kernel, out_shape=(shape(ROWS, D), shape(ROWS, D...  12.9 us
    pallas_call x1, Pallas kernels, second_back(): pl.pallas_call(second_back_kernel, out_shape=(shape(ROWS // 2, QKV), shap...  8.22 us
    pallas_call x1, Pallas kernels, finish(): pl.pallas_call(functools.partial(finish_kernel, scale), out_shape=WEIGHT_...  4.94 us
    ppermute x9, waiting for transfers between devices, neighbour(): return lax.ppermute(array, ('lat', 'lon'), pairs)  4.56 us
  transfers between devices with their start and end apart: 33, of which 19 were waited for; matrix products, arithmetic and copies ran while one was open for 1% of the time, Pallas kernels for 18%

profile of v2, /device:TPU:0, one launch (start us, length us, event | category | flops | bytes accessed | tf_op | source)
XLA Modules:
  0.0 177.8 jit_solution(658790553077478107)
XLA Ops:
  0.6 2.4 %pack.1 = (bf16[2,12,6,512]{3,2,1,0:T(8,128)(2,1)}, bf16[2,3,48,512]{3,2,1,0:T(8,128)(2,1)}, bf16[2,3,6,512]{3,2,1,0:T(8,128)(2,1)}, bf16[2,12,6,512]{3,2,1,0:T(...) custom-call(bf16[2,12,48,512]{3,2,1,0:T(8,128)(2,1)} %tok.3, bf16[2,12,48,512]{3,2,1,0:T(8,128)(2,1)} %cot.3), custom_call_target="tpu_custom_call" | custom-call | tf_op jit(solution)/shard_map/pack/pallas_call | solution.py:616
  3.0 6.3 %collective-permute-start.1 = (bf16[2,3,48,512]{3,2,1,0:T(8,128)(2,1)}, bf16[2,3,48,512]{3,2,1,0:T(8,128)(2,1)S(1)}, u32[]{:S(2)}, u32[]{:S(2)}) collective-permute-start(bf16[2,3,48,512]{3,2,1,0:T(8,128)(2,1)} %get-tuple-element.56), channel_id=1, source_target_pairs={{0,120},{1,121},{2,122},{3,123},{4,124},{5,125},{6,126},{7,127},{8... | collective-permute-start | bytes 884744 | tf_op jit(solution)/shard_map/ppermute | solution.py:790
  9.3 2.9 %collective-permute-start = (bf16[2,12,6,512]{3,2,1,0:T(8,128)(2,1)}, bf16[2,12,6,512]{3,2,1,0:T(8,128)(2,1)S(1)}, u32[]{:S(2)}, u32[]{:S(2)}) collective-permute-start(bf16[2,12,6,512]{3,2,1,0:T(8,128)(2,1)} %get-tuple-element.55), channel_id=1, source_target_pairs={{0,7},{1,0},{2,1},{3,2},{4,3},{5,4},{6,5},{7,6},{8,15},{9,8},{10,9... | collective-permute-start | bytes 442376 | tf_op jit(solution)/shard_map/ppermute | solution.py:790
  12.1 0.3 collective-permute-start.2
  12.4 1.1 collective-permute-start.3
  13.5 2.2 %collective-permute-start.4 = (bf16[2,3,48,512]{3,2,1,0:T(8,128)(2,1)}, bf16[2,3,48,512]{3,2,1,0:T(8,128)(2,1)S(1)}, u32[]{:S(2)}, u32[]{:S(2)}) collective-permute-start(bf16[2,3,48,512]{3,2,1,0:T(8,128)(2,1)} %get-tuple-element.63), channel_id=1, source_target_pairs={{0,120},{1,121},{2,122},{3,123},{4,124},{5,125},{6,126},{7,127},{8... | collective-permute-start | bytes 884744 | tf_op jit(solution)/shard_map/ppermute | solution.py:790
  15.7 2.4 %collective-permute-done.2.tok_both = bf16[2,3,6,512]{3,2,1,0:T(8,128)(2,1)S(1)} collective-permute-done((bf16[2,3,6,512]{3,2,1,0:T(8,128)(2,1)}, bf16[2,3,6,512]{3,2,1,0:T(8,128)(2,1)S(1)}, u32[]{:S(2)}, u32[]{:S(2)}) %collective-permute-start.2) | collective-permute-done | bytes 36896 | tf_op jit(solution)/shard_map/ppermute | solution.py:790
  18.1 7.2 %collective-permute-start.5 = (bf16[2,3,6,512]{3,2,1,0:T(8,128)(2,1)}, bf16[2,3,6,512]{3,2,1,0:T(8,128)(2,1)S(1)}, u32[]{:S(2)}, u32[]{:S(2)}) collective-permute-start(bf16[2,3,6,512]{3,2,1,0:T(8,128)(2,1)} %get-tuple-element.64), channel_id=1, source_target_pairs={{0,127},{1,120},{2,121},{3,122},{4,123},{5,124},{6,125},{7,126},{8... | collective-permute-start | bytes 110600 | tf_op jit(solution)/shard_map/ppermute | solution.py:790
  25.4 0.6 copy-done.13
  26.1 12.9 %attention.1 = (bf16[1152,512]{1,0:T(8,128)(2,1)}, bf16[1152,512]{1,0:T(8,128)(2,1)}, bf16[512,1152]{1,0:T(8,128)(2,1)}, bf16[1152,1536]{1,0:T(8,128)(2,1)}, bf16[8,9,144,128]{3,2,1,0:T(8,128)(2,1)}) custom-call(bf16[2,12,48,512]{3,2,1,0:T(8,128)(2,1)} %tok.3, bf16[2,12,6,512]{3,2,1,0:T(8,128)(2,1)} %copy-done.13, bf16[2,3,48,512]{3,2,1,0:T(8,128)(2,1)} %copy-done.11, ...), custom_call_target="tpu_custom_call" | custom-call | flops 7247757312 | bytes 20000000 | tf_op jit(solution)/shard_map/attention/pallas_call | solution.py:634
  39.0 0.6 copy-done.14
  39.7 0.1 copy-done.10
  39.8 28.2 %mlp.1 = (bf16[1152,512]{1,0:T(8,128)(2,1)}, f32[1152,512]{1,0:T(8,128)}, bf16[16,576,128]{2,1,0:T(8,128)(2,1)}, bf16[16,576,128]{2,1,0:T(8,128)(2,1)}, f32[1,512]{1,0:T(1,128)}) custom-call(bf16[1152,512]{1,0:T(8,128)(2,1)} %get-tuple-element.58.xw, bf16[1152,512]{1,0:T(8,128)(2,1)} %get-tuple-element.61.mix, bf16[2,12,48,512]{3,2,1,0:T(8,128)(2,1)} %cot.3, ...), custom_call_target="tpu_custom_call" | custom-call | flops 19327352832 | bytes 40000000 | tf_op jit(solution)/shard_map/mlp/pallas_call | solution.py:655
  68.0 0.3 collective-permute-start.6
  68.3 1.3 copy-done.4
  69.6 3.8 %first_back.1 = (bf16[576,1536]{1,0:T(8,128)(2,1)S(1)}, f32[9,144,128]{2,1,0:T(8,128)S(1)}) custom-call(bf16[1152,1536]{1,0:T(8,128)(2,1)S(1)} %copy-done.2, bf16[8,9,144,128]{3,2,1,0:T(8,128)(2,1)S(1)} %copy-done.3, bf16[1152,512]{1,0:T(8,128)(2,1)S(1)} %copy-done.4), custom_call_target="tpu_custom_call" | custom-call | flops 5435817984 | bytes 10000000 | tf_op jit(solution)/shard_map/first_back/pallas_call | solution.py:686
  73.4 0.6 add_convert_fusion
  74.0 0.1 fusion.10
  74.3 1.9 %collective-permute-start.7 = (bf16[4,576,128]{2,1,0:T(8,128)(2,1)S(1)}, bf16[4,576,128]{2,1,0:T(8,128)(2,1)S(1)}, u32[]{:S(2)}, u32[]{:S(2)}) collective-permute-start(bf16[4,576,128]{2,1,0:T(8,128)(2,1)S(1)} %get-tuple-element.102), channel_id=1, source_target_pairs={{0,2},{1,3},{2,4},{3,5},{4,6},{5,7},{6,0},{7,1},{8,9},{9,24},{10,1... | collective-permute-start | bytes 1769480 | tf_op jit(solution)/shard_map/ppermute | solution.py:818
  76.2 8.2 %second_back.1 = (bf16[576,1536]{1,0:T(8,128)(2,1)S(1)}, bf16[16,240,128]{2,1,0:T(8,128)(2,1)S(1)}, bf16[16,240,128]{2,1,0:T(8,128)(2,1)S(1)}) custom-call(bf16[1152,1536]{1,0:T(8,128)(2,1)} %get-tuple-element.59.qkv, bf16[8,9,144,128]{3,2,1,0:T(8,128)(2,1)S(1)} %copy-done.3, bf16[1152,512]{1,0:T(8,128)(2,1)S(1)} %copy-done.4, ...), custom_call_target="tpu_custom_call" | custom-call | flops 7247757312 | bytes 10000000 | tf_op jit(solution)/shard_map/second_back/pallas_call | solution.py:702
  84.5 1.3 collective-permute-done.8
  85.8 6.2 %collective-permute-done.7 = bf16[4,576,128]{2,1,0:T(8,128)(2,1)S(1)} collective-permute-done((bf16[4,576,128]{2,1,0:T(8,128)(2,1)S(1)}, bf16[4,576,128]{2,1,0:T(8,128)(2,1)S(1)}, u32[]{:S(2)}, u32[]{:S(2)}) %collective-permute-start.7) | collective-permute-done | bytes 589856 | tf_op jit(solution)/shard_map/ppermute | solution.py:818
  92.0 0.3 add_convert_fusion.2
  92.4 2.6 %collective-permute-done.10 = bf16[16,240,128]{2,1,0:T(8,128)(2,1)S(1)} collective-permute-done((bf16[16,240,128]{2,1,0:T(8,128)(2,1)S(1)}, bf16[16,240,128]{2,1,0:T(8,128)(2,1)S(1)}, u32[]{:S(2)}, u32[]{:S(2)}) %collective-permute-start.10) | collective-permute-done | bytes 983072 | tf_op jit(solution)/shard_map/ppermute | solution.py:822
  95.0 0.3 add_convert_fusion.1
  95.3 1.1 collective-permute-start.13
  96.5 1.0 collective-permute-start.11
  97.5 4.1 %collective-permute-done.13 = bf16[4,240,128]{2,1,0:T(8,128)(2,1)S(1)} collective-permute-done((bf16[4,240,128]{2,1,0:T(8,128)(2,1)S(1)}, bf16[4,240,128]{2,1,0:T(8,128)(2,1)S(1)}, u32[]{:S(2)}, u32[]{:S(2)}) %collective-permute-start.13) | collective-permute-done | bytes 245792 | tf_op jit(solution)/shard_map/ppermute | solution.py:818
  101.6 2.7 %collective-permute-done.12 = bf16[4,240,128]{2,1,0:T(8,128)(2,1)S(1)} collective-permute-done((bf16[4,240,128]{2,1,0:T(8,128)(2,1)S(1)}, bf16[4,240,128]{2,1,0:T(8,128)(2,1)S(1)}, u32[]{:S(2)}, u32[]{:S(2)}) %collective-permute-start.12) | collective-permute-done | bytes 245792 | tf_op jit(solution)/shard_map/ppermute | solution.py:818
  104.3 2.5 %collective-permute-done.11 = bf16[4,240,128]{2,1,0:T(8,128)(2,1)S(1)} collective-permute-done((bf16[4,240,128]{2,1,0:T(8,128)(2,1)S(1)}, bf16[4,240,128]{2,1,0:T(8,128)(2,1)S(1)}, u32[]{:S(2)}, u32[]{:S(2)}) %collective-permute-start.11) | collective-permute-done | bytes 245792 | tf_op jit(solution)/shard_map/ppermute | solution.py:818
  106.8 0.1 add_convert_fusion.3
  107.1 1.3 collective-permute-start.15
  108.3 1.3 collective-permute-start.14
  109.7 3.2 %collective-permute-done.16 = bf16[816,128]{1,0:T(8,128)(2,1)S(1)} collective-permute-done((bf16[816,128]{1,0:T(8,128)(2,1)S(1)}, bf16[816,128]{1,0:T(8,128)(2,1)S(1)}, u32[]{:S(2)}, u32[]{:S(2)}) %collective-permute-start.16) | collective-permute-done | bytes 208928 | tf_op jit(solution)/shard_map/ppermute | solution.py:818
  112.9 1.7 collective-permute-done.15
  114.6 2.1 %collective-permute-done.14 = bf16[816,128]{1,0:T(8,128)(2,1)S(1)} collective-permute-done((bf16[816,128]{1,0:T(8,128)(2,1)S(1)}, bf16[816,128]{1,0:T(8,128)(2,1)S(1)}, u32[]{:S(2)}, u32[]{:S(2)}) %collective-permute-start.14) | collective-permute-done | bytes 208928 | tf_op jit(solution)/shard_map/ppermute | solution.py:818
  116.7 0.1 fusion.2
  116.8 0.9 collective-permute-start.20
  117.7 1.2 collective-permute-start.19
  118.9 2.5 %collective-permute-start.18 = (bf16[816,128]{1,0:T(8,128)(2,1)S(1)}, bf16[816,128]{1,0:T(8,128)(2,1)S(1)}, u32[]{:S(2)}, u32[]{:S(2)}) collective-permute-start(bf16[816,128]{1,0:T(8,128)(2,1)S(1)} %fusion.2), channel_id=1, source_target_pairs={{0,64},{1,65},{2,66},{3,67},{4,68},{5,69},{6,70},{7,71},{8,12},{9,... | collective-permute-start | bytes 626696 | tf_op jit(solution)/shard_map/ppermute | solution.py:818
  121.5 3.2 %branch.1 = (bf16[2,9,42,512]{3,2,1,0:T(8,128)(2,1)S(1)}, bf16[2,9,6,512]{3,2,1,0:T(8,128)(2,1)S(1)}, bf16[2,3,42,512]{3,2,1,0:T(8,128)(2,1)S(1)}, bf16[2,3,6,512]{3,2,1,0:T(8,128)(2,1)S(1)}) custom-call(bf16[1152,512]{1,0:T(8,128)(2,1)S(1)} %copy-done.7, bf16[576,1536]{1,0:T(8,128)(2,1)S(1)} %get-tuple-element.76.grads_before.grads_first, ...), custom_call_target="tpu_custom_call" | custom-call | flops 7247757312 | bytes 10000000 | tf_op jit(solution)/shard_map/branch/pallas_call | solution.py:720
  124.7 2.7 %collective-permute-done.18 = bf16[816,128]{1,0:T(8,128)(2,1)S(1)} collective-permute-done((bf16[816,128]{1,0:T(8,128)(2,1)S(1)}, bf16[816,128]{1,0:T(8,128)(2,1)S(1)}, u32[]{:S(2)}, u32[]{:S(2)}) %collective-permute-start.18) | collective-permute-done | bytes 208928 | tf_op jit(solution)/shard_map/ppermute | solution.py:818
  127.5 0.1 add_convert_fusion.4
  127.6 0.8 collective-permute-start.23
  128.4 2.4 %collective-permute-start.22 = (bf16[816,128]{1,0:T(8,128)(2,1)S(1)}, bf16[816,128]{1,0:T(8,128)(2,1)S(1)}, u32[]{:S(2)}, u32[]{:S(2)}) collective-permute-start(bf16[816,128]{1,0:T(8,128)(2,1)S(1)} %add_convert_fusion.4), channel_id=1, source_target_pairs={{0,16},{1,17},{2,18},{3,19},{4,20},{5,21},{6,22},{7,23},{8,72},{9,... | collective-permute-start | bytes 626696 | tf_op jit(solution)/shard_map/ppermute | solution.py:818
  130.8 0.6 collective-permute-start.21
  131.5 0.4 collective-permute-start.24
  131.9 1.5 collective-permute-done.23
  133.4 1.2 collective-permute-start.17
  134.7 2.0 %collective-permute-done.22 = bf16[816,128]{1,0:T(8,128)(2,1)S(1)} collective-permute-done((bf16[816,128]{1,0:T(8,128)(2,1)S(1)}, bf16[816,128]{1,0:T(8,128)(2,1)S(1)}, u32[]{:S(2)}, u32[]{:S(2)}) %collective-permute-start.22) | collective-permute-done | bytes 208928 | tf_op jit(solution)/shard_map/ppermute | solution.py:818
  136.7 4.9 %collective-permute-done.21 = bf16[816,128]{1,0:T(8,128)(2,1)S(1)} collective-permute-done((bf16[816,128]{1,0:T(8,128)(2,1)S(1)}, bf16[816,128]{1,0:T(8,128)(2,1)S(1)}, u32[]{:S(2)}, u32[]{:S(2)}) %collective-permute-start.21) | collective-permute-done | bytes 208928 | tf_op jit(solution)/shard_map/ppermute | solution.py:818
  141.6 0.1 pad_maximum_fusion.refs_0_
  141.7 1.9 %collective-permute-done.17 = bf16[2,3,6,512]{3,2,1,0:T(8,128)(2,1)S(1)} collective-permute-done((bf16[2,3,6,512]{3,2,1,0:T(8,128)(2,1)S(1)}, bf16[2,3,6,512]{3,2,1,0:T(8,128)(2,1)S(1)}, u32[]{:S(2)}, u32[]{:S(2)}) %collective-permute-start.17) | collective-permute-done | bytes 36896 | tf_op jit(solution)/shard_map/ppermute | solution.py:790
  143.6 0.3 collective-permute-done.25
  143.9 0.3 collective-permute-start.26
  144.2 1.2 collective-permute-start.27
  145.4 2.1 %collective-permute-start.28 = (bf16[4,816,128]{2,1,0:T(8,128)(2,1)S(1)}, bf16[4,816,128]{2,1,0:T(8,128)(2,1)S(1)}, u32[]{:S(2)}, u32[]{:S(2)}) collective-permute-start(bf16[4,816,128]{2,1,0:T(8,128)(2,1)S(1)} %pad_maximum_fusion.refs_0_), channel_id=1, source_target_pairs={{0,6},{1,7},{2,0},{3,1},{4,2},{5,3},{6,4},{7,5},{8,25},{9,8},{10,2... | collective-permute-start | bytes 2506760 | tf_op jit(solution)/shard_map/ppermute | solution.py:818
  147.5 0.2 collective-permute-start.29
  147.7 18.9 %collective-permute-done.26.refs_1_ = bf16[4,816,128]{2,1,0:T(8,128)(2,1)S(1)} collective-permute-done((bf16[4,816,128]{2,1,0:T(8,128)(2,1)S(1)}, bf16[4,816,128]{2,1,0:T(8,128)(2,1)S(1)}, u32[]{:S(2)}, u32[]{:S(2)}) %collective-permute-start.26) | collective-permute-done | bytes 835616 | tf_op jit(solution)/shard_map/ppermute | solution.py:818
  166.6 0.5 collective-permute-start.31
  167.1 0.4 collective-permute-done.28.refs_3_
  167.5 3.5 %finish_own.1 = (f32[512,2048]{1,0:T(8,128)}, f32[2048,512]{1,0:T(8,128)}, f32[512,1536]{1,0:T(8,128)}, f32[512,512]{1,0:T(8,128)}, f32[512,128]{1,0:T(8,128)S(1)}, /*index=5*/bf16[32,48,128]{2,1,0:T(8,128)(2,1)S(1)}) custom-call(bf16[4,816,128]{2,1,0:T(8,128)(2,1)S(1)} %pad_maximum_fusion.refs_0_, bf16[4,816,128]{2,1,0:T(8,128)(2,1)S(1)} %collective-permute-done.26.refs_1_, ...), custom_call_target="tpu_custom_call" | custom-call | flops 10000000 | bytes 10000000 | tf_op jit(solution)/shard_map/finish_own/pallas_call | solution.py:753
  171.0 1.6 maximum_maximum_fusion
  172.6 4.9 %finish.1 = (f32[512,2048]{1,0:T(8,128)}, f32[2048,512]{1,0:T(8,128)}, f32[512,1536]{1,0:T(8,128)}, f32[512,512]{1,0:T(8,128)}, f32[8,144,144]{2,1,0:T(8,128)}, /*index=5*/f32[1,512]{1,0:T(1,128)}, f32[1,512]{1,0:T(1,128)}) custom-call(bf16[4,816,128]{2,1,0:T(8,128)(2,1)S(1)} %collective-per, ...), custom_call_target="tpu_custom_call", output_to_operand_aliasing={{0}: (8, {}), {1}: (9, {}), {2}: (10, {}), {3}: (11, {})} | custom-call | flops 10000000 | bytes 10000000 | tf_op jit(solution)/shard_map/finish/pallas_call | solution.py:766
  (53 shorter events, 0.8 us)
Async XLA Ops:
  3.0 22.3 %collective-permute-start.1 = (bf16[2,3,48,512]{3,2,1,0:T(8,128)(2,1)}, bf16[2,3,48,512]{3,2,1,0:T(8,128)(2,1)S(1)}, u32[]{:S(2)}, u32[]{:S(2)}) collective-permute-start(bf16[2,3,48,512]{3,2,1,0:T(8,128)(2,1)} %get-tuple-element.56), channel_id=1, source_target_pairs={{0,120},{1,121},{2,122},{3,123},{4,124},{5,125},{6,126},{7,127},{8... | collective-permute-start | bytes 884744 | tf_op jit(solution)/shard_map/ppermute | solution.py:790
  9.3 16.1 %collective-permute-start = (bf16[2,12,6,512]{3,2,1,0:T(8,128)(2,1)}, bf16[2,12,6,512]{3,2,1,0:T(8,128)(2,1)S(1)}, u32[]{:S(2)}, u32[]{:S(2)}) collective-permute-start(bf16[2,12,6,512]{3,2,1,0:T(8,128)(2,1)} %get-tuple-element.55), channel_id=1, source_target_pairs={{0,7},{1,0},{2,1},{3,2},{4,3},{5,4},{6,5},{7,6},{8,15},{9,8},{10,9... | collective-permute-start | bytes 442376 | tf_op jit(solution)/shard_map/ppermute | solution.py:790
  12.1 6.0 %collective-permute-start.2 = (bf16[2,3,6,512]{3,2,1,0:T(8,128)(2,1)}, bf16[2,3,6,512]{3,2,1,0:T(8,128)(2,1)S(1)}, u32[]{:S(2)}, u32[]{:S(2)}) collective-permute-start(bf16[2,3,6,512]{3,2,1,0:T(8,128)(2,1)} %get-tuple-element.57), channel_id=1, source_target_pairs={{0,127},{1,120},{2,121},{3,122},{4,123},{5,124},{6,125},{7,126},{8... | collective-permute-start | bytes 110600 | tf_op jit(solution)/shard_map/ppermute | solution.py:790
  12.4 26.6 %collective-permute-start.3 = (bf16[2,12,6,512]{3,2,1,0:T(8,128)(2,1)}, bf16[2,12,6,512]{3,2,1,0:T(8,128)(2,1)S(1)}, u32[]{:S(2)}, u32[]{:S(2)}) collective-permute-start(bf16[2,12,6,512]{3,2,1,0:T(8,128)(2,1)} %get-tuple-element.62), channel_id=1, source_target_pairs={{0,7},{1,0},{2,1},{3,2},{4,3},{5,4},{6,5},{7,6},{8,15},{9,8},{10,9... | collective-permute-start | bytes 442376 | tf_op jit(solution)/shard_map/ppermute | solution.py:790
  13.5 25.5 %collective-permute-start.4 = (bf16[2,3,48,512]{3,2,1,0:T(8,128)(2,1)}, bf16[2,3,48,512]{3,2,1,0:T(8,128)(2,1)S(1)}, u32[]{:S(2)}, u32[]{:S(2)}) collective-permute-start(bf16[2,3,48,512]{3,2,1,0:T(8,128)(2,1)} %get-tuple-element.63), channel_id=1, source_target_pairs={{0,120},{1,121},{2,122},{3,123},{4,124},{5,125},{6,126},{7,127},{8... | collective-permute-start | bytes 884744 | tf_op jit(solution)/shard_map/ppermute | solution.py:790
  18.1 7.3 %copy-start.15 = (bf16[2,3,6,512]{3,2,1,0:T(8,128)(2,1)}, bf16[2,3,6,512]{3,2,1,0:T(8,128)(2,1)S(1)}, u32[]{:S(2)}) copy-start(bf16[2,3,6,512]{3,2,1,0:T(8,128)(2,1)S(1)} %collective-permute-done.2.tok_both) | copy-start | bytes 110596
  18.1 20.9 %collective-permute-start.5 = (bf16[2,3,6,512]{3,2,1,0:T(8,128)(2,1)}, bf16[2,3,6,512]{3,2,1,0:T(8,128)(2,1)S(1)}, u32[]{:S(2)}, u32[]{:S(2)}) collective-permute-start(bf16[2,3,6,512]{3,2,1,0:T(8,128)(2,1)} %get-tuple-element.64), channel_id=1, source_target_pairs={{0,127},{1,120},{2,121},{3,122},{4,123},{5,124},{6,125},{7,126},{8... | collective-permute-start | bytes 110600 | tf_op jit(solution)/shard_map/ppermute | solution.py:790
  25.3 0.7 copy-start.13
  25.3 0.8 copy-start.11
  39.0 0.6 copy-start.14
  39.0 0.7 copy-start.12
  39.0 0.8 copy-start.10
  39.8 28.5 %copy-start.2 = (bf16[1152,1536]{1,0:T(8,128)(2,1)S(1)}, bf16[1152,1536]{1,0:T(8,128)(2,1)}, u32[]{:S(2)}) copy-start(bf16[1152,1536]{1,0:T(8,128)(2,1)} %get-tuple-element.59.qkv) | copy-start | bytes 10616836
  39.8 28.5 %copy-start.3 = (bf16[8,9,144,128]{3,2,1,0:T(8,128)(2,1)S(1)}, bf16[8,9,144,128]{3,2,1,0:T(8,128)(2,1)}, u32[]{:S(2)}) copy-start(bf16[8,9,144,128]{3,2,1,0:T(8,128)(2,1)} %get-tuple-element.60.probs) | copy-start | bytes 7962628
  68.0 5.4 %collective-permute-start.6 = (bf16[16,576,128]{2,1,0:T(8,128)(2,1)}, bf16[16,576,128]{2,1,0:T(8,128)(2,1)S(1)}, u32[]{:S(2)}, u32[]{:S(2)}) collective-permute-start(bf16[16,576,128]{2,1,0:T(8,128)(2,1)} %get-tuple-element.68), channel_id=1, source_target_pairs={{0,8},{8,0},{16,24},{24,16},{32,40},{40,32},{48,56},{56,48},{64,72... | collective-permute-start | bytes 7077896 | tf_op jit(solution)/shard_map/ppermute | solution.py:822
  68.3 1.3 copy-start.4
  69.6 3.8 %copy-start.9 = (bf16[16,576,128]{2,1,0:T(8,128)(2,1)S(1)}, bf16[16,576,128]{2,1,0:T(8,128)(2,1)}, u32[]{:S(2)}) copy-start(bf16[16,576,128]{2,1,0:T(8,128)(2,1)} %get-tuple-element.67) | copy-start | bytes 7077892
  74.0 2.3 %copy-start.6 = (bf16[512,1152]{1,0:T(8,128)(2,1)S(1)}, bf16[512,1152]{1,0:T(8,128)(2,1)}, u32[]{:S(2)}) copy-start(bf16[512,1152]{1,0:T(8,128)(2,1)} %get-tuple-element.69.act_t) | copy-start | bytes 3538948
  74.0 2.2 %copy-start.8 = (f32[1,512]{1,0:T(1,128)S(1)}, f32[1,512]{1,0:T(1,128)}, u32[]{:S(2)}) copy-start(f32[1,512]{1,0:T(1,128)} %get-tuple-element.70.sum_gain_two) | copy-start | bytes 6148
  74.1 10.3 %collective-permute-start.9 = (bf16[4,576,128]{2,1,0:T(8,128)(2,1)S(1)}, bf16[4,576,128]{2,1,0:T(8,128)(2,1)S(1)}, u32[]{:S(2)}, u32[]{:S(2)}) collective-permute-start(bf16[4,576,128]{2,1,0:T(8,128)(2,1)S(1)} %get-tuple-element.103), channel_id=1, source_target_pairs={{0,6},{1,7},{2,0},{3,1},{4,2},{5,3},{6,4},{7,5},{8,25},{9,8},{10,2... | collective-permute-start | bytes 1769480 | tf_op jit(solution)/shard_map/ppermute | solution.py:818
  74.2 11.6 %collective-permute-start.8 = (bf16[4,576,128]{2,1,0:T(8,128)(2,1)S(1)}, bf16[4,576,128]{2,1,0:T(8,128)(2,1)S(1)}, u32[]{:S(2)}, u32[]{:S(2)}) collective-permute-start(bf16[4,576,128]{2,1,0:T(8,128)(2,1)S(1)} %get-tuple-element.104), channel_id=1, source_target_pairs={{0,4},{1,5},{2,6},{3,7},{4,0},{5,1},{6,2},{7,3},{8,24},{9,25},{10,... | collective-permute-start | bytes 1769480 | tf_op jit(solution)/shard_map/ppermute | solution.py:818
  74.3 17.7 %collective-permute-start.7 = (bf16[4,576,128]{2,1,0:T(8,128)(2,1)S(1)}, bf16[4,576,128]{2,1,0:T(8,128)(2,1)S(1)}, u32[]{:S(2)}, u32[]{:S(2)}) collective-permute-start(bf16[4,576,128]{2,1,0:T(8,128)(2,1)S(1)} %get-tuple-element.102), channel_id=1, source_target_pairs={{0,2},{1,3},{2,4},{3,5},{4,6},{5,7},{6,0},{7,1},{8,9},{9,24},{10,1... | collective-permute-start | bytes 1769480 | tf_op jit(solution)/shard_map/ppermute | solution.py:818
  92.3 2.6 %collective-permute-start.10 = (bf16[16,240,128]{2,1,0:T(8,128)(2,1)S(1)}, bf16[16,240,128]{2,1,0:T(8,128)(2,1)S(1)}, u32[]{:S(2)}, u32[]{:S(2)}) collective-permute-start(bf16[16,240,128]{2,1,0:T(8,128)(2,1)S(1)} %get-tuple-element.75), channel_id=1, source_target_pairs={{0,8},{8,0},{16,24},{24,16},{32,40},{40,32},{48,56},{56,48},{64,72... | collective-permute-start | bytes 2949128 | tf_op jit(solution)/shard_map/ppermute | solution.py:822
  95.2 26.2 %copy-start.7 = (bf16[1152,512]{1,0:T(8,128)(2,1)S(1)}, bf16[1152,512]{1,0:T(8,128)(2,1)}, u32[]{:S(2)}) copy-start(bf16[1152,512]{1,0:T(8,128)(2,1)} %get-tuple-element.58.xw) | copy-start | bytes 3538948
  95.3 6.3 %collective-permute-start.13 = (bf16[4,240,128]{2,1,0:T(8,128)(2,1)S(1)}, bf16[4,240,128]{2,1,0:T(8,128)(2,1)S(1)}, u32[]{:S(2)}, u32[]{:S(2)}) collective-permute-start(bf16[4,240,128]{2,1,0:T(8,128)(2,1)S(1)} %get-tuple-element.106), channel_id=1, source_target_pairs={{0,6},{1,7},{2,0},{3,1},{4,2},{5,3},{6,4},{7,5},{8,25},{9,8},{10,2... | collective-permute-start | bytes 737288 | tf_op jit(solution)/shard_map/ppermute | solution.py:818
  96.4 7.8 %collective-permute-start.12 = (bf16[4,240,128]{2,1,0:T(8,128)(2,1)S(1)}, bf16[4,240,128]{2,1,0:T(8,128)(2,1)S(1)}, u32[]{:S(2)}, u32[]{:S(2)}) collective-permute-start(bf16[4,240,128]{2,1,0:T(8,128)(2,1)S(1)} %get-tuple-element.107), channel_id=1, source_target_pairs={{0,4},{1,5},{2,6},{3,7},{4,0},{5,1},{6,2},{7,3},{8,24},{9,25},{10,... | collective-permute-start | bytes 737288 | tf_op jit(solution)/shard_map/ppermute | solution.py:818
  96.5 25.0 %copy-start = (bf16[512,1536]{1,0:T(8,128)(2,1)S(1)}, bf16[512,1536]{1,0:T(8,128)(2,1)}, u32[]{:S(2)}) copy-start(bf16[512,1536]{1,0:T(8,128)(2,1)} %refs_4_.3) | copy-start | bytes 4718596
  96.5 25.0 %copy-start.1 = (f32[512]{0:T(512)S(1)}, f32[512]{0:T(512)}, u32[]{:S(2)}) copy-start(f32[512]{0:T(512)} %param.16) | copy-start | bytes 6148
  96.5 25.0 %copy-start.5 = (f32[1152,512]{1,0:T(8,128)S(1)}, f32[1152,512]{1,0:T(8,128)}, u32[]{:S(2)}) copy-start(f32[1152,512]{1,0:T(8,128)} %get-tuple-element.78.grad_res) | copy-start | bytes 7077892
  96.5 10.3 %collective-permute-start.11 = (bf16[4,240,128]{2,1,0:T(8,128)(2,1)S(1)}, bf16[4,240,128]{2,1,0:T(8,128)(2,1)S(1)}, u32[]{:S(2)}, u32[]{:S(2)}) collective-permute-start(bf16[4,240,128]{2,1,0:T(8,128)(2,1)S(1)} %get-tuple-element.105), channel_id=1, source_target_pairs={{0,2},{1,3},{2,4},{3,5},{4,6},{5,7},{6,0},{7,1},{8,9},{9,24},{10,1... | collective-permute-start | bytes 737288 | tf_op jit(solution)/shard_map/ppermute | solution.py:818
  107.0 5.9 %collective-permute-start.16 = (bf16[816,128]{1,0:T(8,128)(2,1)S(1)}, bf16[816,128]{1,0:T(8,128)(2,1)S(1)}, u32[]{:S(2)}, u32[]{:S(2)}) collective-permute-start(bf16[816,128]{1,0:T(8,128)(2,1)S(1)} %get-tuple-element.109), channel_id=1, source_target_pairs={{0,17},{1,0},{2,19},{3,2},{4,21},{5,4},{6,23},{7,6},{8,104},{9,105... | collective-permute-start | bytes 626696 | tf_op jit(solution)/shard_map/ppermute | solution.py:818
  107.1 7.5 %collective-permute-start.15 = (bf16[816,128]{1,0:T(8,128)(2,1)S(1)}, bf16[816,128]{1,0:T(8,128)(2,1)S(1)}, u32[]{:S(2)}, u32[]{:S(2)}) collective-permute-start(bf16[816,128]{1,0:T(8,128)(2,1)S(1)} %get-tuple-element.110), channel_id=1, source_target_pairs={{0,16},{1,17},{2,18},{3,19},{4,20},{5,21},{6,22},{7,23},{8,72},{9,... | collective-permute-start | bytes 626696 | tf_op jit(solution)/shard_map/ppermute | solution.py:818
  108.3 8.4 %collective-permute-start.14 = (bf16[816,128]{1,0:T(8,128)(2,1)S(1)}, bf16[816,128]{1,0:T(8,128)(2,1)S(1)}, u32[]{:S(2)}, u32[]{:S(2)}) collective-permute-start(bf16[816,128]{1,0:T(8,128)(2,1)S(1)} %get-tuple-element.108), channel_id=1, source_target_pairs={{0,1},{1,16},{2,3},{3,18},{4,5},{5,20},{6,7},{7,22},{8,40},{9,41},... | collective-permute-start | bytes 626696 | tf_op jit(solution)/shard_map/ppermute | solution.py:818
  116.8 7.8 %collective-permute-start.20 = (bf16[816,128]{1,0:T(8,128)(2,1)S(1)}, bf16[816,128]{1,0:T(8,128)(2,1)S(1)}, u32[]{:S(2)}, u32[]{:S(2)}) collective-permute-start(bf16[816,128]{1,0:T(8,128)(2,1)S(1)} %fusion.2), channel_id=1, source_target_pairs={{0,96},{1,97},{2,98},{3,99},{4,100},{5,101},{6,102},{7,103},{8,14}... | collective-permute-start | bytes 626696 | tf_op jit(solution)/shard_map/ppermute | solution.py:818
  117.7 7.0 %collective-permute-start.19 = (bf16[816,128]{1,0:T(8,128)(2,1)S(1)}, bf16[816,128]{1,0:T(8,128)(2,1)S(1)}, u32[]{:S(2)}, u32[]{:S(2)}) collective-permute-start(bf16[816,128]{1,0:T(8,128)(2,1)S(1)} %fusion.2), channel_id=1, source_target_pairs={{0,32},{1,33},{2,34},{3,35},{4,36},{5,37},{6,38},{7,39},{8,10},{9,... | collective-permute-start | bytes 626696 | tf_op jit(solution)/shard_map/ppermute | solution.py:818
  118.9 8.5 %collective-permute-start.18 = (bf16[816,128]{1,0:T(8,128)(2,1)S(1)}, bf16[816,128]{1,0:T(8,128)(2,1)S(1)}, u32[]{:S(2)}, u32[]{:S(2)}) collective-permute-start(bf16[816,128]{1,0:T(8,128)(2,1)S(1)} %fusion.2), channel_id=1, source_target_pairs={{0,64},{1,65},{2,66},{3,67},{4,68},{5,69},{6,70},{7,71},{8,12},{9,... | collective-permute-start | bytes 626696 | tf_op jit(solution)/shard_map/ppermute | solution.py:818
  127.6 5.9 %collective-permute-start.23 = (bf16[816,128]{1,0:T(8,128)(2,1)S(1)}, bf16[816,128]{1,0:T(8,128)(2,1)S(1)}, u32[]{:S(2)}, u32[]{:S(2)}) collective-permute-start(bf16[816,128]{1,0:T(8,128)(2,1)S(1)} %add_convert_fusion.4), channel_id=1, source_target_pairs={{0,17},{1,0},{2,19},{3,2},{4,21},{5,4},{6,23},{7,6},{8,104},{9,105... | collective-permute-start | bytes 626696 | tf_op jit(solution)/shard_map/ppermute | solution.py:818
  128.4 8.3 %collective-permute-start.22 = (bf16[816,128]{1,0:T(8,128)(2,1)S(1)}, bf16[816,128]{1,0:T(8,128)(2,1)S(1)}, u32[]{:S(2)}, u32[]{:S(2)}) collective-permute-start(bf16[816,128]{1,0:T(8,128)(2,1)S(1)} %add_convert_fusion.4), channel_id=1, source_target_pairs={{0,16},{1,17},{2,18},{3,19},{4,20},{5,21},{6,22},{7,23},{8,72},{9,... | collective-permute-start | bytes 626696 | tf_op jit(solution)/shard_map/ppermute | solution.py:818
  130.8 10.8 %collective-permute-start.21 = (bf16[816,128]{1,0:T(8,128)(2,1)S(1)}, bf16[816,128]{1,0:T(8,128)(2,1)S(1)}, u32[]{:S(2)}, u32[]{:S(2)}) collective-permute-start(bf16[816,128]{1,0:T(8,128)(2,1)S(1)} %add_convert_fusion.4), channel_id=1, source_target_pairs={{0,1},{1,16},{2,3},{3,18},{4,5},{5,20},{6,7},{7,22},{8,40},{9,41},... | collective-permute-start | bytes 626696 | tf_op jit(solution)/shard_map/ppermute | solution.py:818
  131.5 12.4 %collective-permute-start.25 = (bf16[2,3,42,512]{3,2,1,0:T(8,128)(2,1)S(1)}, bf16[2,3,42,512]{3,2,1,0:T(8,128)(2,1)S(1)}, u32[]{:S(2)}, u32[]{:S(2)}) collective-permute-start(bf16[2,3,42,512]{3,2,1,0:T(8,128)(2,1)S(1)} %get-tuple-element.82), channel_id=1, source_target_pairs={{0,8},{1,9},{2,10},{3,11},{4,12},{5,13},{6,14},{7,15},{8,16},{9,17... | collective-permute-start | bytes 774152 | tf_op jit(solution)/shard_map/ppermute | solution.py:790
  131.5 12.1 %collective-permute-start.24 = (bf16[2,9,6,512]{3,2,1,0:T(8,128)(2,1)S(1)}, bf16[2,9,6,512]{3,2,1,0:T(8,128)(2,1)S(1)}, u32[]{:S(2)}, u32[]{:S(2)}) collective-permute-start(bf16[2,9,6,512]{3,2,1,0:T(8,128)(2,1)S(1)} %get-tuple-element.81), channel_id=1, source_target_pairs={{0,1},{1,2},{2,3},{3,4},{4,5},{5,6},{6,7},{7,0},{8,9},{9,10},{10,1... | collective-permute-start | bytes 331784 | tf_op jit(solution)/shard_map/ppermute | solution.py:790
  133.4 10.2 %collective-permute-start.17 = (bf16[2,3,6,512]{3,2,1,0:T(8,128)(2,1)S(1)}, bf16[2,3,6,512]{3,2,1,0:T(8,128)(2,1)S(1)}, u32[]{:S(2)}, u32[]{:S(2)}) collective-permute-start(bf16[2,3,6,512]{3,2,1,0:T(8,128)(2,1)S(1)} %get-tuple-element.79), channel_id=1, source_target_pairs={{0,9},{1,10},{2,11},{3,12},{4,13},{5,14},{6,15},{7,8},{8,17},{9,18... | collective-permute-start | bytes 110600 | tf_op jit(solution)/shard_map/ppermute | solution.py:790
  143.9 22.7 %collective-permute-start.26 = (bf16[4,816,128]{2,1,0:T(8,128)(2,1)S(1)}, bf16[4,816,128]{2,1,0:T(8,128)(2,1)S(1)}, u32[]{:S(2)}, u32[]{:S(2)}) collective-permute-start(bf16[4,816,128]{2,1,0:T(8,128)(2,1)S(1)} %pad_maximum_fusion.refs_0_), channel_id=1, source_target_pairs={{0,2},{1,3},{2,4},{3,5},{4,6},{5,7},{6,0},{7,1},{8,9},{9,24},{10,1... | collective-permute-start | bytes 2506760 | tf_op jit(solution)/shard_map/ppermute | solution.py:818
  144.2 22.4 %collective-permute-start.27 = (bf16[4,816,128]{2,1,0:T(8,128)(2,1)S(1)}, bf16[4,816,128]{2,1,0:T(8,128)(2,1)S(1)}, u32[]{:S(2)}, u32[]{:S(2)}) collective-permute-start(bf16[4,816,128]{2,1,0:T(8,128)(2,1)S(1)} %pad_maximum_fusion.refs_0_), channel_id=1, source_target_pairs={{0,4},{1,5},{2,6},{3,7},{4,0},{5,1},{6,2},{7,3},{8,24},{9,25},{10,... | collective-permute-start | bytes 2506760 | tf_op jit(solution)/shard_map/ppermute | solution.py:818
  145.4 22.0 %collective-permute-start.28 = (bf16[4,816,128]{2,1,0:T(8,128)(2,1)S(1)}, bf16[4,816,128]{2,1,0:T(8,128)(2,1)S(1)}, u32[]{:S(2)}, u32[]{:S(2)}) collective-permute-start(bf16[4,816,128]{2,1,0:T(8,128)(2,1)S(1)} %pad_maximum_fusion.refs_0_), channel_id=1, source_target_pairs={{0,6},{1,7},{2,0},{3,1},{4,2},{5,3},{6,4},{7,5},{8,25},{9,8},{10,2... | collective-permute-start | bytes 2506760 | tf_op jit(solution)/shard_map/ppermute | solution.py:818
  147.5 25.1 %collective-permute-start.29 = (bf16[4,816,128]{2,1,0:T(8,128)(2,1)S(1)}, bf16[4,816,128]{2,1,0:T(8,128)(2,1)S(1)}, u32[]{:S(2)}, u32[]{:S(2)}) collective-permute-start(bf16[4,816,128]{2,1,0:T(8,128)(2,1)S(1)} %pad_maximum_fusion.refs_0_), channel_id=1, source_target_pairs={{0,8},{8,0},{16,24},{24,16},{32,40},{40,32},{48,56},{56,48},{64,72... | collective-permute-start | bytes 2506760 | tf_op jit(solution)/shard_map/ppermute | solution.py:822
  166.6 6.0 %collective-permute-start.30 = (bf16[4,816,128]{2,1,0:T(8,128)(2,1)S(1)}, bf16[4,816,128]{2,1,0:T(8,128)(2,1)S(1)}, u32[]{:S(2)}, u32[]{:S(2)}) collective-permute-start(bf16[4,816,128]{2,1,0:T(8,128)(2,1)S(1)} %collective-permute-done.26.refs_1_), channel_id=1, source_target_pairs={{0,8},{8,0},{16,24},{24,16},{32,40},{40,32},{48,56},{56,48},{64,72... | collective-permute-start | bytes 2506760 | tf_op jit(solution)/shard_map/ppermute | solution.py:822
  166.6 6.0 %collective-permute-start.31 = (bf16[4,816,128]{2,1,0:T(8,128)(2,1)S(1)}, bf16[4,816,128]{2,1,0:T(8,128)(2,1)S(1)}, u32[]{:S(2)}, u32[]{:S(2)}) collective-permute-start(bf16[4,816,128]{2,1,0:T(8,128)(2,1)S(1)} %collective-permute-done.27.refs_2_), channel_id=1, source_target_pairs={{0,8},{8,0},{16,24},{24,16},{32,40},{40,32},{48,56},{56,48},{64,72... | collective-permute-start | bytes 2506760 | tf_op jit(solution)/shard_map/ppermute | solution.py:822
  167.5 5.2 %collective-permute-start.32 = (bf16[4,816,128]{2,1,0:T(8,128)(2,1)S(1)}, bf16[4,816,128]{2,1,0:T(8,128)(2,1)S(1)}, u32[]{:S(2)}, u32[]{:S(2)}) collective-permute-start(bf16[4,816,128]{2,1,0:T(8,128)(2,1)S(1)} %collective-permute-done.28.refs_3_), channel_id=1, source_target_pairs={{0,8},{8,0},{16,24},{24,16},{32,40},{40,32},{48,56},{56,48},{64,72... | collective-permute-start | bytes 2506760 | tf_op jit(solution)/shard_map/ppermute | solution.py:822

commit v3 on v1

--- a/solution.py
+++ b/solution.py
@@ -838,11 +838,13 @@
     return ((share.astype(F32) + two) + (one + three)).astype(BF16)
 
 
-def spread(share, before):
+def spread(share, home):
     held = jnp.stack([share] + [along(share, 1, k) for k in (1, 2, 3)])
-    held = after(held, before)
+    held = after(held, home)
+    grad_tokens = assemble(*[after(piece, held) for piece in home])
     own = [held] + [along(held, 0, k) for k in (1, 2, 3)]
-    return own, [other_core(piece) for piece in own]
+    other = [other_core(held)] + [other_core(after(piece, grad_tokens)) for piece in own[1:]]
+    return own, other, grad_tokens
 
 
 def local(tokens, cotangent, w_qkv, w_proj, w_up, w_down, pair_bias, gain_one, gain_two):
@@ -869,13 +871,13 @@
     home = branch(xw, after(grads_first, share), grads_second, grad_res, w_qkv, gain_one)
     share = after(last_sum(share), home)
     home = send_home(*home)
-    own, other = spread(share, home)
+    own, other, grad_tokens = spread(share, home)
     *weights, sums, rest = finish_own(own, w_qkv, scale)
     sum_up, sum_down, sum_qkv, sum_proj, sum_bias, sum_one, sum_two = finish(
         other, w_qkv, gain_one, sums, rest, weights, scale
     )
     return (
-        assemble(*[after(piece, sums) for piece in home]),
+        grad_tokens,
         sum_qkv,
         sum_proj,
         sum_up,

time: 178 us -> 177 us (level)
  waiting for transfers between devices: 58.1 us -> 51.9 us
  starting transfers between devices: 43.7 us -> 48.2 us
    ppermute x18, starting transfers between devices: 21.1 us -> 30.4 us  [along(): return lax.ppermute(array, ('lat', 'lon'), pairs)]
    ppermute x18, waiting for transfers between devices: 53.4 us -> 44.5 us  [along(): return lax.ppermute(array, ('lat', 'lon'), pairs)]
    ppermute x9, starting transfers between devices: 21.4 us -> 17.4 us  [neighbour(): return lax.ppermute(array, ('lat', 'lon'), pairs)]
    ppermute x9, waiting for transfers between devices: 2.14 us -> 4.81 us  [neighbour(): return lax.ppermute(array, ('lat', 'lon'), pairs)]
  transfers between devices with their start and end apart: 33 -> 33, of which waited for: 17 -> 16; matrix products, arithmetic and copies ran while one was open for 1% -> 1% of each run, Pallas kernels for 18% -> 18%
where the time goes in v3:
time: 177 us; the launch traced here: 175 us
  Pallas kernels  64.7 us (37%)
  waiting for transfers between devices  51.9 us (29%)
  starting transfers between devices  48.2 us (27%)
  local copies, waits for them, and re-layouts  5.52 us (3%)
  other arithmetic  3.33 us (2%)
    ppermute x18, waiting for transfers between devices, along(): return lax.ppermute(array, ('lat', 'lon'), pairs)  44.5 us
    ppermute x18, starting transfers between devices, along(): return lax.ppermute(array, ('lat', 'lon'), pairs)  30.4 us
    pallas_call x1, Pallas kernels, mlp_call(): pl.pallas_call(mlp_kernel, out_shape=(shape(ROWS, D), shape(ROWS, D, dtyp...  28.2 us
    ppermute x9, starting transfers between devices, neighbour(): return lax.ppermute(array, ('lat', 'lon'), pairs)  17.4 us
    pallas_call x1, Pallas kernels, attention(): pl.pallas_call(attention_kernel, out_shape=(shape(ROWS, D), shape(ROWS, D...  12.9 us
    pallas_call x1, Pallas kernels, second_back(): pl.pallas_call(second_back_kernel, out_shape=(shape(ROWS // 2, QKV), shap...  8.22 us
    unnamed x36, local copies, waits for them, and re-layouts  5.35 us
    pallas_call x1, Pallas kernels, finish(): pl.pallas_call(functools.partial(finish_kernel, scale), out_shape=WEIGHT_...  4.94 us
  transfers between devices with their start and end apart: 33, of which 16 were waited for; matrix products, arithmetic and copies ran while one was open for 1% of the time, Pallas kernels for 18%

profile of v3, /device:TPU:0, one launch (start us, length us, event | category | flops | bytes accessed | tf_op | source)
XLA Modules:
  0.0 174.8 jit_solution(14986396277340587440)
XLA Ops:
  0.6 1.3 copy-done.1
  1.9 6.3 %collective-permute-start.1 = (bf16[2,3,48,512]{3,2,1,0:T(8,128)(2,1)S(1)}, bf16[2,3,48,512]{3,2,1,0:T(8,128)(2,1)S(1)}, u32[]{:S(2)}, u32[]{:S(2)}) collective-permute-start(bf16[2,3,48,512]{3,2,1,0:T(8,128)(2,1)S(1)} %get-tuple-element.59), channel_id=1, source_target_pairs={{0,120},{1,121},{2,122},{3,123},{4,124},{5,125},{6,126},{7,127},{8... | collective-permute-start | bytes 884744 | tf_op jit(solution)/shard_map/ppermute | solution.py:776
  8.2 2.9 %collective-permute-start = (bf16[2,12,6,512]{3,2,1,0:T(8,128)(2,1)S(1)}, bf16[2,12,6,512]{3,2,1,0:T(8,128)(2,1)S(1)}, u32[]{:S(2)}, u32[]{:S(2)}) collective-permute-start(bf16[2,12,6,512]{3,2,1,0:T(8,128)(2,1)S(1)} %get-tuple-element.58), channel_id=1, source_target_pairs={{0,7},{1,0},{2,1},{3,2},{4,3},{5,4},{6,5},{7,6},{8,15},{9,8},{10,9... | collective-permute-start | bytes 442376 | tf_op jit(solution)/shard_map/ppermute | solution.py:776
  11.1 0.3 collective-permute-start.2
  11.4 1.3 copy-done.2
  12.7 2.2 %collective-permute-start.5 = (bf16[2,3,6,512]{3,2,1,0:T(8,128)(2,1)S(1)}, bf16[2,3,6,512]{3,2,1,0:T(8,128)(2,1)S(1)}, u32[]{:S(2)}, u32[]{:S(2)}) collective-permute-start(bf16[2,3,6,512]{3,2,1,0:T(8,128)(2,1)S(1)} %get-tuple-element.67), channel_id=1, source_target_pairs={{0,127},{1,120},{2,121},{3,122},{4,123},{5,124},{6,125},{7,126},{8... | collective-permute-start | bytes 110600 | tf_op jit(solution)/shard_map/ppermute | solution.py:776
  14.9 1.4 collective-permute-done.2.tok_both
  16.3 1.4 collective-permute-start.4
  17.7 0.6 copy-done.15
  18.4 0.1 copy-done.12
  18.5 12.9 %attention.1 = (bf16[1152,512]{1,0:T(8,128)(2,1)}, bf16[1152,512]{1,0:T(8,128)(2,1)}, bf16[512,1152]{1,0:T(8,128)(2,1)}, bf16[1152,1536]{1,0:T(8,128)(2,1)}, bf16[8,9,144,128]{3,2,1,0:T(8,128)(2,1)}) custom-call(bf16[2,12,48,512]{3,2,1,0:T(8,128)(2,1)} %tok.1, bf16[2,12,6,512]{3,2,1,0:T(8,128)(2,1)} %copy-done.15, bf16[2,3,48,512]{3,2,1,0:T(8,128)(2,1)} %copy-done.12, ...), custom_call_target="tpu_custom_call" | custom-call | flops 7247757312 | bytes 20000000 | tf_op jit(solution)/shard_map/attention/pallas_call | solution.py:620
  31.4 0.6 copy-done.16
  32.0 0.1 copy-done.14
  32.1 0.1 copy-done.13
  32.2 28.2 %mlp.1 = (bf16[1152,512]{1,0:T(8,128)(2,1)}, f32[1152,512]{1,0:T(8,128)}, bf16[16,576,128]{2,1,0:T(8,128)(2,1)}, bf16[16,576,128]{2,1,0:T(8,128)(2,1)}, f32[1,512]{1,0:T(1,128)}) custom-call(bf16[1152,512]{1,0:T(8,128)(2,1)} %get-tuple-element.61.xw, bf16[1152,512]{1,0:T(8,128)(2,1)} %get-tuple-element.64.mix, bf16[2,12,48,512]{3,2,1,0:T(8,128)(2,1)} %cot.1, ...), custom_call_target="tpu_custom_call" | custom-call | flops 19327352832 | bytes 40000000 | tf_op jit(solution)/shard_map/mlp/pallas_call | solution.py:641
  60.4 0.3 collective-permute-start.6
  60.7 1.3 copy-done.6
  62.0 3.7 %first_back.1 = (bf16[576,1536]{1,0:T(8,128)(2,1)S(1)}, f32[9,144,128]{2,1,0:T(8,128)S(1)}) custom-call(bf16[1152,1536]{1,0:T(8,128)(2,1)S(1)} %copy-done.4, bf16[8,9,144,128]{3,2,1,0:T(8,128)(2,1)S(1)} %copy-done.5, bf16[1152,512]{1,0:T(8,128)(2,1)S(1)} %copy-done.6), custom_call_target="tpu_custom_call" | custom-call | flops 5435817984 | bytes 10000000 | tf_op jit(solution)/shard_map/first_back/pallas_call | solution.py:672
  65.8 0.6 add_convert_fusion
  66.4 0.1 fusion.10
  66.5 3.6 %collective-permute-start.7 = (bf16[4,576,128]{2,1,0:T(8,128)(2,1)S(1)}, bf16[4,576,128]{2,1,0:T(8,128)(2,1)S(1)}, u32[]{:S(2)}, u32[]{:S(2)}) collective-permute-start(bf16[4,576,128]{2,1,0:T(8,128)(2,1)S(1)} %get-tuple-element.108), channel_id=1, source_target_pairs={{0,2},{1,3},{2,4},{3,5},{4,6},{5,7},{6,0},{7,1},{8,9},{9,24},{10,1... | collective-permute-start | bytes 1769480 | tf_op jit(solution)/shard_map/ppermute | solution.py:805
  70.2 0.1 collective-permute-start.9
  70.3 3.4 %collective-permute-start.8 = (bf16[4,576,128]{2,1,0:T(8,128)(2,1)S(1)}, bf16[4,576,128]{2,1,0:T(8,128)(2,1)S(1)}, u32[]{:S(2)}, u32[]{:S(2)}) collective-permute-start(bf16[4,576,128]{2,1,0:T(8,128)(2,1)S(1)} %get-tuple-element.110), channel_id=1, source_target_pairs={{0,4},{1,5},{2,6},{3,7},{4,0},{5,1},{6,2},{7,3},{8,24},{9,25},{10,... | collective-permute-start | bytes 1769480 | tf_op jit(solution)/shard_map/ppermute | solution.py:805
  73.7 8.2 %second_back.1 = (bf16[576,1536]{1,0:T(8,128)(2,1)S(1)}, bf16[16,240,128]{2,1,0:T(8,128)(2,1)S(1)}, bf16[16,240,128]{2,1,0:T(8,128)(2,1)S(1)}) custom-call(bf16[1152,1536]{1,0:T(8,128)(2,1)} %get-tuple-element.62.qkv, bf16[8,9,144,128]{3,2,1,0:T(8,128)(2,1)S(1)} %copy-done.5, bf16[1152,512]{1,0:T(8,128)(2,1)S(1)} %copy-done.6, ...), custom_call_target="tpu_custom_call" | custom-call | flops 7247757312 | bytes 10000000 | tf_op jit(solution)/shard_map/second_back/pallas_call | solution.py:688
  82.0 3.9 %collective-permute-done.8 = bf16[4,576,128]{2,1,0:T(8,128)(2,1)S(1)} collective-permute-done((bf16[4,576,128]{2,1,0:T(8,128)(2,1)S(1)}, bf16[4,576,128]{2,1,0:T(8,128)(2,1)S(1)}, u32[]{:S(2)}, u32[]{:S(2)}) %collective-permute-start.8) | collective-permute-done | bytes 589856 | tf_op jit(solution)/shard_map/ppermute | solution.py:805
  85.9 0.3 add_convert_fusion.2
  86.2 0.1 collective-permute-start.10
  86.3 2.6 %collective-permute-done.10 = bf16[16,240,128]{2,1,0:T(8,128)(2,1)S(1)} collective-permute-done((bf16[16,240,128]{2,1,0:T(8,128)(2,1)S(1)}, bf16[16,240,128]{2,1,0:T(8,128)(2,1)S(1)}, u32[]{:S(2)}, u32[]{:S(2)}) %collective-permute-start.10) | collective-permute-done | bytes 983072 | tf_op jit(solution)/shard_map/ppermute | solution.py:809
  88.8 0.3 add_convert_fusion.1
  89.2 2.1 %collective-permute-start.11 = (bf16[4,240,128]{2,1,0:T(8,128)(2,1)S(1)}, bf16[4,240,128]{2,1,0:T(8,128)(2,1)S(1)}, u32[]{:S(2)}, u32[]{:S(2)}) collective-permute-start(bf16[4,240,128]{2,1,0:T(8,128)(2,1)S(1)} %get-tuple-element.111), channel_id=1, source_target_pairs={{0,2},{1,3},{2,4},{3,5},{4,6},{5,7},{6,0},{7,1},{8,9},{9,24},{10,1... | collective-permute-start | bytes 737288 | tf_op jit(solution)/shard_map/ppermute | solution.py:805
  91.2 1.3 collective-permute-start.13
  92.5 1.5 collective-permute-start.12
  94.0 2.7 %collective-permute-done.11 = bf16[4,240,128]{2,1,0:T(8,128)(2,1)S(1)} collective-permute-done((bf16[4,240,128]{2,1,0:T(8,128)(2,1)S(1)}, bf16[4,240,128]{2,1,0:T(8,128)(2,1)S(1)}, u32[]{:S(2)}, u32[]{:S(2)}) %collective-permute-start.11) | collective-permute-done | bytes 245792 | tf_op jit(solution)/shard_map/ppermute | solution.py:805
  96.7 0.8 collective-permute-done.13
  97.4 3.3 %collective-permute-done.12 = bf16[4,240,128]{2,1,0:T(8,128)(2,1)S(1)} collective-permute-done((bf16[4,240,128]{2,1,0:T(8,128)(2,1)S(1)}, bf16[4,240,128]{2,1,0:T(8,128)(2,1)S(1)}, u32[]{:S(2)}, u32[]{:S(2)}) %collective-permute-start.12) | collective-permute-done | bytes 245792 | tf_op jit(solution)/shard_map/ppermute | solution.py:805
  100.7 0.1 add_convert_fusion.3
  100.9 3.3 %collective-permute-start.14 = (bf16[816,128]{1,0:T(8,128)(2,1)S(1)}, bf16[816,128]{1,0:T(8,128)(2,1)S(1)}, u32[]{:S(2)}, u32[]{:S(2)}) collective-permute-start(bf16[816,128]{1,0:T(8,128)(2,1)S(1)} %get-tuple-element.114), channel_id=1, source_target_pairs={{0,1},{1,16},{2,3},{3,18},{4,5},{5,20},{6,7},{7,22},{8,40},{9,41},... | collective-permute-start | bytes 626696 | tf_op jit(solution)/shard_map/ppermute | solution.py:805
  104.2 2.8 %collective-permute-start.15 = (bf16[816,128]{1,0:T(8,128)(2,1)S(1)}, bf16[816,128]{1,0:T(8,128)(2,1)S(1)}, u32[]{:S(2)}, u32[]{:S(2)}) collective-permute-start(bf16[816,128]{1,0:T(8,128)(2,1)S(1)} %get-tuple-element.116), channel_id=1, source_target_pairs={{0,16},{1,17},{2,18},{3,19},{4,20},{5,21},{6,22},{7,23},{8,72},{9,... | collective-permute-start | bytes 626696 | tf_op jit(solution)/shard_map/ppermute | solution.py:805
  107.0 1.0 collective-permute-done.14
  108.0 2.0 %collective-permute-done.16 = bf16[816,128]{1,0:T(8,128)(2,1)S(1)} collective-permute-done((bf16[816,128]{1,0:T(8,128)(2,1)S(1)}, bf16[816,128]{1,0:T(8,128)(2,1)S(1)}, u32[]{:S(2)}, u32[]{:S(2)}) %collective-permute-start.16) | collective-permute-done | bytes 208928 | tf_op jit(solution)/shard_map/ppermute | solution.py:805
  110.0 1.5 collective-permute-done.15
  111.5 0.1 fusion.2
  111.6 3.8 %collective-permute-start.20 = (bf16[816,128]{1,0:T(8,128)(2,1)S(1)}, bf16[816,128]{1,0:T(8,128)(2,1)S(1)}, u32[]{:S(2)}, u32[]{:S(2)}) collective-permute-start(bf16[816,128]{1,0:T(8,128)(2,1)S(1)} %fusion.2), channel_id=1, source_target_pairs={{0,96},{1,97},{2,98},{3,99},{4,100},{5,101},{6,102},{7,103},{8,14}... | collective-permute-start | bytes 626696 | tf_op jit(solution)/shard_map/ppermute | solution.py:805
  115.4 1.9 %collective-permute-start.18 = (bf16[816,128]{1,0:T(8,128)(2,1)S(1)}, bf16[816,128]{1,0:T(8,128)(2,1)S(1)}, u32[]{:S(2)}, u32[]{:S(2)}) collective-permute-start(bf16[816,128]{1,0:T(8,128)(2,1)S(1)} %fusion.2), channel_id=1, source_target_pairs={{0,64},{1,65},{2,66},{3,67},{4,68},{5,69},{6,70},{7,71},{8,12},{9,... | collective-permute-start | bytes 626696 | tf_op jit(solution)/shard_map/ppermute | solution.py:805
  117.3 3.2 %branch.1 = (bf16[2,9,42,512]{3,2,1,0:T(8,128)(2,1)S(1)}, bf16[2,9,6,512]{3,2,1,0:T(8,128)(2,1)S(1)}, bf16[2,3,42,512]{3,2,1,0:T(8,128)(2,1)S(1)}, bf16[2,3,6,512]{3,2,1,0:T(8,128)(2,1)S(1)}) custom-call(bf16[1152,512]{1,0:T(8,128)(2,1)S(1)} %copy-done.9, bf16[576,1536]{1,0:T(8,128)(2,1)S(1)} %get-tuple-element.79.grads_before.grads_first, ...), custom_call_target="tpu_custom_call" | custom-call | flops 7247757312 | bytes 10000000 | tf_op jit(solution)/shard_map/branch/pallas_call | solution.py:706
  120.5 4.2 %collective-permute-done.19 = bf16[816,128]{1,0:T(8,128)(2,1)S(1)} collective-permute-done((bf16[816,128]{1,0:T(8,128)(2,1)S(1)}, bf16[816,128]{1,0:T(8,128)(2,1)S(1)}, u32[]{:S(2)}, u32[]{:S(2)}) %collective-permute-start.19) | collective-permute-done | bytes 208928 | tf_op jit(solution)/shard_map/ppermute | solution.py:805
  124.7 0.1 add_convert_fusion.4
  124.8 2.0 %collective-permute-start.23 = (bf16[816,128]{1,0:T(8,128)(2,1)S(1)}, bf16[816,128]{1,0:T(8,128)(2,1)S(1)}, u32[]{:S(2)}, u32[]{:S(2)}) collective-permute-start(bf16[816,128]{1,0:T(8,128)(2,1)S(1)} %add_convert_fusion.4), channel_id=1, source_target_pairs={{0,17},{1,0},{2,19},{3,2},{4,21},{5,4},{6,23},{7,6},{8,104},{9,105... | collective-permute-start | bytes 626696 | tf_op jit(solution)/shard_map/ppermute | solution.py:805
  126.8 0.5 collective-permute-start.22
  127.3 0.7 collective-permute-start.21
  128.0 3.1 %collective-permute-start.17 = (bf16[2,3,6,512]{3,2,1,0:T(8,128)(2,1)S(1)}, bf16[2,3,6,512]{3,2,1,0:T(8,128)(2,1)S(1)}, u32[]{:S(2)}, u32[]{:S(2)}) collective-permute-start(bf16[2,3,6,512]{3,2,1,0:T(8,128)(2,1)S(1)} %get-tuple-element.82), channel_id=1, source_target_pairs={{0,9},{1,10},{2,11},{3,12},{4,13},{5,14},{6,15},{7,8},{8,17},{9,18... | collective-permute-start | bytes 110600 | tf_op jit(solution)/shard_map/ppermute | solution.py:776
  131.1 4.5 %collective-permute-done.23 = bf16[816,128]{1,0:T(8,128)(2,1)S(1)} collective-permute-done((bf16[816,128]{1,0:T(8,128)(2,1)S(1)}, bf16[816,128]{1,0:T(8,128)(2,1)S(1)}, u32[]{:S(2)}, u32[]{:S(2)}) %collective-permute-start.23) | collective-permute-done | bytes 208928 | tf_op jit(solution)/shard_map/ppermute | solution.py:805
  135.6 1.3 collective-permute-start.24
  136.9 2.5 %collective-permute-done.21 = bf16[816,128]{1,0:T(8,128)(2,1)S(1)} collective-permute-done((bf16[816,128]{1,0:T(8,128)(2,1)S(1)}, bf16[816,128]{1,0:T(8,128)(2,1)S(1)}, u32[]{:S(2)}, u32[]{:S(2)}) %collective-permute-start.21) | collective-permute-done | bytes 208928 | tf_op jit(solution)/shard_map/ppermute | solution.py:805
  139.5 0.1 pad_maximum_fusion.refs_0_
  139.6 3.3 %collective-permute-done.24 = bf16[2,9,6,512]{3,2,1,0:T(8,128)(2,1)S(1)} collective-permute-done((bf16[2,9,6,512]{3,2,1,0:T(8,128)(2,1)S(1)}, bf16[2,9,6,512]{3,2,1,0:T(8,128)(2,1)S(1)}, u32[]{:S(2)}, u32[]{:S(2)}) %collective-permute-start.24) | collective-permute-done | bytes 110624 | tf_op jit(solution)/shard_map/ppermute | solution.py:776
  142.9 0.2 collective-permute-start.31
  143.2 3.2 %collective-permute-start.29 = (bf16[4,816,128]{2,1,0:T(8,128)(2,1)S(1)}, bf16[4,816,128]{2,1,0:T(8,128)(2,1)S(1)}, u32[]{:S(2)}, u32[]{:S(2)}) collective-permute-start(bf16[4,816,128]{2,1,0:T(8,128)(2,1)S(1)} %pad_maximum_fusion.refs_0_), channel_id=1, source_target_pairs={{0,4},{1,5},{2,6},{3,7},{4,0},{5,1},{6,2},{7,3},{8,24},{9,25},{10,... | collective-permute-start | bytes 2506760 | tf_op jit(solution)/shard_map/ppermute | solution.py:805
  146.4 1.6 maximum_maximum_fusion
  148.0 7.4 %collective-permute-done.31.refs_3_ = bf16[4,816,128]{2,1,0:T(8,128)(2,1)S(1)} collective-permute-done((bf16[4,816,128]{2,1,0:T(8,128)(2,1)S(1)}, bf16[4,816,128]{2,1,0:T(8,128)(2,1)S(1)}, u32[]{:S(2)}, u32[]{:S(2)}) %collective-permute-start.31) | collective-permute-done | bytes 835616 | tf_op jit(solution)/shard_map/ppermute | solution.py:805
  155.5 1.8 %collective-permute-done.29.refs_2_ = bf16[4,816,128]{2,1,0:T(8,128)(2,1)S(1)} collective-permute-done((bf16[4,816,128]{2,1,0:T(8,128)(2,1)S(1)}, bf16[4,816,128]{2,1,0:T(8,128)(2,1)S(1)}, u32[]{:S(2)}, u32[]{:S(2)}) %collective-permute-start.29) | collective-permute-done | bytes 835616 | tf_op jit(solution)/shard_map/ppermute | solution.py:805
  157.3 8.8 %collective-permute-done.27.refs_1_ = bf16[4,816,128]{2,1,0:T(8,128)(2,1)S(1)} collective-permute-done((bf16[4,816,128]{2,1,0:T(8,128)(2,1)S(1)}, bf16[4,816,128]{2,1,0:T(8,128)(2,1)S(1)}, u32[]{:S(2)}, u32[]{:S(2)}) %collective-permute-start.27) | collective-permute-done | bytes 835616 | tf_op jit(solution)/shard_map/ppermute | solution.py:805
  166.1 3.5 %finish_own.1 = (f32[512,2048]{1,0:T(8,128)}, f32[2048,512]{1,0:T(8,128)}, f32[512,1536]{1,0:T(8,128)}, f32[512,512]{1,0:T(8,128)}, f32[512,128]{1,0:T(8,128)S(1)}, /*index=5*/bf16[32,48,128]{2,1,0:T(8,128)(2,1)S(1)}) custom-call(bf16[4,816,128]{2,1,0:T(8,128)(2,1)S(1)} %pad_maximum_fusion.refs_0_, bf16[4,816,128]{2,1,0:T(8,128)(2,1)S(1)} %collective-permute-done.27.refs_1_, ...), custom_call_target="tpu_custom_call" | custom-call | flops 10000000 | bytes 10000000 | tf_op jit(solution)/shard_map/finish_own/pallas_call | solution.py:739
  169.7 4.9 %finish.1 = (f32[512,2048]{1,0:T(8,128)}, f32[2048,512]{1,0:T(8,128)}, f32[512,1536]{1,0:T(8,128)}, f32[512,512]{1,0:T(8,128)}, f32[8,144,144]{2,1,0:T(8,128)}, /*index=5*/f32[1,512]{1,0:T(1,128)}, f32[1,512]{1,0:T(1,128)}) custom-call(bf16[4,816,128]{2,1,0:T(8,128)(2,1)S(1)} %collective-per, ...), custom_call_target="tpu_custom_call", output_to_operand_aliasing={{0}: (8, {}), {1}: (9, {}), {2}: (10, {}), {3}: (11, {})} | custom-call | flops 10000000 | bytes 10000000 | tf_op jit(solution)/shard_map/finish/pallas_call | solution.py:752
  (58 shorter events, 0.4 us)
Async XLA Ops:
  0.6 1.3 copy-start.1
  1.9 15.8 %collective-permute-start.1 = (bf16[2,3,48,512]{3,2,1,0:T(8,128)(2,1)S(1)}, bf16[2,3,48,512]{3,2,1,0:T(8,128)(2,1)S(1)}, u32[]{:S(2)}, u32[]{:S(2)}) collective-permute-start(bf16[2,3,48,512]{3,2,1,0:T(8,128)(2,1)S(1)} %get-tuple-element.59), channel_id=1, source_target_pairs={{0,120},{1,121},{2,122},{3,123},{4,124},{5,125},{6,126},{7,127},{8... | collective-permute-start | bytes 884744 | tf_op jit(solution)/shard_map/ppermute | solution.py:776
  8.2 9.5 %collective-permute-start = (bf16[2,12,6,512]{3,2,1,0:T(8,128)(2,1)S(1)}, bf16[2,12,6,512]{3,2,1,0:T(8,128)(2,1)S(1)}, u32[]{:S(2)}, u32[]{:S(2)}) collective-permute-start(bf16[2,12,6,512]{3,2,1,0:T(8,128)(2,1)S(1)} %get-tuple-element.58), channel_id=1, source_target_pairs={{0,7},{1,0},{2,1},{3,2},{4,3},{5,4},{6,5},{7,6},{8,15},{9,8},{10,9... | collective-permute-start | bytes 442376 | tf_op jit(solution)/shard_map/ppermute | solution.py:776
  11.1 5.2 %collective-permute-start.2 = (bf16[2,3,6,512]{3,2,1,0:T(8,128)(2,1)S(1)}, bf16[2,3,6,512]{3,2,1,0:T(8,128)(2,1)S(1)}, u32[]{:S(2)}, u32[]{:S(2)}) collective-permute-start(bf16[2,3,6,512]{3,2,1,0:T(8,128)(2,1)S(1)} %get-tuple-element.60), channel_id=1, source_target_pairs={{0,127},{1,120},{2,121},{3,122},{4,123},{5,124},{6,125},{7,126},{8... | collective-permute-start | bytes 110600 | tf_op jit(solution)/shard_map/ppermute | solution.py:776
  11.4 1.3 copy-start.2
  12.7 18.7 %collective-permute-start.5 = (bf16[2,3,6,512]{3,2,1,0:T(8,128)(2,1)S(1)}, bf16[2,3,6,512]{3,2,1,0:T(8,128)(2,1)S(1)}, u32[]{:S(2)}, u32[]{:S(2)}) collective-permute-start(bf16[2,3,6,512]{3,2,1,0:T(8,128)(2,1)S(1)} %get-tuple-element.67), channel_id=1, source_target_pairs={{0,127},{1,120},{2,121},{3,122},{4,123},{5,124},{6,125},{7,126},{8... | collective-permute-start | bytes 110600 | tf_op jit(solution)/shard_map/ppermute | solution.py:776
  14.9 16.5 %collective-permute-start.3 = (bf16[2,12,6,512]{3,2,1,0:T(8,128)(2,1)S(1)}, bf16[2,12,6,512]{3,2,1,0:T(8,128)(2,1)S(1)}, u32[]{:S(2)}, u32[]{:S(2)}) collective-permute-start(bf16[2,12,6,512]{3,2,1,0:T(8,128)(2,1)S(1)} %get-tuple-element.65), channel_id=1, source_target_pairs={{0,7},{1,0},{2,1},{3,2},{4,3},{5,4},{6,5},{7,6},{8,15},{9,8},{10,9... | collective-permute-start | bytes 442376 | tf_op jit(solution)/shard_map/ppermute | solution.py:776
  16.3 1.4 copy-start.17
  16.3 15.1 %collective-permute-start.4 = (bf16[2,3,48,512]{3,2,1,0:T(8,128)(2,1)S(1)}, bf16[2,3,48,512]{3,2,1,0:T(8,128)(2,1)S(1)}, u32[]{:S(2)}, u32[]{:S(2)}) collective-permute-start(bf16[2,3,48,512]{3,2,1,0:T(8,128)(2,1)S(1)} %get-tuple-element.66), channel_id=1, source_target_pairs={{0,120},{1,121},{2,122},{3,123},{4,124},{5,125},{6,126},{7,127},{8... | collective-permute-start | bytes 884744 | tf_op jit(solution)/shard_map/ppermute | solution.py:776
  17.7 0.7 copy-start.15
  17.7 0.8 copy-start.12
  31.4 0.6 copy-start.16
  31.4 0.7 copy-start.14
  31.4 0.8 copy-start.13
  32.2 28.5 %copy-start.4 = (bf16[1152,1536]{1,0:T(8,128)(2,1)S(1)}, bf16[1152,1536]{1,0:T(8,128)(2,1)}, u32[]{:S(2)}) copy-start(bf16[1152,1536]{1,0:T(8,128)(2,1)} %get-tuple-element.62.qkv) | copy-start | bytes 10616836
  32.2 28.5 %copy-start.5 = (bf16[8,9,144,128]{3,2,1,0:T(8,128)(2,1)S(1)}, bf16[8,9,144,128]{3,2,1,0:T(8,128)(2,1)}, u32[]{:S(2)}) copy-start(bf16[8,9,144,128]{3,2,1,0:T(8,128)(2,1)} %get-tuple-element.63.probs) | copy-start | bytes 7962628
  60.4 5.4 %collective-permute-start.6 = (bf16[16,576,128]{2,1,0:T(8,128)(2,1)}, bf16[16,576,128]{2,1,0:T(8,128)(2,1)S(1)}, u32[]{:S(2)}, u32[]{:S(2)}) collective-permute-start(bf16[16,576,128]{2,1,0:T(8,128)(2,1)} %get-tuple-element.71), channel_id=1, source_target_pairs={{0,8},{8,0},{16,24},{24,16},{32,40},{40,32},{48,56},{56,48},{64,72... | collective-permute-start | bytes 7077896 | tf_op jit(solution)/shard_map/ppermute | solution.py:809
  60.7 1.3 copy-start.6
  62.0 3.8 %copy-start.11 = (bf16[16,576,128]{2,1,0:T(8,128)(2,1)S(1)}, bf16[16,576,128]{2,1,0:T(8,128)(2,1)}, u32[]{:S(2)}) copy-start(bf16[16,576,128]{2,1,0:T(8,128)(2,1)} %get-tuple-element.70) | copy-start | bytes 7077892
  66.4 7.3 %copy-start.8 = (bf16[512,1152]{1,0:T(8,128)(2,1)S(1)}, bf16[512,1152]{1,0:T(8,128)(2,1)}, u32[]{:S(2)}) copy-start(bf16[512,1152]{1,0:T(8,128)(2,1)} %get-tuple-element.72.act_t) | copy-start | bytes 3538948
  66.4 7.3 %copy-start.10 = (f32[1,512]{1,0:T(1,128)S(1)}, f32[1,512]{1,0:T(1,128)}, u32[]{:S(2)}) copy-start(f32[1,512]{1,0:T(1,128)} %get-tuple-element.73.sum_gain_two) | copy-start | bytes 6148
  66.5 15.4 %collective-permute-start.7 = (bf16[4,576,128]{2,1,0:T(8,128)(2,1)S(1)}, bf16[4,576,128]{2,1,0:T(8,128)(2,1)S(1)}, u32[]{:S(2)}, u32[]{:S(2)}) collective-permute-start(bf16[4,576,128]{2,1,0:T(8,128)(2,1)S(1)} %get-tuple-element.108), channel_id=1, source_target_pairs={{0,2},{1,3},{2,4},{3,5},{4,6},{5,7},{6,0},{7,1},{8,9},{9,24},{10,1... | collective-permute-start | bytes 1769480 | tf_op jit(solution)/shard_map/ppermute | solution.py:805
  70.2 11.8 %collective-permute-start.9 = (bf16[4,576,128]{2,1,0:T(8,128)(2,1)S(1)}, bf16[4,576,128]{2,1,0:T(8,128)(2,1)S(1)}, u32[]{:S(2)}, u32[]{:S(2)}) collective-permute-start(bf16[4,576,128]{2,1,0:T(8,128)(2,1)S(1)} %get-tuple-element.109), channel_id=1, source_target_pairs={{0,6},{1,7},{2,0},{3,1},{4,2},{5,3},{6,4},{7,5},{8,25},{9,8},{10,2... | collective-permute-start | bytes 1769480 | tf_op jit(solution)/shard_map/ppermute | solution.py:805
  70.3 15.6 %collective-permute-start.8 = (bf16[4,576,128]{2,1,0:T(8,128)(2,1)S(1)}, bf16[4,576,128]{2,1,0:T(8,128)(2,1)S(1)}, u32[]{:S(2)}, u32[]{:S(2)}) collective-permute-start(bf16[4,576,128]{2,1,0:T(8,128)(2,1)S(1)} %get-tuple-element.110), channel_id=1, source_target_pairs={{0,4},{1,5},{2,6},{3,7},{4,0},{5,1},{6,2},{7,3},{8,24},{9,25},{10,... | collective-permute-start | bytes 1769480 | tf_op jit(solution)/shard_map/ppermute | solution.py:805
  86.2 2.6 %collective-permute-start.10 = (bf16[16,240,128]{2,1,0:T(8,128)(2,1)S(1)}, bf16[16,240,128]{2,1,0:T(8,128)(2,1)S(1)}, u32[]{:S(2)}, u32[]{:S(2)}) collective-permute-start(bf16[16,240,128]{2,1,0:T(8,128)(2,1)S(1)} %get-tuple-element.78), channel_id=1, source_target_pairs={{0,8},{8,0},{16,24},{24,16},{32,40},{40,32},{48,56},{56,48},{64,72... | collective-permute-start | bytes 2949128 | tf_op jit(solution)/shard_map/ppermute | solution.py:809
  89.1 28.2 %copy-start.9 = (bf16[1152,512]{1,0:T(8,128)(2,1)S(1)}, bf16[1152,512]{1,0:T(8,128)(2,1)}, u32[]{:S(2)}) copy-start(bf16[1152,512]{1,0:T(8,128)(2,1)} %get-tuple-element.61.xw) | copy-start | bytes 3538948
  89.2 7.5 %collective-permute-start.11 = (bf16[4,240,128]{2,1,0:T(8,128)(2,1)S(1)}, bf16[4,240,128]{2,1,0:T(8,128)(2,1)S(1)}, u32[]{:S(2)}, u32[]{:S(2)}) collective-permute-start(bf16[4,240,128]{2,1,0:T(8,128)(2,1)S(1)} %get-tuple-element.111), channel_id=1, source_target_pairs={{0,2},{1,3},{2,4},{3,5},{4,6},{5,7},{6,0},{7,1},{8,9},{9,24},{10,1... | collective-permute-start | bytes 737288 | tf_op jit(solution)/shard_map/ppermute | solution.py:805
  91.2 6.2 %collective-permute-start.13 = (bf16[4,240,128]{2,1,0:T(8,128)(2,1)S(1)}, bf16[4,240,128]{2,1,0:T(8,128)(2,1)S(1)}, u32[]{:S(2)}, u32[]{:S(2)}) collective-permute-start(bf16[4,240,128]{2,1,0:T(8,128)(2,1)S(1)} %get-tuple-element.112), channel_id=1, source_target_pairs={{0,6},{1,7},{2,0},{3,1},{4,2},{5,3},{6,4},{7,5},{8,25},{9,8},{10,2... | collective-permute-start | bytes 737288 | tf_op jit(solution)/shard_map/ppermute | solution.py:805
  92.5 24.8 %copy-start = (bf16[512,1536]{1,0:T(8,128)(2,1)S(1)}, bf16[512,1536]{1,0:T(8,128)(2,1)}, u32[]{:S(2)}) copy-start(bf16[512,1536]{1,0:T(8,128)(2,1)} %refs_4_.3) | copy-start | bytes 4718596
  92.5 24.8 %copy-start.3 = (f32[512]{0:T(512)S(1)}, f32[512]{0:T(512)}, u32[]{:S(2)}) copy-start(f32[512]{0:T(512)} %param.16) | copy-start | bytes 6148
  92.5 24.8 %copy-start.7 = (f32[1152,512]{1,0:T(8,128)S(1)}, f32[1152,512]{1,0:T(8,128)}, u32[]{:S(2)}) copy-start(f32[1152,512]{1,0:T(8,128)} %get-tuple-element.81.grad_res) | copy-start | bytes 7077892
  92.5 8.2 %collective-permute-start.12 = (bf16[4,240,128]{2,1,0:T(8,128)(2,1)S(1)}, bf16[4,240,128]{2,1,0:T(8,128)(2,1)S(1)}, u32[]{:S(2)}, u32[]{:S(2)}) collective-permute-start(bf16[4,240,128]{2,1,0:T(8,128)(2,1)S(1)} %get-tuple-element.113), channel_id=1, source_target_pairs={{0,4},{1,5},{2,6},{3,7},{4,0},{5,1},{6,2},{7,3},{8,24},{9,25},{10,... | collective-permute-start | bytes 737288 | tf_op jit(solution)/shard_map/ppermute | solution.py:805
  100.9 7.1 %collective-permute-start.14 = (bf16[816,128]{1,0:T(8,128)(2,1)S(1)}, bf16[816,128]{1,0:T(8,128)(2,1)S(1)}, u32[]{:S(2)}, u32[]{:S(2)}) collective-permute-start(bf16[816,128]{1,0:T(8,128)(2,1)S(1)} %get-tuple-element.114), channel_id=1, source_target_pairs={{0,1},{1,16},{2,3},{3,18},{4,5},{5,20},{6,7},{7,22},{8,40},{9,41},... | collective-permute-start | bytes 626696 | tf_op jit(solution)/shard_map/ppermute | solution.py:805
  104.2 5.8 %collective-permute-start.16 = (bf16[816,128]{1,0:T(8,128)(2,1)S(1)}, bf16[816,128]{1,0:T(8,128)(2,1)S(1)}, u32[]{:S(2)}, u32[]{:S(2)}) collective-permute-start(bf16[816,128]{1,0:T(8,128)(2,1)S(1)} %get-tuple-element.115), channel_id=1, source_target_pairs={{0,17},{1,0},{2,19},{3,2},{4,21},{5,4},{6,23},{7,6},{8,104},{9,105... | collective-permute-start | bytes 626696 | tf_op jit(solution)/shard_map/ppermute | solution.py:805
  104.2 7.3 %collective-permute-start.15 = (bf16[816,128]{1,0:T(8,128)(2,1)S(1)}, bf16[816,128]{1,0:T(8,128)(2,1)S(1)}, u32[]{:S(2)}, u32[]{:S(2)}) collective-permute-start(bf16[816,128]{1,0:T(8,128)(2,1)S(1)} %get-tuple-element.116), channel_id=1, source_target_pairs={{0,16},{1,17},{2,18},{3,19},{4,20},{5,21},{6,22},{7,23},{8,72},{9,... | collective-permute-start | bytes 626696 | tf_op jit(solution)/shard_map/ppermute | solution.py:805
  111.6 8.9 %collective-permute-start.20 = (bf16[816,128]{1,0:T(8,128)(2,1)S(1)}, bf16[816,128]{1,0:T(8,128)(2,1)S(1)}, u32[]{:S(2)}, u32[]{:S(2)}) collective-permute-start(bf16[816,128]{1,0:T(8,128)(2,1)S(1)} %fusion.2), channel_id=1, source_target_pairs={{0,96},{1,97},{2,98},{3,99},{4,100},{5,101},{6,102},{7,103},{8,14}... | collective-permute-start | bytes 626696 | tf_op jit(solution)/shard_map/ppermute | solution.py:805
  115.4 9.3 %collective-permute-start.19 = (bf16[816,128]{1,0:T(8,128)(2,1)S(1)}, bf16[816,128]{1,0:T(8,128)(2,1)S(1)}, u32[]{:S(2)}, u32[]{:S(2)}) collective-permute-start(bf16[816,128]{1,0:T(8,128)(2,1)S(1)} %fusion.2), channel_id=1, source_target_pairs={{0,32},{1,33},{2,34},{3,35},{4,36},{5,37},{6,38},{7,39},{8,10},{9,... | collective-permute-start | bytes 626696 | tf_op jit(solution)/shard_map/ppermute | solution.py:805
  115.4 9.3 %collective-permute-start.18 = (bf16[816,128]{1,0:T(8,128)(2,1)S(1)}, bf16[816,128]{1,0:T(8,128)(2,1)S(1)}, u32[]{:S(2)}, u32[]{:S(2)}) collective-permute-start(bf16[816,128]{1,0:T(8,128)(2,1)S(1)} %fusion.2), channel_id=1, source_target_pairs={{0,64},{1,65},{2,66},{3,67},{4,68},{5,69},{6,70},{7,71},{8,12},{9,... | collective-permute-start | bytes 626696 | tf_op jit(solution)/shard_map/ppermute | solution.py:805
  124.8 10.8 %collective-permute-start.23 = (bf16[816,128]{1,0:T(8,128)(2,1)S(1)}, bf16[816,128]{1,0:T(8,128)(2,1)S(1)}, u32[]{:S(2)}, u32[]{:S(2)}) collective-permute-start(bf16[816,128]{1,0:T(8,128)(2,1)S(1)} %add_convert_fusion.4), channel_id=1, source_target_pairs={{0,17},{1,0},{2,19},{3,2},{4,21},{5,4},{6,23},{7,6},{8,104},{9,105... | collective-permute-start | bytes 626696 | tf_op jit(solution)/shard_map/ppermute | solution.py:805
  126.8 10.1 %collective-permute-start.22 = (bf16[816,128]{1,0:T(8,128)(2,1)S(1)}, bf16[816,128]{1,0:T(8,128)(2,1)S(1)}, u32[]{:S(2)}, u32[]{:S(2)}) collective-permute-start(bf16[816,128]{1,0:T(8,128)(2,1)S(1)} %add_convert_fusion.4), channel_id=1, source_target_pairs={{0,16},{1,17},{2,18},{3,19},{4,20},{5,21},{6,22},{7,23},{8,72},{9,... | collective-permute-start | bytes 626696 | tf_op jit(solution)/shard_map/ppermute | solution.py:805
  127.3 12.2 %collective-permute-start.21 = (bf16[816,128]{1,0:T(8,128)(2,1)S(1)}, bf16[816,128]{1,0:T(8,128)(2,1)S(1)}, u32[]{:S(2)}, u32[]{:S(2)}) collective-permute-start(bf16[816,128]{1,0:T(8,128)(2,1)S(1)} %add_convert_fusion.4), channel_id=1, source_target_pairs={{0,1},{1,16},{2,3},{3,18},{4,5},{5,20},{6,7},{7,22},{8,40},{9,41},... | collective-permute-start | bytes 626696 | tf_op jit(solution)/shard_map/ppermute | solution.py:805
  128.0 15.0 %collective-permute-start.25 = (bf16[2,3,42,512]{3,2,1,0:T(8,128)(2,1)S(1)}, bf16[2,3,42,512]{3,2,1,0:T(8,128)(2,1)S(1)}, u32[]{:S(2)}, u32[]{:S(2)}) collective-permute-start(bf16[2,3,42,512]{3,2,1,0:T(8,128)(2,1)S(1)} %get-tuple-element.85), channel_id=1, source_target_pairs={{0,8},{1,9},{2,10},{3,11},{4,12},{5,13},{6,14},{7,15},{8,16},{9,17... | collective-permute-start | bytes 774152 | tf_op jit(solution)/shard_map/ppermute | solution.py:776
  128.0 11.6 %collective-permute-start.17 = (bf16[2,3,6,512]{3,2,1,0:T(8,128)(2,1)S(1)}, bf16[2,3,6,512]{3,2,1,0:T(8,128)(2,1)S(1)}, u32[]{:S(2)}, u32[]{:S(2)}) collective-permute-start(bf16[2,3,6,512]{3,2,1,0:T(8,128)(2,1)S(1)} %get-tuple-element.82), channel_id=1, source_target_pairs={{0,9},{1,10},{2,11},{3,12},{4,13},{5,14},{6,15},{7,8},{8,17},{9,18... | collective-permute-start | bytes 110600 | tf_op jit(solution)/shard_map/ppermute | solution.py:776
  135.6 7.4 %collective-permute-start.24 = (bf16[2,9,6,512]{3,2,1,0:T(8,128)(2,1)S(1)}, bf16[2,9,6,512]{3,2,1,0:T(8,128)(2,1)S(1)}, u32[]{:S(2)}, u32[]{:S(2)}) collective-permute-start(bf16[2,9,6,512]{3,2,1,0:T(8,128)(2,1)S(1)} %get-tuple-element.84), channel_id=1, source_target_pairs={{0,1},{1,2},{2,3},{3,4},{4,5},{5,6},{6,7},{7,0},{8,9},{9,10},{10,1... | collective-permute-start | bytes 331784 | tf_op jit(solution)/shard_map/ppermute | solution.py:776
  142.9 12.5 %collective-permute-start.31 = (bf16[4,816,128]{2,1,0:T(8,128)(2,1)S(1)}, bf16[4,816,128]{2,1,0:T(8,128)(2,1)S(1)}, u32[]{:S(2)}, u32[]{:S(2)}) collective-permute-start(bf16[4,816,128]{2,1,0:T(8,128)(2,1)S(1)} %pad_maximum_fusion.refs_0_), channel_id=1, source_target_pairs={{0,6},{1,7},{2,0},{3,1},{4,2},{5,3},{6,4},{7,5},{8,25},{9,8},{10,2... | collective-permute-start | bytes 2506760 | tf_op jit(solution)/shard_map/ppermute | solution.py:805
  143.2 14.1 %collective-permute-start.29 = (bf16[4,816,128]{2,1,0:T(8,128)(2,1)S(1)}, bf16[4,816,128]{2,1,0:T(8,128)(2,1)S(1)}, u32[]{:S(2)}, u32[]{:S(2)}) collective-permute-start(bf16[4,816,128]{2,1,0:T(8,128)(2,1)S(1)} %pad_maximum_fusion.refs_0_), channel_id=1, source_target_pairs={{0,4},{1,5},{2,6},{3,7},{4,0},{5,1},{6,2},{7,3},{8,24},{9,25},{10,... | collective-permute-start | bytes 2506760 | tf_op jit(solution)/shard_map/ppermute | solution.py:805
  146.4 19.7 %collective-permute-start.27 = (bf16[4,816,128]{2,1,0:T(8,128)(2,1)S(1)}, bf16[4,816,128]{2,1,0:T(8,128)(2,1)S(1)}, u32[]{:S(2)}, u32[]{:S(2)}) collective-permute-start(bf16[4,816,128]{2,1,0:T(8,128)(2,1)S(1)} %pad_maximum_fusion.refs_0_), channel_id=1, source_target_pairs={{0,2},{1,3},{2,4},{3,5},{4,6},{5,7},{6,0},{7,1},{8,9},{9,24},{10,1... | collective-permute-start | bytes 2506760 | tf_op jit(solution)/shard_map/ppermute | solution.py:805
  146.4 23.3 %collective-permute-start.26 = (bf16[4,816,128]{2,1,0:T(8,128)(2,1)S(1)}, bf16[4,816,128]{2,1,0:T(8,128)(2,1)S(1)}, u32[]{:S(2)}, u32[]{:S(2)}) collective-permute-start(bf16[4,816,128]{2,1,0:T(8,128)(2,1)S(1)} %pad_maximum_fusion.refs_0_), channel_id=1, source_target_pairs={{0,8},{8,0},{16,24},{24,16},{32,40},{40,32},{48,56},{56,48},{64,72... | collective-permute-start | bytes 2506760 | tf_op jit(solution)/shard_map/ppermute | solution.py:809
  155.5 14.2 %collective-permute-start.32 = (bf16[4,816,128]{2,1,0:T(8,128)(2,1)S(1)}, bf16[4,816,128]{2,1,0:T(8,128)(2,1)S(1)}, u32[]{:S(2)}, u32[]{:S(2)}) collective-permute-start(bf16[4,816,128]{2,1,0:T(8,128)(2,1)S(1)} %collective-permute-done.31.refs_3_), channel_id=1, source_target_pairs={{0,8},{8,0},{16,24},{24,16},{32,40},{40,32},{48,56},{56,48},{64,72... | collective-permute-start | bytes 2506760 | tf_op jit(solution)/shard_map/ppermute | solution.py:809
  157.3 12.4 %collective-permute-start.30 = (bf16[4,816,128]{2,1,0:T(8,128)(2,1)S(1)}, bf16[4,816,128]{2,1,0:T(8,128)(2,1)S(1)}, u32[]{:S(2)}, u32[]{:S(2)}) collective-permute-start(bf16[4,816,128]{2,1,0:T(8,128)(2,1)S(1)} %collective-permute-done.29.refs_2_), channel_id=1, source_target_pairs={{0,8},{8,0},{16,24},{24,16},{32,40},{40,32},{48,56},{56,48},{64,72... | collective-permute-start | bytes 2506760 | tf_op jit(solution)/shard_map/ppermute | solution.py:809
  166.1 3.6 %collective-permute-start.28 = (bf16[4,816,128]{2,1,0:T(8,128)(2,1)S(1)}, bf16[4,816,128]{2,1,0:T(8,128)(2,1)S(1)}, u32[]{:S(2)}, u32[]{:S(2)}) collective-permute-start(bf16[4,816,128]{2,1,0:T(8,128)(2,1)S(1)} %collective-permute-done.27.refs_1_), channel_id=1, source_target_pairs={{0,8},{8,0},{16,24},{24,16},{32,40},{40,32},{48,56},{56,48},{64,72... | collective-permute-start | bytes 2506760 | tf_op jit(solution)/shard_map/ppermute | solution.py:809
